TPU v7x, 32 devices: a whole 2x2x4 slice. The times are simulated.
32 devices in a mesh: clips: 2 (over y), seq: 8 (over z, x), mp: 2 (over core).
Axes of the slice: x: 2, y: 2, z: 4, core: 2. Of those that a mesh axis runs over, the one named last changes fastest.
Arguments:
- queries: bfloat16 [12, 4096, 128], P('mp', ('clips', 'seq')), parts along dimension 1, may hold values from -6 to 6
- keys: bfloat16 [12, 4096, 128], P('mp', ('clips', 'seq')), parts along dimension 1, may hold values from -6 to 6
- values: bfloat16 [12, 4096, 128], P('mp', ('clips', 'seq')), parts along dimension 1, may hold values from -12 to 12
- out_grad: bfloat16 [12, 4096, 128], P('mp', ('clips', 'seq')), parts along dimension 1, may hold values from -12 to 12
- tile_lists: int32 [12, 8, 4], P('mp'), may hold values from -1 to 7, as said below
Outputs:
- attn_out: bfloat16 [12, 4096, 128], P('mp', ('clips', 'seq')), parts along dimension 1
- query_grad: bfloat16 [12, 4096, 128], P('mp', ('clips', 'seq')), parts along dimension 1
- key_grad: bfloat16 [12, 4096, 128], P('mp', ('clips', 'seq')), parts along dimension 1
- value_grad: bfloat16 [12, 4096, 128], P('mp', ('clips', 'seq')), parts along dimension 1
There are 2 independent parts, one for each index of `clips`. A program takes and returns all parts, laid end to end along the dimension named above; an argument that names none is the same for every part. Nothing has to cross between parts.
Inputs may be any that keep to these rules, and one draw needn't show every extreme that they name: `tile_lists`: tile ids count (time + row) * 8 + column over a grid of 1 x 1 x 8 tiles. Entry 0 of the list of head h and query tile q is q itself; the further entries name distinct tiles that share a face with q inside the grid, filled entries first and -1 in empty ones. For every tile and each of its six face directions, at most 3 heads of each group of 6 consecutive heads name that neighbour.
All inputs are finite; a program needn't handle non-finite values.
Results may differ from a plain program's by a relative error of at most 0.0067.
Values may be sent and summed in bfloat16 or wider, within the bound.
No kernel may reach another device: no remote copies, remote signals or barrier semaphores. Data moves between devices by JAX's collectives and lax.ppermute only.
A program may use at most 64 MiB of HBM per device.

v0:
```python
import jax
import jax.numpy as jnp
from jax import lax
from jax.sharding import PartitionSpec as P

HCAP = 3
GX = 8


def passed_along(block, axis, distance):
    devices = range(lax.axis_size(axis))
    route = [(i - distance, i) for i in devices if i - distance in devices]
    return lax.ppermute(block, axis, route)


def direction_offsets(tile_count):
    row_tiles = min(4, tile_count // 8)
    layer_size = GX * row_tiles
    result = [1, -1]
    if row_tiles > 1:
        result = result + [GX, -GX]
    if tile_count // layer_size > 1:
        result = result + [layer_size, -layer_size]
    return result


def heads_naming(tile_lists, reader, named, tile_count):
    inside = (reader >= 0) & (reader < tile_count)
    reader_lists = lax.dynamic_index_in_dim(
        tile_lists, jnp.clip(reader, 0, tile_count - 1), 1, keepdims=False
    )
    return inside & jnp.any(reader_lists == named, axis=1)


def packing(head_mask):
    position = jnp.cumsum(head_mask.astype(jnp.int32)) - 1
    slot_ids = jnp.arange(HCAP, dtype=jnp.int32)
    return (head_mask[None, :] & (position[None, :] == slot_ids[:, None])).astype(jnp.bfloat16)


def pack_heads(placer, stacked):
    return jnp.einsum("ch,xhtd->xctd", placer, stacked, preferred_element_type=jnp.float32).astype(
        jnp.bfloat16
    )


def unpack_heads(placer, packed):
    return jnp.einsum("ch,xctd->xhtd", placer, packed, preferred_element_type=jnp.float32).astype(
        jnp.bfloat16
    )


def send_keys_used(key_value, send_placer, recv_placer, offset):
    packed = passed_along(pack_heads(send_placer, key_value), "seq", -offset)
    return unpack_heads(recv_placer, packed)


def send_grads_used(gradients, send_placer, recv_placer, offset):
    packed = passed_along(pack_heads(recv_placer, gradients), "seq", offset)
    return unpack_heads(send_placer, packed)


def per_device(queries, keys, values, out_grad, tile_lists):
    heads_here = queries.shape[0]
    head_width = queries.shape[2]
    tile_count = lax.axis_size("seq")
    own_tile = lax.axis_index("seq")
    offsets = direction_offsets(tile_count)
    score_scale = head_width ** (-0.5)
    own_lists = lax.dynamic_index_in_dim(tile_lists, own_tile, 1, keepdims=False)
    live_slots = own_lists >= 0
    key_value = jnp.stack([keys, values])
    fetched = [key_value]
    placers = []
    for offset in offsets:
        send_placer = packing(heads_naming(tile_lists, own_tile - offset, own_tile, tile_count))
        recv_placer = packing(heads_naming(tile_lists, own_tile, own_tile + offset, tile_count))
        placers.append((send_placer, recv_placer))
        fetched.append(send_keys_used(key_value, send_placer, recv_placer, offset))
    candidate_ids = [own_tile] + [own_tile + offset for offset in offsets]
    chooser = jnp.stack(
        [live_slots & (own_lists == candidate) for candidate in candidate_ids], axis=-1
    ).astype(jnp.bfloat16)
    candidates = jnp.stack(fetched)

    def attend(block_index):
        first_head = block_index * 2
        query_block = lax.dynamic_slice_in_dim(queries, first_head, 2, 0)
        grad_block = lax.dynamic_slice_in_dim(out_grad, first_head, 2, 0)
        chooser_block = lax.dynamic_slice_in_dim(chooser, first_head, 2, 0)
        live_block = lax.dynamic_slice_in_dim(live_slots, first_head, 2, 0)
        candidates_block = lax.dynamic_slice_in_dim(candidates, first_head, 2, 2)
        key_chosen = jnp.einsum(
            "hjc,chtd->hjtd",
            chooser_block,
            candidates_block[:, 0],
            preferred_element_type=jnp.float32,
        ).astype(jnp.bfloat16)
        value_chosen = jnp.einsum(
            "hjc,chtd->hjtd",
            chooser_block,
            candidates_block[:, 1],
            preferred_element_type=jnp.float32,
        ).astype(jnp.bfloat16)
        scores = (
            jnp.einsum(
                "hid,hjtd->hijt", query_block, key_chosen, preferred_element_type=jnp.float32
            )
            * score_scale
        )
        scores = jnp.where(live_block[:, None, :, None], scores, -jnp.inf)
        row_max = jnp.max(scores, axis=(2, 3), keepdims=True)
        weights = jnp.exp(scores - row_max)
        probs = weights / jnp.sum(weights, axis=(2, 3), keepdims=True)
        probs_low = probs.astype(jnp.bfloat16)
        attention = jnp.einsum(
            "hijt,hjtd->hid", probs_low, value_chosen, preferred_element_type=jnp.float32
        ).astype(jnp.bfloat16)
        prob_grad = jnp.einsum(
            "hid,hjtd->hijt", grad_block, value_chosen, preferred_element_type=jnp.float32
        )
        delta = jnp.sum(probs * prob_grad, axis=(2, 3), keepdims=True)
        score_grad = (probs * (prob_grad - delta)).astype(jnp.bfloat16)
        query_result = (
            jnp.einsum("hijt,hjtd->hid", score_grad, key_chosen, preferred_element_type=jnp.float32)
            * score_scale
        ).astype(jnp.bfloat16)
        key_part = (
            jnp.einsum(
                "hijt,hid->hjtd", score_grad, query_block, preferred_element_type=jnp.float32
            )
            * score_scale
        ).astype(jnp.bfloat16)
        value_part = jnp.einsum(
            "hijt,hid->hjtd", probs_low, grad_block, preferred_element_type=jnp.float32
        ).astype(jnp.bfloat16)
        return (attention, query_result, key_part, value_part)

    results = lax.map(attend, jnp.arange(heads_here // 2, dtype=jnp.int32))
    attn_out = results[0].reshape(queries.shape)
    query_grad = results[1].reshape(queries.shape)
    key_part = results[2].reshape((heads_here,) + results[2].shape[2:])
    value_part = results[3].reshape((heads_here,) + results[3].shape[2:])
    key_back = jnp.einsum(
        "hjc,hjtd->chtd", chooser, key_part, preferred_element_type=jnp.float32
    ).astype(jnp.bfloat16)
    value_back = jnp.einsum(
        "hjc,hjtd->chtd", chooser, value_part, preferred_element_type=jnp.float32
    ).astype(jnp.bfloat16)
    returned_terms = jnp.stack([key_back, value_back], axis=1)
    total = returned_terms[0].astype(jnp.float32)
    for number, offset in enumerate(offsets):
        arrived = send_grads_used(
            returned_terms[number + 1], placers[number][0], placers[number][1], offset
        )
        total = total + arrived.astype(jnp.float32)
    return (attn_out, query_grad, total[0].astype(jnp.bfloat16), total[1].astype(jnp.bfloat16))


def solution(mesh):
    placed = (
        P("mp", ("clips", "seq"), None),
        P("mp", ("clips", "seq"), None),
        P("mp", ("clips", "seq"), None),
        P("mp", ("clips", "seq"), None),
        P("mp", None, None),
    )
    return jax.shard_map(
        per_device,
        mesh=mesh,
        in_specs=placed,
        out_specs=(
            P("mp", ("clips", "seq"), None),
            P("mp", ("clips", "seq"), None),
            P("mp", ("clips", "seq"), None),
            P("mp", ("clips", "seq"), None),
        ),
        check_vma=False,
    )
```

profile of v0, /device:TPU:0, one launch (start us, length us, event | category | flops | bytes accessed | tf_op | source)
XLA Modules:
  0.0 111.0 jit_solution(8116822144961996906)
XLA Ops:
  2.1 1.7 %copy_bitcast_fusion.4 = (bf16[1,6,256,128]{3,1,2,0:T(8,128)(2,1)S(1)}, bf16[1,6,256,128]{3,1,2,0:T(8,128)(2,1)S(1)}) fusion(bf16[6,256,128]{2,1,0:T(8,128)(2,1)} %param.9, bf16[6,256,128]{2,1,0:T(8,128)(2,1)} %param.8), kind=kLoop, calls=%fused_computation.89 | loop fusion | bytes 1572864 | tf_op jit(solution)/shard_map/stack | solution.py:72
  4.2 4.9 %collective-permute-start.1 = (bf16[2,3,256,128]{3,1,2,0:T(4,128)(2,1)S(1)}, bf16[2,3,256,128]{3,1,2,0:T(4,128)(2,1)S(1)}, u32[]{:S(2)}, u32[]{:S(2)}) collective-permute-start(bf16[2,3,256,128]{3,1,2,0:T(4,128)(2,1)S(1)} %fusion.55), channel_id=1, source_target_pairs={{0,2},{2,4},{4,6},{6,8},{8,10},{10,12},{12,14},{1,3},{3,5},{5,7},{... | collective-permute-start | bytes 1179656 | tf_op jit(solution)/shard_map/ppermute | solution.py:13
  10.4 1.3 %collective-permute-start = (bf16[2,3,256,128]{3,1,2,0:T(4,128)(2,1)S(1)}, bf16[2,3,256,128]{3,1,2,0:T(4,128)(2,1)S(1)}, u32[]{:S(2)}, u32[]{:S(2)}) collective-permute-start(bf16[2,3,256,128]{3,1,2,0:T(4,128)(2,1)S(1)} %fusion.54), channel_id=1, source_target_pairs={{2,0},{4,2},{6,4},{8,6},{10,8},{12,10},{14,12},{3,1},{5,3},{7,5},{... | collective-permute-start | bytes 1179656 | tf_op jit(solution)/shard_map/ppermute | solution.py:13
  12.1 1.2 %fusion.62 = bf16[1,2,6,256,128]{4,2,3,1,0:T(8,128)(2,1)} fusion(bf16[1,6,256,128]{3,1,2,0:T(8,128)(2,1)S(1)} %get-tuple-element.156, bf16[1,6,256,128]{3,1,2,0:T(8,128)(2,1)S(1)} %get-tuple-element.157), kind=kLoop, calls=%fused_computation.93 | loop fusion | flops 393216 | bytes 1572864 | tf_op jit(solution)/shard_map/stack | solution.py:84
  14.5 16.9 %collective-permute-done.1 = bf16[2,3,256,128]{3,1,2,0:T(4,128)(2,1)S(1)} collective-permute-done((bf16[2,3,256,128]{3,1,2,0:T(4,128)(2,1)S(1)}, bf16[2,3,256,128]{3,1,2,0:T(4,128)(2,1)S(1)}, u32[]{:S(2)}, u32[]{:S(2)}) %collective-permute-start.1) | collective-permute-done | bytes 393248 | tf_op jit(solution)/shard_map/ppermute | solution.py:13
  33.8 39.8 %while.16 = (s32[]{:T(128)}, bf16[3,2,256,128]{3,2,1,0:T(8,128)(2,1)}, bf16[3,2,256,128]{3,2,1,0:T(8,128)(2,1)}, bf16[3,2,4,256,128]{4,3,2,1,0:T(8,128)(2,1)}, b...) while((s32[]{:T(128)}, ...), condition=%wide.region_12.13_spmd, body=%wide.region_8.12_spmd.sunk | while | flops 825686528 | bytes 28868708 | solution.py:139
  40.1 1.5 %fusion.121 = bf16[3,2,256,128]{3,2,1,0:T(8,128)(2,1)} fusion(bf16[3,2,256,128]{3,2,1,0:T(8,128)(2,1)} %get-tuple-element.254, s32[]{:T(128)S(6)} %copy.163, bf16[2,4,256,128]{3,1,2,0:T(4,128)(2,1)S(1)} %convolution_convert_fusion.13, f32[2,256,4,256]{1,3,2,0:T(8,128)S(1)} %get-tuple-element.233, f32[2,256]{1,0:T(2,128)S(1)} %fusion.120, ...), kind=kOutput, calls=%fused_computation.24.clone.1 | convolution fusion | flops 136904704 | bytes 2756620 | tf_op jit(solution)/shard_map/while/body/eval_jaxpr/hijt,hjtd->hid/dot_general | solution.py:116
  41.6 1.5 %fusion.124 = bf16[3,2,4,256,128]{4,3,2,1,0:T(8,128)(2,1)} fusion(bf16[3,2,4,256,128]{4,3,2,1,0:T(8,128)(2,1)} %get-tuple-element.257, s32[]{:T(128)S(6)} %copy.163, bf16[6,256,128]{2,1,0:T(8,128)(2,1)S(1)} %copy-done.19, s32[]{:T(128)S(6)} %select_n.52, f32[2,256,4,256]{1,3,2,0:T(8,128)S(1)} %get-tuple-element.233, f32[2,256]{1,0:T(2,128)S(1)} %fusion.120, ...), kind=kOutput, calls=%fused_computation.15.clone.1 | convolution fusion | flops 137101312 | bytes 2757128 | tf_op jit(solution)/shard_map/while/body/eval_jaxpr/hijt,hid->hjtd/dot_general | solution.py:134
  44.6 1.2 %fusion.122 = bf16[3,2,256,128]{3,2,1,0:T(8,128)(2,1)} fusion(bf16[3,2,256,128]{3,2,1,0:T(8,128)(2,1)} %get-tuple-element.255, s32[]{:T(128)S(6)} %copy.163, bf16[2,256,4,256]{1,3,2,0:T(8,128)(2,1)S(1)} %multiply_convert_fusion.2, bf16[2,4,256,128]{3,1,2,0:T(4,128)(2,1)S(1)} %convolution_convert_fusion.14), kind=kOutput, calls=%fused_computation.22.clone.1 | convolution fusion | flops 134348800 | bytes 1703940 | tf_op jit(solution)/shard_map/while/body/eval_jaxpr/hijt,hjtd->hid/dot_general | solution.py:125
  45.8 1.2 %fusion.123 = bf16[3,2,4,256,128]{4,3,2,1,0:T(8,128)(2,1)} fusion(bf16[3,2,4,256,128]{4,3,2,1,0:T(8,128)(2,1)} %get-tuple-element.256, s32[]{:T(128)S(6)} %copy.163, bf16[2,256,4,256]{1,3,2,0:T(8,128)(2,1)S(1)} %multiply_convert_fusion.2, bf16[6,256,128]{2,1,0:T(8,128)(2,1)S(1)} %get-tuple-element.276, s32[]{:T(128)S(6)} %select_n.52), kind=kOutput, calls=%fused_computation.13.clone.1 | convolution fusion | flops 134742016 | bytes 1703944 | tf_op jit(solution)/shard_map/while/body/eval_jaxpr/hijt,hid->hjtd/dot_general | solution.py:129
  53.4 1.5 %fusion.121 = bf16[3,2,256,128]{3,2,1,0:T(8,128)(2,1)} fusion(bf16[3,2,256,128]{3,2,1,0:T(8,128)(2,1)} %get-tuple-element.254, s32[]{:T(128)S(6)} %copy.163, bf16[2,4,256,128]{3,1,2,0:T(4,128)(2,1)S(1)} %convolution_convert_fusion.13, f32[2,256,4,256]{1,3,2,0:T(8,128)S(1)} %get-tuple-element.233, f32[2,256]{1,0:T(2,128)S(1)} %fusion.120, ...), kind=kOutput, calls=%fused_computation.24.clone.1 | convolution fusion | flops 136904704 | bytes 2756620 | tf_op jit(solution)/shard_map/while/body/eval_jaxpr/hijt,hjtd->hid/dot_general | solution.py:116
  54.9 1.5 %fusion.124 = bf16[3,2,4,256,128]{4,3,2,1,0:T(8,128)(2,1)} fusion(bf16[3,2,4,256,128]{4,3,2,1,0:T(8,128)(2,1)} %get-tuple-element.257, s32[]{:T(128)S(6)} %copy.163, bf16[6,256,128]{2,1,0:T(8,128)(2,1)S(1)} %copy-done.19, s32[]{:T(128)S(6)} %select_n.52, f32[2,256,4,256]{1,3,2,0:T(8,128)S(1)} %get-tuple-element.233, f32[2,256]{1,0:T(2,128)S(1)} %fusion.120, ...), kind=kOutput, calls=%fused_computation.15.clone.1 | convolution fusion | flops 137101312 | bytes 2757128 | tf_op jit(solution)/shard_map/while/body/eval_jaxpr/hijt,hid->hjtd/dot_general | solution.py:134
  57.9 1.2 %fusion.122 = bf16[3,2,256,128]{3,2,1,0:T(8,128)(2,1)} fusion(bf16[3,2,256,128]{3,2,1,0:T(8,128)(2,1)} %get-tuple-element.255, s32[]{:T(128)S(6)} %copy.163, bf16[2,256,4,256]{1,3,2,0:T(8,128)(2,1)S(1)} %multiply_convert_fusion.2, bf16[2,4,256,128]{3,1,2,0:T(4,128)(2,1)S(1)} %convolution_convert_fusion.14), kind=kOutput, calls=%fused_computation.22.clone.1 | convolution fusion | flops 134348800 | bytes 1703940 | tf_op jit(solution)/shard_map/while/body/eval_jaxpr/hijt,hjtd->hid/dot_general | solution.py:125
  59.1 1.2 %fusion.123 = bf16[3,2,4,256,128]{4,3,2,1,0:T(8,128)(2,1)} fusion(bf16[3,2,4,256,128]{4,3,2,1,0:T(8,128)(2,1)} %get-tuple-element.256, s32[]{:T(128)S(6)} %copy.163, bf16[2,256,4,256]{1,3,2,0:T(8,128)(2,1)S(1)} %multiply_convert_fusion.2, bf16[6,256,128]{2,1,0:T(8,128)(2,1)S(1)} %get-tuple-element.276, s32[]{:T(128)S(6)} %select_n.52), kind=kOutput, calls=%fused_computation.13.clone.1 | convolution fusion | flops 134742016 | bytes 1703944 | tf_op jit(solution)/shard_map/while/body/eval_jaxpr/hijt,hid->hjtd/dot_general | solution.py:129
  66.7 1.5 %fusion.121 = bf16[3,2,256,128]{3,2,1,0:T(8,128)(2,1)} fusion(bf16[3,2,256,128]{3,2,1,0:T(8,128)(2,1)} %get-tuple-element.254, s32[]{:T(128)S(6)} %copy.163, bf16[2,4,256,128]{3,1,2,0:T(4,128)(2,1)S(1)} %convolution_convert_fusion.13, f32[2,256,4,256]{1,3,2,0:T(8,128)S(1)} %get-tuple-element.233, f32[2,256]{1,0:T(2,128)S(1)} %fusion.120, ...), kind=kOutput, calls=%fused_computation.24.clone.1 | convolution fusion | flops 136904704 | bytes 2756620 | tf_op jit(solution)/shard_map/while/body/eval_jaxpr/hijt,hjtd->hid/dot_general | solution.py:116
  68.2 1.5 %fusion.124 = bf16[3,2,4,256,128]{4,3,2,1,0:T(8,128)(2,1)} fusion(bf16[3,2,4,256,128]{4,3,2,1,0:T(8,128)(2,1)} %get-tuple-element.257, s32[]{:T(128)S(6)} %copy.163, bf16[6,256,128]{2,1,0:T(8,128)(2,1)S(1)} %copy-done.19, s32[]{:T(128)S(6)} %select_n.52, f32[2,256,4,256]{1,3,2,0:T(8,128)S(1)} %get-tuple-element.233, f32[2,256]{1,0:T(2,128)S(1)} %fusion.120, ...), kind=kOutput, calls=%fused_computation.15.clone.1 | convolution fusion | flops 137101312 | bytes 2757128 | tf_op jit(solution)/shard_map/while/body/eval_jaxpr/hijt,hid->hjtd/dot_general | solution.py:134
  71.2 1.2 %fusion.122 = bf16[3,2,256,128]{3,2,1,0:T(8,128)(2,1)} fusion(bf16[3,2,256,128]{3,2,1,0:T(8,128)(2,1)} %get-tuple-element.255, s32[]{:T(128)S(6)} %copy.163, bf16[2,256,4,256]{1,3,2,0:T(8,128)(2,1)S(1)} %multiply_convert_fusion.2, bf16[2,4,256,128]{3,1,2,0:T(4,128)(2,1)S(1)} %convolution_convert_fusion.14), kind=kOutput, calls=%fused_computation.22.clone.1 | convolution fusion | flops 134348800 | bytes 1703940 | tf_op jit(solution)/shard_map/while/body/eval_jaxpr/hijt,hjtd->hid/dot_general | solution.py:125
  72.4 1.2 %fusion.123 = bf16[3,2,4,256,128]{4,3,2,1,0:T(8,128)(2,1)} fusion(bf16[3,2,4,256,128]{4,3,2,1,0:T(8,128)(2,1)} %get-tuple-element.256, s32[]{:T(128)S(6)} %copy.163, bf16[2,256,4,256]{1,3,2,0:T(8,128)(2,1)S(1)} %multiply_convert_fusion.2, bf16[6,256,128]{2,1,0:T(8,128)(2,1)S(1)} %get-tuple-element.276, s32[]{:T(128)S(6)} %select_n.52), kind=kOutput, calls=%fused_computation.13.clone.1 | convolution fusion | flops 134742016 | bytes 1703944 | tf_op jit(solution)/shard_map/while/body/eval_jaxpr/hijt,hid->hjtd/dot_general | solution.py:129
  73.7 2.8 %fusion.49 = bf16[3,1,6,256,128]{4,0,3,2,1:T(4,128)(2,1)S(1)} fusion(bf16[6,4,256,128]{3,2,1,0:T(8,128)(2,1)} %bitcast.218, pred[6,4,3]{1,2,0:T(4,128)(4,1)} %get-tuple-element.134), kind=kOutput, calls=%fused_computation.73 | convolution fusion | flops 5308416 | bytes 2752584 | tf_op jit(solution)/shard_map/hjc,hjtd->chtd/dot_general | solution.py:147
  76.5 1.3 %fusion.46 = bf16[3,1,6,256,128]{4,0,3,2,1:T(4,128)(2,1)S(1)} fusion(bf16[6,4,256,128]{3,2,1,0:T(8,128)(2,1)S(1)} %bitcast.219, pred[6,4,3]{1,2,0:T(4,128)(4,1)S(1)} %copy-done.4), kind=kOutput, calls=%fused_computation.72 | convolution fusion | flops 5308416 | bytes 2752584 | tf_op jit(solution)/shard_map/hjc,hjtd->chtd/dot_general | solution.py:144
  77.9 4.0 %pad_maximum_fusion.1 = (bf16[1,2,6,256,128]{4,0,3,2,1:T(2,128)(2,1)S(1)}, f32[1,2,6,256,128]{4,0,3,2,1:T(1,128)S(1)}, bf16[1,2,6,256,128]{4,0,3,2,1:T(2,128)(2,1)S(1)}) fusion(bf16[3,1,6,256,128]{4,0,3,2,1:T(4,128)(2,1)S(1)} %fusion.49, bf16[3,1,6,256,128]{4,0,3,2,1:T(4,128)(2,1)S(1)} %fusion.46), kind=kLoop, calls=%fused_computation.61 | loop fusion | flops 4718592 | bytes 5505024 | tf_op jit(solution)/shard_map/stack | solution.py:150
  82.9 4.4 %collective-permute-start.2 = (bf16[2,3,256,128]{3,1,2,0:T(4,128)(2,1)S(1)}, bf16[2,3,256,128]{3,1,2,0:T(4,128)(2,1)S(1)}, u32[]{:S(2)}, u32[]{:S(2)}) collective-permute-start(bf16[2,3,256,128]{3,1,2,0:T(4,128)(2,1)S(1)} %fusion.56), channel_id=1, source_target_pairs={{0,2},{2,4},{4,6},{6,8},{8,10},{10,12},{12,14},{1,3},{3,5},{5,7},{... | collective-permute-start | bytes 1179656 | tf_op jit(solution)/shard_map/ppermute | solution.py:13
  88.3 1.3 %collective-permute-start.3 = (bf16[2,3,256,128]{3,1,2,0:T(4,128)(2,1)S(1)}, bf16[2,3,256,128]{3,1,2,0:T(4,128)(2,1)S(1)}, u32[]{:S(2)}, u32[]{:S(2)}) collective-permute-start(bf16[2,3,256,128]{3,1,2,0:T(4,128)(2,1)S(1)} %fusion.57), channel_id=1, source_target_pairs={{2,0},{4,2},{6,4},{8,6},{10,8},{12,10},{14,12},{3,1},{5,3},{7,5},{... | collective-permute-start | bytes 1179656 | tf_op jit(solution)/shard_map/ppermute | solution.py:13
  89.6 19.2 %collective-permute-done.2 = bf16[2,3,256,128]{3,1,2,0:T(4,128)(2,1)S(1)} collective-permute-done((bf16[2,3,256,128]{3,1,2,0:T(4,128)(2,1)S(1)}, bf16[2,3,256,128]{3,1,2,0:T(4,128)(2,1)S(1)}, u32[]{:S(2)}, u32[]{:S(2)}) %collective-permute-start.2) | collective-permute-done | bytes 393248 | tf_op jit(solution)/shard_map/ppermute | solution.py:13
  (126 shorter events, 32.9 us)
Async XLA Ops:
  1.9 1.9 %copy-start.9 = (pred[6]{0:T(512)(128)(4,1)}, pred[6]{0:T(512)(128)(4,1)S(1)}, u32[]{:S(2)}) copy-start(pred[6]{0:T(512)(128)(4,1)S(1)} %get-tuple-element.132) | copy-start | bytes 22
  2.1 7.0 %copy-start.13 = (s32[6]{0:T(128)}, s32[6]{0:T(128)S(1)}, u32[]{:S(2)}) copy-start(s32[6]{0:T(128)S(1)} %add_bitcast_fusion.1) | copy-start | bytes 76
  4.2 27.2 %collective-permute-start.1 = (bf16[2,3,256,128]{3,1,2,0:T(4,128)(2,1)S(1)}, bf16[2,3,256,128]{3,1,2,0:T(4,128)(2,1)S(1)}, u32[]{:S(2)}, u32[]{:S(2)}) collective-permute-start(bf16[2,3,256,128]{3,1,2,0:T(4,128)(2,1)S(1)} %fusion.55), channel_id=1, source_target_pairs={{0,2},{2,4},{4,6},{6,8},{8,10},{10,12},{12,14},{1,3},{3,5},{5,7},{... | collective-permute-start | bytes 1179656 | tf_op jit(solution)/shard_map/ppermute | solution.py:13
  10.4 21.6 %collective-permute-start = (bf16[2,3,256,128]{3,1,2,0:T(4,128)(2,1)S(1)}, bf16[2,3,256,128]{3,1,2,0:T(4,128)(2,1)S(1)}, u32[]{:S(2)}, u32[]{:S(2)}) collective-permute-start(bf16[2,3,256,128]{3,1,2,0:T(4,128)(2,1)S(1)} %fusion.54), channel_id=1, source_target_pairs={{2,0},{4,2},{6,4},{8,6},{10,8},{12,10},{14,12},{3,1},{5,3},{7,5},{... | collective-permute-start | bytes 1179656 | tf_op jit(solution)/shard_map/ppermute | solution.py:13
  12.0 20.0 %copy-start.5 = (s32[6]{0:T(128)}, s32[6]{0:T(128)S(1)}, u32[]{:S(2)}) copy-start(s32[6]{0:T(128)S(1)} %add_bitcast_fusion.2) | copy-start | bytes 76
  12.0 20.0 %copy-start.2 = (pred[6]{0:T(512)(128)(4,1)}, pred[6]{0:T(512)(128)(4,1)S(1)}, u32[]{:S(2)}) copy-start(pred[6]{0:T(512)(128)(4,1)S(1)} %get-tuple-element.130) | copy-start | bytes 22
  14.5 18.0 %copy-start = (bf16[1,2,6,256,128]{4,2,3,1,0:T(8,128)(2,1)S(1)}, bf16[1,2,6,256,128]{4,2,3,1,0:T(8,128)(2,1)}, u32[]{:S(2)}) copy-start(bf16[1,2,6,256,128]{4,2,3,1,0:T(8,128)(2,1)} %fusion.62) | copy-start | bytes 2359300
  14.5 17.5 %copy-start.7 = (s32[6]{0:T(128)}, s32[6]{0:T(128)S(1)}, u32[]{:S(2)}) copy-start(s32[6]{0:T(128)S(1)} %add_bitcast_fusion) | copy-start | bytes 76
  33.8 1.8 %copy-start.17 = (pred[6,4]{0,1:T(4,128)(4,1)}, pred[6,4]{0,1:T(4,128)(4,1)S(1)}, u32[]{:S(2)}) copy-start(pred[6,4]{0,1:T(4,128)(4,1)S(1)} %get-tuple-element.275) | copy-start | bytes 76 | tf_op jit(solution)/shard_map/while
  44.6 2.5 %copy-start.18 = (pred[6,4]{0,1:T(4,128)(4,1)S(1)}, pred[6,4]{0,1:T(4,128)(4,1)}, u32[]{:S(2)}) copy-start(pred[6,4]{0,1:T(4,128)(4,1)} %copy-done.17) | copy-start | bytes 76 | tf_op jit(solution)/shard_map/while
  57.9 2.5 %copy-start.18 = (pred[6,4]{0,1:T(4,128)(4,1)S(1)}, pred[6,4]{0,1:T(4,128)(4,1)}, u32[]{:S(2)}) copy-start(pred[6,4]{0,1:T(4,128)(4,1)} %copy-done.17) | copy-start | bytes 76 | tf_op jit(solution)/shard_map/while
  60.4 1.8 %copy-start.17 = (pred[6,4]{0,1:T(4,128)(4,1)}, pred[6,4]{0,1:T(4,128)(4,1)S(1)}, u32[]{:S(2)}) copy-start(pred[6,4]{0,1:T(4,128)(4,1)S(1)} %get-tuple-element.275) | copy-start | bytes 76 | tf_op jit(solution)/shard_map/while
  71.2 2.5 %copy-start.18 = (pred[6,4]{0,1:T(4,128)(4,1)S(1)}, pred[6,4]{0,1:T(4,128)(4,1)}, u32[]{:S(2)}) copy-start(pred[6,4]{0,1:T(4,128)(4,1)} %copy-done.17) | copy-start | bytes 76 | tf_op jit(solution)/shard_map/while
  73.7 2.8 %copy-start.4 = (pred[6,4,3]{1,2,0:T(4,128)(4,1)S(1)}, pred[6,4,3]{1,2,0:T(4,128)(4,1)}, u32[]{:S(2)}) copy-start(pred[6,4,3]{1,2,0:T(4,128)(4,1)} %get-tuple-element.134) | copy-start | bytes 220
  73.7 2.9 %copy-start.20 = (bf16[3,2,4,256,128]{4,3,2,1,0:T(8,128)(2,1)S(1)}, bf16[3,2,4,256,128]{4,3,2,1,0:T(8,128)(2,1)}, u32[]{:S(2)}) copy-start(bf16[3,2,4,256,128]{4,3,2,1,0:T(8,128)(2,1)} %get-tuple-element.66) | copy-start | bytes 4718596
  77.8 4.0 %copy-start.6 = (s32[6]{0:T(128)S(1)}, s32[6]{0:T(128)}, u32[]{:S(2)}) copy-start(s32[6]{0:T(128)} %copy-done.5) | copy-start | bytes 76
  77.8 9.5 %copy-start.3 = (pred[6]{0:T(512)(128)(4,1)S(1)}, pred[6]{0:T(512)(128)(4,1)}, u32[]{:S(2)}) copy-start(pred[6]{0:T(512)(128)(4,1)} %copy-done.2) | copy-start | bytes 22
  77.9 9.5 %copy-start.8 = (s32[6]{0:T(128)S(1)}, s32[6]{0:T(128)}, u32[]{:S(2)}) copy-start(s32[6]{0:T(128)} %copy-done.7) | copy-start | bytes 76
  81.8 27.0 %copy-start.12 = (pred[6]{0:T(512)(128)(4,1)S(1)}, pred[6]{0:T(512)(128)(4,1)}, u32[]{:S(2)}) copy-start(pred[6]{0:T(512)(128)(4,1)} %copy-done.11) | copy-start | bytes 22
  81.8 27.0 %copy-start.16 = (s32[6]{0:T(128)S(1)}, s32[6]{0:T(128)}, u32[]{:S(2)}) copy-start(s32[6]{0:T(128)} %copy-done.15) | copy-start | bytes 76
  81.9 27.5 %copy-start.10 = (pred[6]{0:T(512)(128)(4,1)S(1)}, pred[6]{0:T(512)(128)(4,1)}, u32[]{:S(2)}) copy-start(pred[6]{0:T(512)(128)(4,1)} %copy-done.9) | copy-start | bytes 22
  81.9 27.5 %copy-start.14 = (s32[6]{0:T(128)S(1)}, s32[6]{0:T(128)}, u32[]{:S(2)}) copy-start(s32[6]{0:T(128)} %copy-done.13) | copy-start | bytes 76
  82.9 25.9 %collective-permute-start.2 = (bf16[2,3,256,128]{3,1,2,0:T(4,128)(2,1)S(1)}, bf16[2,3,256,128]{3,1,2,0:T(4,128)(2,1)S(1)}, u32[]{:S(2)}, u32[]{:S(2)}) collective-permute-start(bf16[2,3,256,128]{3,1,2,0:T(4,128)(2,1)S(1)} %fusion.56), channel_id=1, source_target_pairs={{0,2},{2,4},{4,6},{6,8},{8,10},{10,12},{12,14},{1,3},{3,5},{5,7},{... | collective-permute-start | bytes 1179656 | tf_op jit(solution)/shard_map/ppermute | solution.py:13
  88.3 21.0 %collective-permute-start.3 = (bf16[2,3,256,128]{3,1,2,0:T(4,128)(2,1)S(1)}, bf16[2,3,256,128]{3,1,2,0:T(4,128)(2,1)S(1)}, u32[]{:S(2)}, u32[]{:S(2)}) collective-permute-start(bf16[2,3,256,128]{3,1,2,0:T(4,128)(2,1)S(1)} %fusion.57), channel_id=1, source_target_pairs={{2,0},{4,2},{6,4},{8,6},{10,8},{12,10},{14,12},{3,1},{5,3},{7,5},{... | collective-permute-start | bytes 1179656 | tf_op jit(solution)/shard_map/ppermute | solution.py:13
  (7 other events, 8.8 us)
where the time goes:
time: 113 us; the launch traced here: 111 us
  waiting for transfers between devices  36.1 us (32%)
  matrix products  33.3 us (29%)
  local copies, waits for them, and re-layouts  15.4 us (14%)
  starting transfers between devices  11.9 us (11%)
  other arithmetic  11.4 us (10%)
  loops' own time  1.87 us (2%)
    ppermute x4, waiting for transfers between devices, passed_along(): return lax.ppermute(block, axis, route)  36.1 us
    ppermute x4, starting transfers between devices, passed_along(): return lax.ppermute(block, axis, route)  11.9 us
    dot_general x3, matrix products, attend(): jnp.einsum('hijt,hjtd->hid', probs_low, value_chosen, preferred_element_t...  4.54 us
    dot_general x3, matrix products, attend(): jnp.einsum('hijt,hid->hjtd', probs_low, grad_block, preferred_element_typ...  4.39 us
    another operation x1, other arithmetic, per_device(): returned_terms = jnp.stack([key_back, value_back], axis=1)  3.95 us
    dynamic_slice x6, local copies, waits for them, and re-layouts, attend(): live_block = lax.dynamic_slice_in_dim(live_slots, first_head, 2, 0)  3.83 us
    dot_general x3, matrix products, attend(): jnp.einsum('hijt,hid->hjtd', score_grad, query_block, preferred_element_t...  3.72 us
    dot_general x3, matrix products, attend(): jnp.einsum('hijt,hjtd->hid', score_grad, key_chosen, preferred_element_ty...  3.66 us
  transfers between devices with their start and end apart: 4, of which 2 were waited for; matrix products, arithmetic and copies ran while one was open for 5% of the time, Pallas kernels for 0%

commit v1 on v0

v1 whole, which is shorter than its diff:
```python
import functools

import jax
import jax.numpy as jnp
from jax import lax
from jax.experimental import pallas as pl
from jax.experimental.pallas import tpu as pltpu
from jax.sharding import PartitionSpec as P

GX = 8
LOG2E = 1.4426950408889634
VMEM_LIMIT = 48 * 1024 * 1024


def channel_list(tile_count):
    row_tiles = min(4, tile_count // GX)
    layer_size = GX * row_tiles
    distances = [1]
    if row_tiles > 1:
        distances.append(GX)
    if tile_count // layer_size > 1:
        distances.append(layer_size)
    return [(distance, colour) for distance in distances for colour in (0, 1)]


def swap_route(channel, tile_count):
    distance, colour = channel
    route = []
    for low in range(tile_count - distance):
        if (low // distance) % 2 == colour:
            route += [(low, low + distance), (low + distance, low)]
    return route


def swapped(block, channel):
    return lax.ppermute(block, "seq", swap_route(channel, lax.axis_size("seq")))


def partner_of(own_tile, channel):
    distance, colour = channel
    is_low = lax.rem(lax.div(own_tile, distance), 2) == colour
    return jnp.where(is_low, own_tile + distance, own_tile - distance)


def dot_nt(a, b):
    return lax.dot_general(a, b, (((1,), (1,)), ((), ())), preferred_element_type=jnp.float32)


def dot_tn(a, b):
    return lax.dot_general(a, b, (((0,), (0,)), ((), ())), preferred_element_type=jnp.float32)


def dot_nn(a, b):
    return lax.dot_general(a, b, (((1,), (0,)), ((), ())), preferred_element_type=jnp.float32)


def pack_keys_kernel(channels, cap, lists, keys, values, table, *rest):
    targets, sems = rest[: len(channels)], rest[len(channels)]
    heads, tile_count, entries = lists.shape
    own_tile = lax.axis_index("seq")
    started = []
    for number, channel in enumerate(channels):
        partner = partner_of(own_tile, channel)
        inside = (partner >= 0) & (partner < tile_count)
        reader = jnp.clip(partner, 0, tile_count - 1)
        for slot in range(cap):
            table[heads * len(channels) + number * cap + slot] = -1
        slot = jnp.int32(0)
        pairs = []
        for head in range(heads):
            wanted = lists[head, reader, 1] == own_tile
            for entry in range(2, entries):
                wanted = wanted | (lists[head, reader, entry] == own_tile)
            wanted = wanted & inside & (slot < cap)
            pairs.append((wanted, head, slot))

            @pl.when(wanted)
            def _():
                table[heads * len(channels) + number * cap + slot] = head
                for part, source in enumerate((keys, values)):
                    pltpu.make_async_copy(
                        source.at[head], targets[number].at[part, slot], sems.at[number, part, head]
                    ).start()

            slot = slot + wanted.astype(jnp.int32)
        started.append(pairs)
    for number, channel in enumerate(channels):
        partner = partner_of(own_tile, channel)
        slot = jnp.int32(0)
        for head in range(heads):
            named = lists[head, own_tile, 1] == partner
            for entry in range(2, entries):
                named = named | (lists[head, own_tile, entry] == partner)
            named = named & (partner >= 0) & (partner < tile_count) & (slot < cap)
            table[head * len(channels) + number] = jnp.where(named, slot, -1)
            slot = slot + named.astype(jnp.int32)
    for number, pairs in enumerate(started):
        for wanted, head, slot in pairs:

            @pl.when(wanted)
            def _():
                for part, source in enumerate((keys, values)):
                    pltpu.make_async_copy(
                        source.at[head], targets[number].at[part, slot], sems.at[number, part, head]
                    ).wait()


def pack_queries_kernel(channels, cap, table, queries, grads, *rest):
    targets, sems = rest[: len(channels)], rest[len(channels)]
    heads = queries.shape[0]
    for stage in ("start", "wait"):
        for number in range(len(channels)):
            for head in range(heads):
                slot = table[head * len(channels) + number]

                @pl.when(slot >= 0)
                def _():
                    for part, source in enumerate((queries, grads)):
                        copy = pltpu.make_async_copy(
                            source.at[head],
                            targets[number].at[part, slot],
                            sems.at[number, part, head],
                        )
                        if stage == "start":
                            copy.start()
                        else:
                            copy.wait()


def attend_kernel(channels, extra, scale, table, q_ref, k_ref, v_ref, g_ref, *rest):
    count = len(channels)
    fetched = rest[:count]
    o_ref, dq_ref, dk_ref, dv_ref = rest[count : count + 4]
    stats = rest[count + 4 : 2 * count + 4]
    more_keys, more_values, row_stats = rest[2 * count + 4 :]
    head = pl.program_id(0)
    slots = [table[head * count + number] for number in range(count)]
    live = jnp.int32(0)
    for number in range(count):

        @pl.when(slots[number] >= 0)
        def _():
            more_keys[live] = fetched[number][0, slots[number]]
            more_values[live] = fetched[number][1, slots[number]]

        live = live + (slots[number] >= 0).astype(jnp.int32)

    def attend(tiles):
        query, grad = q_ref[0], g_ref[0]
        keys = [k_ref[0]] + [more_keys[tile] for tile in range(tiles)]
        values = [v_ref[0]] + [more_values[tile] for tile in range(tiles)]
        scores = [dot_nt(key, query) * (scale * LOG2E) for key in keys]
        top = functools.reduce(jnp.maximum, [jnp.max(s, axis=0, keepdims=True) for s in scores])
        weights = [jnp.exp2(s - top) for s in scores]
        total = sum(jnp.sum(w, axis=0, keepdims=True) for w in weights)
        inverse = 1.0 / total
        probs = [w * inverse for w in weights]
        prob_grads = [dot_nt(value, grad) for value in values]
        delta = sum(
            jnp.sum(p * pg, axis=0, keepdims=True) for p, pg in zip(probs, prob_grads)
        )
        probs_low = [p.astype(jnp.bfloat16) for p in probs]
        score_grads = [
            (p * (pg - delta)).astype(jnp.bfloat16) for p, pg in zip(probs, prob_grads)
        ]
        attention = sum(dot_tn(value, p) for value, p in zip(values, probs_low))
        query_grad = sum(dot_tn(key, sg) for key, sg in zip(keys, score_grads))
        o_ref[0] = attention.T.astype(jnp.bfloat16)
        dq_ref[0] = (query_grad * scale).T.astype(jnp.bfloat16)
        dk_ref[0] = (dot_nn(score_grads[0], query) * scale).astype(jnp.bfloat16)
        dv_ref[0] = dot_nn(probs_low[0], grad).astype(jnp.bfloat16)
        row_stats[0:1] = top + jnp.log2(total)
        row_stats[1:2] = delta

    for tiles in range(extra + 1):
        pl.when(live == tiles)(functools.partial(attend, tiles))
    for number in range(count):

        @pl.when(slots[number] >= 0)
        def _():
            stats[number][slots[number]] = row_stats[...]


def owner_kernel(channels, cap, scale, table, k_ref, v_ref, dk_own, dv_own, *rest):
    count = len(channels)
    arrived, stats = rest[:count], rest[count : 2 * count]
    dk_ref, dv_ref, dk_sum, dv_sum = rest[2 * count :]
    heads = k_ref.shape[0]
    for head in range(heads):
        dk_sum[head] = dk_own[head].astype(jnp.float32)
        dv_sum[head] = dv_own[head].astype(jnp.float32)
    for number in range(count):
        for slot in range(cap):
            head = table[heads * count + number * cap + slot]

            @pl.when(head >= 0)
            def _():
                query, grad = arrived[number][0, slot], arrived[number][1, slot]
                level = stats[number][slot, 0:1]
                delta = stats[number][slot, 1:2]
                score = dot_nt(k_ref[head], query) * (scale * LOG2E)
                prob = jnp.exp2(score - level)
                prob_grad = dot_nt(v_ref[head], grad)
                score_grad = (prob * (prob_grad - delta)).astype(jnp.bfloat16)
                dk_sum[head] += dot_nn(score_grad, query) * scale
                dv_sum[head] += dot_nn(prob.astype(jnp.bfloat16), grad)

    for head in range(heads):
        dk_ref[head] = dk_sum[head].astype(jnp.bfloat16)
        dv_ref[head] = dv_sum[head].astype(jnp.bfloat16)


def per_device(queries, keys, values, out_grad, tile_lists):
    heads, tokens, width = queries.shape
    tile_count = lax.axis_size("seq")
    channels = channel_list(tile_count)
    count = len(channels)
    cap = heads // 2
    extra = min(count, tile_lists.shape[2] - 1)
    scale = width ** (-0.5)
    smem = pl.BlockSpec(memory_space=pltpu.SMEM)
    anywhere = pl.BlockSpec(memory_space=pl.ANY)
    vmem = pl.BlockSpec(memory_space=pltpu.VMEM)
    params = pltpu.CompilerParams(vmem_limit_bytes=VMEM_LIMIT)
    packed = jax.ShapeDtypeStruct((2, cap, tokens, width), jnp.bfloat16)
    whole = jax.ShapeDtypeStruct((heads, tokens, width), jnp.bfloat16)
    copies = pltpu.SemaphoreType.DMA((count, 2, heads))
    table, *key_value = pl.pallas_call(
        functools.partial(pack_keys_kernel, channels, cap),
        out_shape=[jax.ShapeDtypeStruct((count * (heads + cap),), jnp.int32)] + [packed] * count,
        in_specs=[smem, anywhere, anywhere],
        out_specs=[smem] + [anywhere] * count,
        scratch_shapes=[copies],
        compiler_params=params,
        name="pack_keys",
    )(tile_lists, keys, values)
    fetched = [swapped(block, channel) for block, channel in zip(key_value, channels)]
    query_grads = pl.pallas_call(
        functools.partial(pack_queries_kernel, channels, cap),
        out_shape=[packed] * count,
        in_specs=[smem, anywhere, anywhere],
        out_specs=[anywhere] * count,
        scratch_shapes=[copies],
        compiler_params=params,
        name="pack_queries",
    )(table, queries, out_grad)
    arrived = [swapped(block, channel) for block, channel in zip(query_grads, channels)]
    row_stats = jax.ShapeDtypeStruct((cap, 2, tokens), jnp.float32)
    one_head = pl.BlockSpec((1, tokens, width), lambda head: (head, 0, 0))
    attn_out, query_grad, own_dk, own_dv, *stats = pl.pallas_call(
        functools.partial(attend_kernel, channels, extra, scale),
        grid=(heads,),
        out_shape=[whole] * 4 + [row_stats] * count,
        in_specs=[smem]
        + [one_head] * 4
        + [pl.BlockSpec((2, cap, tokens, width), lambda head: (0, 0, 0, 0))] * count,
        out_specs=[one_head] * 4
        + [pl.BlockSpec((cap, 2, tokens), lambda head: (0, 0, 0))] * count,
        scratch_shapes=[
            pltpu.VMEM((extra, tokens, width), jnp.bfloat16),
            pltpu.VMEM((extra, tokens, width), jnp.bfloat16),
            pltpu.VMEM((2, tokens), jnp.float32),
        ],
        compiler_params=params,
        name="attend",
    )(table, queries, keys, values, out_grad, *fetched)
    stats = [swapped(block, channel) for block, channel in zip(stats, channels)]
    key_grad, value_grad = pl.pallas_call(
        functools.partial(owner_kernel, channels, cap, scale),
        out_shape=[whole] * 2,
        in_specs=[smem] + [vmem] * (4 + 2 * count),
        out_specs=[vmem] * 2,
        scratch_shapes=[pltpu.VMEM((heads, tokens, width), jnp.float32)] * 2,
        compiler_params=params,
        name="owner",
    )(table, keys, values, own_dk, own_dv, *arrived, *stats)
    return attn_out, query_grad, key_grad, value_grad


def solution(mesh):
    tokens_placed = P("mp", ("clips", "seq"), None)
    return jax.shard_map(
        per_device,
        mesh=mesh,
        in_specs=(tokens_placed,) * 4 + (P("mp", None, None),),
        out_specs=(tokens_placed,) * 4,
        check_vma=False,
    )
```

time: 113 us -> 52.7 us (0.47)
  the two profiles are of different devices: /device:TPU:0 before, /device:TPU:8 now
where the time goes in v1:
time: 52.7 us; the launch traced here: 52.9 us
  waiting for transfers between devices  23.5 us (45%)
  Pallas kernels  13.8 us (26%)
  starting transfers between devices  12.1 us (23%)
  local copies, waits for them, and re-layouts  2.82 us (5%)
  between operations  0.73 us (1%)
    ppermute x6, waiting for transfers between devices, swapped(): return lax.ppermute(block, 'seq', swap_route(channel, lax.axis_size('seq')))  23.5 us
    ppermute x6, starting transfers between devices, swapped(): return lax.ppermute(block, 'seq', swap_route(channel, lax.axis_size('seq')))  12.1 us
    pallas_call x1, Pallas kernels, per_device(): pl.pallas_call(functools.partial(attend_kernel, channels, extra, scale),...  5.63 us
    pallas_call x1, Pallas kernels, per_device(): pl.pallas_call(functools.partial(owner_kernel, channels, cap, scale), out...  3.85 us
    pallas_call x1, Pallas kernels, per_device(): pl.pallas_call(functools.partial(pack_keys_kernel, channels, cap), out_sh...  3.05 us
    unnamed x13, local copies, waits for them, and re-layouts  2.82 us
    pallas_call x1, Pallas kernels, per_device(): pl.pallas_call(functools.partial(pack_queries_kernel, channels, cap), out...  1.25 us
  transfers between devices with their start and end apart: 6, of which 3 were waited for; matrix products, arithmetic and copies ran while one was open for 0% of the time, Pallas kernels for 13%

profile of v1, /device:TPU:8, one launch (start us, length us, event | category | flops | bytes accessed | tf_op | source)
XLA Modules:
  0.0 52.9 jit_solution(15011426128264526764)
XLA Ops:
  0.6 0.8 %copy.9.lists = s32[6,8,4]{2,1,0:T(8,128)S(1)} copy(s32[6,8,4]{1,2,0:T(4,128)} %param.9) | data formatting | bytes 1536 | tf_op args[4]
  1.4 1.0 %copy-done = bf16[6,256,128]{2,1,0:T(8,128)(2,1)S(1)} copy-done((bf16[6,256,128]{2,1,0:T(8,128)(2,1)S(1)}, bf16[6,256,128]{2,1,0:T(8,128)(2,1)}, u32[]{:S(2)}) %copy-start) | copy-done | bytes 393240
  2.4 1.0 %copy-done.2 = bf16[6,256,128]{2,1,0:T(8,128)(2,1)S(1)} copy-done((bf16[6,256,128]{2,1,0:T(8,128)(2,1)S(1)}, bf16[6,256,128]{2,1,0:T(8,128)(2,1)}, u32[]{:S(2)}) %copy-start.2) | copy-done | bytes 393240
  3.4 3.0 %pack_keys.1 = (s32[18]{0:T(128)S(1)}, bf16[2,3,256,128]{3,2,1,0:T(8,128)(2,1)S(1)}, bf16[2,3,256,128]{3,2,1,0:T(8,128)(2,1)S(1)}) custom-call(s32[6,8,4]{2,1,0:T(8,128)S(1)} %copy.9.lists, bf16[6,256,128]{2,1,0:T(8,128)(2,1)S(1)} %copy-done, bf16[6,256,128]{2,1,0:T(8,128)(2,1)S(1)} %copy-done.2), custom_call_target="tpu_custom_call" | custom-call | tf_op jit(solution)/shard_map/pack_keys/pallas_call | solution.py:228
  6.5 1.1 %collective-permute-start = (bf16[2,3,256,128]{3,2,1,0:T(8,128)(2,1)S(1)}, bf16[2,3,256,128]{3,2,1,0:T(8,128)(2,1)S(1)}, u32[]{:S(2)}, u32[]{:S(2)}) collective-permute-start(bf16[2,3,256,128]{3,2,1,0:T(8,128)(2,1)S(1)} %get-tuple-element.18), channel_id=1, source_target_pairs={{0,2},{2,0},{4,6},{6,4},{8,10},{10,8},{12,14},{14,12},{1,3},{3,1},... | collective-permute-start | bytes 1179656 | tf_op jit(solution)/shard_map/ppermute | solution.py:36
  7.5 2.0 %collective-permute-start.1 = (bf16[2,3,256,128]{3,2,1,0:T(8,128)(2,1)S(1)}, bf16[2,3,256,128]{3,2,1,0:T(8,128)(2,1)S(1)}, u32[]{:S(2)}, u32[]{:S(2)}) collective-permute-start(bf16[2,3,256,128]{3,2,1,0:T(8,128)(2,1)S(1)} %get-tuple-element.19), channel_id=1, source_target_pairs={{2,4},{4,2},{6,8},{8,6},{10,12},{12,10},{3,5},{5,3},{7,9},{9,7},{1... | collective-permute-start | bytes 1179656 | tf_op jit(solution)/shard_map/ppermute | solution.py:36
  9.5 0.0 copy-done.4
  9.5 0.0 copy-done.5
  9.5 0.0 copy-start.1
  9.6 0.0 copy-start.3
  9.6 1.3 %pack_queries.1 = (bf16[2,3,256,128]{3,2,1,0:T(8,128)(2,1)S(1)}, bf16[2,3,256,128]{3,2,1,0:T(8,128)(2,1)S(1)}) custom-call(s32[18]{0:T(128)S(1)} %get-tuple-element.17.table, bf16[6,256,128]{2,1,0:T(8,128)(2,1)S(1)} %copy-done.4, bf16[6,256,128]{2,1,0:T(8,128)(2,1)S(1)} %copy-done.5), custom_call_target="tpu_custom_call" | custom-call | tf_op jit(solution)/shard_map/pack_queries/pallas_call | solution.py:238
  10.8 3.7 %collective-permute-start.2 = (bf16[2,3,256,128]{3,2,1,0:T(8,128)(2,1)S(1)}, bf16[2,3,256,128]{3,2,1,0:T(8,128)(2,1)S(1)}, u32[]{:S(2)}, u32[]{:S(2)}) collective-permute-start(bf16[2,3,256,128]{3,2,1,0:T(8,128)(2,1)S(1)} %get-tuple-element.24), channel_id=1, source_target_pairs={{0,2},{2,0},{4,6},{6,4},{8,10},{10,8},{12,14},{14,12},{1,3},{3,1},... | collective-permute-start | bytes 1179656 | tf_op jit(solution)/shard_map/ppermute | solution.py:36
  14.5 1.9 %collective-permute-start.3 = (bf16[2,3,256,128]{3,2,1,0:T(8,128)(2,1)S(1)}, bf16[2,3,256,128]{3,2,1,0:T(8,128)(2,1)S(1)}, u32[]{:S(2)}, u32[]{:S(2)}) collective-permute-start(bf16[2,3,256,128]{3,2,1,0:T(8,128)(2,1)S(1)} %get-tuple-element.25), channel_id=1, source_target_pairs={{2,4},{4,2},{6,8},{8,6},{10,12},{12,10},{3,5},{5,3},{7,9},{9,7},{1... | collective-permute-start | bytes 1179656 | tf_op jit(solution)/shard_map/ppermute | solution.py:36
  16.4 19.0 %collective-permute-done.rest_0_ = bf16[2,3,256,128]{3,2,1,0:T(8,128)(2,1)S(1)} collective-permute-done((bf16[2,3,256,128]{3,2,1,0:T(8,128)(2,1)S(1)}, bf16[2,3,256,128]{3,2,1,0:T(8,128)(2,1)S(1)}, u32[]{:S(2)}, u32[]{:S(2)}) %collective-permute-start) | collective-permute-done | bytes 393248 | tf_op jit(solution)/shard_map/ppermute | solution.py:36
  35.4 0.0 collective-permute-done.1.rest_1_
  35.4 0.0 copy-done.1
  35.4 5.6 %attend.1 = (bf16[6,256,128]{2,1,0:T(8,128)(2,1)}, bf16[6,256,128]{2,1,0:T(8,128)(2,1)}, bf16[6,256,128]{2,1,0:T(8,128)(2,1)S(1)}, bf16[6,256,128]{2,1,0:T(8,128...) custom-call(s32[18]{0:T(128)S(1)} %get-tuple-element.17.table, bf16[6,256,128]{2,1,0:T(8,128)(2,1)S(1)} %copy-done.4, ...), custom_call_target="tpu_custom_call" | custom-call | tf_op jit(solution)/shard_map/attend/pallas_call | solution.py:250
  41.1 1.6 %collective-permute-start.4 = (f32[3,2,256]{2,1,0:T(2,128)S(1)}, f32[3,2,256]{2,1,0:T(2,128)S(1)}, u32[]{:S(2)}, u32[]{:S(2)}) collective-permute-start(f32[3,2,256]{2,1,0:T(2,128)S(1)} %get-tuple-element.26), channel_id=1, source_target_pairs={{0,2},{2,0},{4,6},{6,4},{8,10},{10,8},{12,14},{14,12},{1,3},{3,1},... | collective-permute-start | bytes 18440 | tf_op jit(solution)/shard_map/ppermute | solution.py:36
  42.7 1.9 %collective-permute-start.5 = (f32[3,2,256]{2,1,0:T(2,128)S(1)}, f32[3,2,256]{2,1,0:T(2,128)S(1)}, u32[]{:S(2)}, u32[]{:S(2)}) collective-permute-start(f32[3,2,256]{2,1,0:T(2,128)S(1)} %get-tuple-element.27), channel_id=1, source_target_pairs={{2,4},{4,2},{6,8},{8,6},{10,12},{12,10},{3,5},{5,3},{7,9},{9,7},{1... | collective-permute-start | bytes 18440 | tf_op jit(solution)/shard_map/ppermute | solution.py:36
  44.6 0.0 collective-permute-done.2.rest_0_
  44.6 0.0 collective-permute-done.3.rest_1_
  44.6 0.1 collective-permute-done.4.rest_2_
  44.7 4.4 %collective-permute-done.5.rest_3_ = f32[3,2,256]{2,1,0:T(2,128)S(1)} collective-permute-done((f32[3,2,256]{2,1,0:T(2,128)S(1)}, f32[3,2,256]{2,1,0:T(2,128)S(1)}, u32[]{:S(2)}, u32[]{:S(2)}) %collective-permute-start.5) | collective-permute-done | bytes 6176 | tf_op jit(solution)/shard_map/ppermute | solution.py:36
  49.1 3.8 %owner.1 = (bf16[6,256,128]{2,1,0:T(8,128)(2,1)}, bf16[6,256,128]{2,1,0:T(8,128)(2,1)}) custom-call(s32[18]{0:T(128)S(1)} %get-tuple-element.17.table, bf16[6,256,128]{2,1,0:T(8,128)(2,1)S(1)} %copy-done.1, bf16[6,256,128]{2,1,0:T(8,128)(2,1)S(1)} %copy-done.3, bf16[6,256,128]{2,1,0:T(8,128)(2,1)S(1)} %get-tuple-element.22.dk_own, ...), custom_call_target="tpu_custom_call" | custom-call | tf_op jit(solution)/shard_map/owner/pallas_call | solution.py:268
  (5 shorter events, 0.0 us)
Async XLA Ops:
  1.4 1.0 %copy-start = (bf16[6,256,128]{2,1,0:T(8,128)(2,1)S(1)}, bf16[6,256,128]{2,1,0:T(8,128)(2,1)}, u32[]{:S(2)}) copy-start(bf16[6,256,128]{2,1,0:T(8,128)(2,1)} %k_ref.3) | copy-start | bytes 1179652
  2.4 1.0 %copy-start.2 = (bf16[6,256,128]{2,1,0:T(8,128)(2,1)S(1)}, bf16[6,256,128]{2,1,0:T(8,128)(2,1)}, u32[]{:S(2)}) copy-start(bf16[6,256,128]{2,1,0:T(8,128)(2,1)} %v_ref.3) | copy-start | bytes 1179652
  3.4 6.1 %copy-start.4 = (bf16[6,256,128]{2,1,0:T(8,128)(2,1)S(1)}, bf16[6,256,128]{2,1,0:T(8,128)(2,1)}, u32[]{:S(2)}) copy-start(bf16[6,256,128]{2,1,0:T(8,128)(2,1)} %queries.1) | copy-start | bytes 1179652
  3.4 6.1 %copy-start.5 = (bf16[6,256,128]{2,1,0:T(8,128)(2,1)S(1)}, bf16[6,256,128]{2,1,0:T(8,128)(2,1)}, u32[]{:S(2)}) copy-start(bf16[6,256,128]{2,1,0:T(8,128)(2,1)} %grads.1) | copy-start | bytes 1179652
  6.5 28.9 %collective-permute-start = (bf16[2,3,256,128]{3,2,1,0:T(8,128)(2,1)S(1)}, bf16[2,3,256,128]{3,2,1,0:T(8,128)(2,1)S(1)}, u32[]{:S(2)}, u32[]{:S(2)}) collective-permute-start(bf16[2,3,256,128]{3,2,1,0:T(8,128)(2,1)S(1)} %get-tuple-element.18), channel_id=1, source_target_pairs={{0,2},{2,0},{4,6},{6,4},{8,10},{10,8},{12,14},{14,12},{1,3},{3,1},... | collective-permute-start | bytes 1179656 | tf_op jit(solution)/shard_map/ppermute | solution.py:36
  7.5 27.9 %collective-permute-start.1 = (bf16[2,3,256,128]{3,2,1,0:T(8,128)(2,1)S(1)}, bf16[2,3,256,128]{3,2,1,0:T(8,128)(2,1)S(1)}, u32[]{:S(2)}, u32[]{:S(2)}) collective-permute-start(bf16[2,3,256,128]{3,2,1,0:T(8,128)(2,1)S(1)} %get-tuple-element.19), channel_id=1, source_target_pairs={{2,4},{4,2},{6,8},{8,6},{10,12},{12,10},{3,5},{5,3},{7,9},{9,7},{1... | collective-permute-start | bytes 1179656 | tf_op jit(solution)/shard_map/ppermute | solution.py:36
  9.5 25.9 %copy-start.1 = (bf16[6,256,128]{2,1,0:T(8,128)(2,1)S(1)}, bf16[6,256,128]{2,1,0:T(8,128)(2,1)}, u32[]{:S(2)}) copy-start(bf16[6,256,128]{2,1,0:T(8,128)(2,1)} %k_ref.3) | copy-start | bytes 1179652
  9.6 25.9 %copy-start.3 = (bf16[6,256,128]{2,1,0:T(8,128)(2,1)S(1)}, bf16[6,256,128]{2,1,0:T(8,128)(2,1)}, u32[]{:S(2)}) copy-start(bf16[6,256,128]{2,1,0:T(8,128)(2,1)} %v_ref.3) | copy-start | bytes 1179652
  10.8 33.8 %collective-permute-start.2 = (bf16[2,3,256,128]{3,2,1,0:T(8,128)(2,1)S(1)}, bf16[2,3,256,128]{3,2,1,0:T(8,128)(2,1)S(1)}, u32[]{:S(2)}, u32[]{:S(2)}) collective-permute-start(bf16[2,3,256,128]{3,2,1,0:T(8,128)(2,1)S(1)} %get-tuple-element.24), channel_id=1, source_target_pairs={{0,2},{2,0},{4,6},{6,4},{8,10},{10,8},{12,14},{14,12},{1,3},{3,1},... | collective-permute-start | bytes 1179656 | tf_op jit(solution)/shard_map/ppermute | solution.py:36
  14.5 30.1 %collective-permute-start.3 = (bf16[2,3,256,128]{3,2,1,0:T(8,128)(2,1)S(1)}, bf16[2,3,256,128]{3,2,1,0:T(8,128)(2,1)S(1)}, u32[]{:S(2)}, u32[]{:S(2)}) collective-permute-start(bf16[2,3,256,128]{3,2,1,0:T(8,128)(2,1)S(1)} %get-tuple-element.25), channel_id=1, source_target_pairs={{2,4},{4,2},{6,8},{8,6},{10,12},{12,10},{3,5},{5,3},{7,9},{9,7},{1... | collective-permute-start | bytes 1179656 | tf_op jit(solution)/shard_map/ppermute | solution.py:36
  41.1 3.6 %collective-permute-start.4 = (f32[3,2,256]{2,1,0:T(2,128)S(1)}, f32[3,2,256]{2,1,0:T(2,128)S(1)}, u32[]{:S(2)}, u32[]{:S(2)}) collective-permute-start(f32[3,2,256]{2,1,0:T(2,128)S(1)} %get-tuple-element.26), channel_id=1, source_target_pairs={{0,2},{2,0},{4,6},{6,4},{8,10},{10,8},{12,14},{14,12},{1,3},{3,1},... | collective-permute-start | bytes 18440 | tf_op jit(solution)/shard_map/ppermute | solution.py:36
  42.7 6.4 %collective-permute-start.5 = (f32[3,2,256]{2,1,0:T(2,128)S(1)}, f32[3,2,256]{2,1,0:T(2,128)S(1)}, u32[]{:S(2)}, u32[]{:S(2)}) collective-permute-start(f32[3,2,256]{2,1,0:T(2,128)S(1)} %get-tuple-element.27), channel_id=1, source_target_pairs={{2,4},{4,2},{6,8},{8,6},{10,12},{12,10},{3,5},{5,3},{7,9},{9,7},{1... | collective-permute-start | bytes 18440 | tf_op jit(solution)/shard_map/ppermute | solution.py:36

commit v2 on v1

v2 whole, which is shorter than its diff:
```python
import functools

import jax
import jax.numpy as jnp
from jax import lax
from jax.experimental import pallas as pl
from jax.experimental.pallas import tpu as pltpu
from jax.sharding import PartitionSpec as P

GX = 8
LOG2E = 1.4426950408889634
LOWEST = -3.0e38
VMEM_LIMIT = 24 * 1024 * 1024


def channel_list(tile_count):
    row_tiles = min(4, tile_count // GX)
    layer_size = GX * row_tiles
    distances = [1]
    if row_tiles > 1:
        distances.append(GX)
    if tile_count // layer_size > 1:
        distances.append(layer_size)
    return [(distance, colour) for distance in distances for colour in (0, 1)]


def swap_route(channel, tile_count):
    distance, colour = channel
    route = []
    for low in range(tile_count - distance):
        if (low // distance) % 2 == colour:
            route += [(low, low + distance), (low + distance, low)]
    return route


def swapped(block, channel):
    return lax.ppermute(block, "seq", swap_route(channel, lax.axis_size("seq")))


def partner_of(own_tile, channel):
    distance, colour = channel
    is_low = lax.rem(lax.div(own_tile, distance), 2) == colour
    return jnp.where(is_low, own_tile + distance, own_tile - distance)


def dot_nt(a, b):
    return lax.dot_general(a, b, (((1,), (1,)), ((), ())), preferred_element_type=jnp.float32)


def dot_tn(a, b):
    return lax.dot_general(a, b, (((0,), (0,)), ((), ())), preferred_element_type=jnp.float32)


def dot_nn(a, b):
    return lax.dot_general(a, b, (((1,), (0,)), ((), ())), preferred_element_type=jnp.float32)


class Table:
    def __init__(self, ref, heads, count, cap):
        self.ref, self.heads, self.count, self.cap = ref, heads, count, cap

    def slot_at(self, head, number):
        return head * self.count + number

    def reader_at(self, number, slot):
        return self.heads * self.count + number * self.cap + slot

    def owner_at(self, number, slot):
        return self.reader_at(self.count + number, slot)

    def size(self):
        return self.owner_at(self.count - 1, self.cap - 1) + 1


def pack_keys_kernel(channels, cap, lists, keys, values, table_ref, *rest):
    *targets, sems = rest
    heads, entries, tile_count = lists.shape
    count = len(channels)
    table = Table(table_ref, heads, count, cap)
    own_tile = lax.axis_index("seq")
    started = []
    for number, channel in enumerate(channels):
        partner = partner_of(own_tile, channel)
        inside = (partner >= 0) & (partner < tile_count)
        reader = jnp.clip(partner, 0, tile_count - 1)
        for slot in range(cap):
            table_ref[table.owner_at(number, slot)] = -1
            table_ref[table.reader_at(number, slot)] = -1
        slot = jnp.int32(0)
        for head in range(heads):
            wanted = lists[head, 1, reader] == own_tile
            for entry in range(2, entries):
                wanted = wanted | (lists[head, entry, reader] == own_tile)
            wanted = wanted & inside & (slot < cap)

            @pl.when(wanted)
            def _():
                table_ref[table.owner_at(number, slot)] = head
                for part, source in enumerate((keys, values)):
                    pltpu.make_async_copy(
                        source.at[head], targets[number].at[part, slot], sems.at[number, part, slot]
                    ).start()

            slot = slot + wanted.astype(jnp.int32)
        started.append(slot)
    for number, channel in enumerate(channels):
        partner = partner_of(own_tile, channel)
        slot = jnp.int32(0)
        for head in range(heads):
            named = lists[head, 1, own_tile] == partner
            for entry in range(2, entries):
                named = named | (lists[head, entry, own_tile] == partner)
            named = named & (partner >= 0) & (partner < tile_count) & (slot < cap)
            table_ref[table.slot_at(head, number)] = jnp.where(named, slot, -1)

            @pl.when(named)
            def _():
                table_ref[table.reader_at(number, slot)] = head

            slot = slot + named.astype(jnp.int32)
    for number in range(count):
        for slot in range(cap):

            @pl.when(slot < started[number])
            def _():
                for part, source in enumerate((keys, values)):
                    pltpu.make_async_copy(
                        source.at[0], targets[number].at[part, slot], sems.at[number, part, slot]
                    ).wait()


def own_kernel(count, cap, scale, table_ref, q_ref, k_ref, v_ref, g_ref, queries, grads, *rest):
    weight_ref, prob_grad_ref, rows_ref, *targets, sems = rest
    heads = queries.shape[0]
    table = Table(table_ref, heads, count, cap)

    def copies(stage):
        for number in range(count):
            for slot in range(cap):
                head = table_ref[table.reader_at(number, slot)]

                @pl.when(head >= 0)
                def _():
                    for part, source in enumerate((queries, grads)):
                        copy = pltpu.make_async_copy(
                            source.at[head],
                            targets[number].at[part, slot],
                            sems.at[number, part, slot],
                        )
                        if stage == "start":
                            copy.start()
                        else:
                            copy.wait()

    pl.when(pl.program_id(0) == 0)(lambda: copies("start"))
    score = dot_nt(k_ref[0], q_ref[0]) * (scale * LOG2E)
    top = jnp.max(score, axis=0, keepdims=True)
    weight = jnp.exp2(score - top)
    prob_grad = dot_nt(v_ref[0], g_ref[0])
    weight_ref[0] = weight
    prob_grad_ref[0] = prob_grad
    rows_ref[0, 0:1] = top
    rows_ref[0, 1:2] = jnp.sum(weight, axis=0, keepdims=True)
    rows_ref[0, 2:3] = jnp.sum(weight * prob_grad, axis=0, keepdims=True)
    pl.when(pl.program_id(0) == heads - 1)(lambda: copies("wait"))


def statistics_kernel(count, cap, scale, table_ref, q_ref, g_ref, own_rows, *rest):
    fetched, rest = rest[:count], rest[count:]
    weight_ref, prob_grad_ref, own_factors, far_factors = rest[:4]
    stats, far_rows = rest[4 : 4 + count], rest[4 + count]
    heads = q_ref.shape[0]
    table = Table(table_ref, heads, count, cap)
    for number in range(count):
        for slot in range(cap):
            head = jnp.maximum(table_ref[table.reader_at(number, slot)], 0)
            place = number * cap + slot
            score = dot_nt(fetched[number][0, slot], q_ref[head]) * (scale * LOG2E)
            top = jnp.max(score, axis=0, keepdims=True)
            weight = jnp.exp2(score - top)
            prob_grad = dot_nt(fetched[number][1, slot], g_ref[head])
            weight_ref[place] = weight
            prob_grad_ref[place] = prob_grad
            far_rows[place, 0:1] = top
            far_rows[place, 1:2] = jnp.sum(weight, axis=0, keepdims=True)
            far_rows[place, 2:3] = jnp.sum(weight * prob_grad, axis=0, keepdims=True)
    for head in range(heads):
        rows = [own_rows[head]]
        slots = [table_ref[table.slot_at(head, number)] for number in range(count)]
        for number in range(count):
            found = far_rows[number * cap + jnp.maximum(slots[number], 0)]
            missing = jnp.where(
                lax.broadcasted_iota(jnp.int32, found.shape, 0) == 0, LOWEST, 0.0
            )
            rows.append(jnp.where(slots[number] >= 0, found, missing))
        top = functools.reduce(jnp.maximum, [row[0:1] for row in rows])
        factors = [jnp.exp2(row[0:1] - top) for row in rows]
        total = sum(factor * row[1:2] for factor, row in zip(factors, rows))
        inverse = 1.0 / total
        delta = sum(factor * row[2:3] for factor, row in zip(factors, rows)) * inverse
        level = top + jnp.log2(total)
        own_factors[head, 0:1] = factors[0] * inverse
        own_factors[head, 1:2] = delta
        for number in range(count):

            @pl.when(slots[number] >= 0)
            def _():
                place = number * cap + slots[number]
                far_factors[place, 0:1] = factors[1 + number] * inverse
                far_factors[place, 1:2] = delta
                stats[number][slots[number], 0:1] = level
                stats[number][slots[number], 1:2] = delta


def reader_kernel(count, cap, scale, table_ref, q_ref, k_ref, v_ref, g_ref, *rest):
    own_weight, own_prob_grad, own_factors, far_weight, far_prob_grad, far_factors = rest[:6]
    fetched, rest = rest[6 : 6 + count], rest[6 + count :]
    o_ref, dq_ref, dk_ref, dv_ref, o_sum, dq_sum = rest
    heads = q_ref.shape[0]
    table = Table(table_ref, heads, count, cap)

    def softmax_grad(weight, prob_grad, factors):
        prob = weight * factors[0:1]
        score_grad = prob * (prob_grad - factors[1:2])
        return prob.astype(jnp.bfloat16), score_grad.astype(jnp.bfloat16)

    for head in range(heads):
        prob, score_grad = softmax_grad(own_weight[head], own_prob_grad[head], own_factors[head])
        o_sum[head] = dot_tn(v_ref[head], prob)
        dq_sum[head] = dot_tn(k_ref[head], score_grad)
        dk_ref[head] = dot_nn(score_grad, q_ref[head]) * scale
        dv_ref[head] = dot_nn(prob, g_ref[head])
    for number in range(count):
        for slot in range(cap):
            head = table_ref[table.reader_at(number, slot)]
            place = number * cap + slot

            @pl.when(head >= 0)
            def _():
                prob, score_grad = softmax_grad(
                    far_weight[place], far_prob_grad[place], far_factors[place]
                )
                o_sum[head] += dot_tn(fetched[number][1, slot], prob)
                dq_sum[head] += dot_tn(fetched[number][0, slot], score_grad)

    for head in range(heads):
        o_ref[head] = o_sum[head].T.astype(jnp.bfloat16)
        dq_ref[head] = (dq_sum[head] * scale).T.astype(jnp.bfloat16)


def owner_kernel(count, cap, scale, number, table_ref, k_ref, v_ref, dk_in, dv_in, *rest):
    arrived, stats, dk_ref, dv_ref, dk_sum, dv_sum = rest
    heads = k_ref.shape[0]
    table = Table(table_ref, heads, count, cap)
    for head in range(heads):
        dk_sum[head] = dk_in[head]
        dv_sum[head] = dv_in[head]
    for slot in range(cap):
        found = table_ref[table.owner_at(number, slot)]
        head = jnp.maximum(found, 0)
        query, grad = arrived[0, slot], arrived[1, slot]
        score = dot_nt(k_ref[head], query) * (scale * LOG2E)
        prob = jnp.exp2(score - stats[slot, 0:1])
        prob_grad = dot_nt(v_ref[head], grad)
        score_grad = (prob * (prob_grad - stats[slot, 1:2])).astype(jnp.bfloat16)
        dk_term = dot_nn(score_grad, query) * scale
        dv_term = dot_nn(prob.astype(jnp.bfloat16), grad)
        dk_sum[head] += jnp.where(found >= 0, dk_term, 0.0)
        dv_sum[head] += jnp.where(found >= 0, dv_term, 0.0)
    for head in range(heads):
        dk_ref[head] = dk_sum[head].astype(dk_ref.dtype)
        dv_ref[head] = dv_sum[head].astype(dv_ref.dtype)


def per_device(queries, keys, values, out_grad, tile_lists):
    heads, tokens, width = queries.shape
    channels = channel_list(lax.axis_size("seq"))
    count = len(channels)
    cap = heads // 2
    scale = width ** (-0.5)
    table_size = Table(None, heads, count, cap).size()
    smem = pl.BlockSpec(memory_space=pltpu.SMEM)
    anywhere = pl.BlockSpec(memory_space=pl.ANY)
    vmem = pl.BlockSpec(memory_space=pltpu.VMEM)
    params = pltpu.CompilerParams(vmem_limit_bytes=VMEM_LIMIT)
    packed = pltpu.VMEM((2, cap, tokens, width), jnp.bfloat16)
    whole = jax.ShapeDtypeStruct((heads, tokens, width), jnp.bfloat16)
    whole_sum = pltpu.VMEM((heads, tokens, width), jnp.float32)
    squares = pltpu.VMEM((heads, tokens, tokens), jnp.float32)
    far_squares = pltpu.VMEM((count * cap, tokens, tokens), jnp.float32)
    row_stats = pltpu.VMEM((cap, 2, tokens), jnp.float32)
    copies = pltpu.SemaphoreType.DMA((count, 2, cap))
    lists, q_far, k_far, v_far, g_far = (
        pltpu.with_memory_space_constraint(array, pltpu.HBM)
        for array in (jnp.swapaxes(tile_lists, 1, 2), queries, keys, values, out_grad)
    )
    table, *key_value = pl.pallas_call(
        functools.partial(pack_keys_kernel, channels, cap),
        out_shape=[jax.ShapeDtypeStruct((table_size,), jnp.int32)] + [packed] * count,
        in_specs=[smem, anywhere, anywhere],
        out_specs=[smem] + [vmem] * count,
        scratch_shapes=[copies],
        compiler_params=params,
        name="pack_keys",
    )(lists, k_far, v_far)
    fetched = [swapped(block, channel) for block, channel in zip(key_value, channels)]
    one_head = pl.BlockSpec((1, tokens, width), lambda head: (head, 0, 0))
    one_square = pl.BlockSpec((1, tokens, tokens), lambda head: (head, 0, 0))
    own_weight, own_prob_grad, own_rows, *query_grads = pl.pallas_call(
        functools.partial(own_kernel, count, cap, scale),
        grid=(heads,),
        out_shape=[squares] * 2 + [pltpu.VMEM((heads, 3, tokens), jnp.float32)] + [packed] * count,
        in_specs=[smem] + [one_head] * 4 + [anywhere] * 2,
        out_specs=[one_square] * 2
        + [pl.BlockSpec((1, 3, tokens), lambda head: (head, 0, 0))]
        + [pl.BlockSpec(memory_space=pltpu.VMEM)] * count,
        scratch_shapes=[copies],
        compiler_params=params,
        name="own_scores",
    )(table, q_far, k_far, v_far, g_far, q_far, g_far)
    arrived = [swapped(block, channel) for block, channel in zip(query_grads, channels)]
    far_weight, far_prob_grad, own_factors, far_factors, *stats = pl.pallas_call(
        functools.partial(statistics_kernel, count, cap, scale),
        out_shape=[far_squares] * 2
        + [pltpu.VMEM((heads, 2, tokens), jnp.float32)]
        + [pltpu.VMEM((count * cap, 2, tokens), jnp.float32)]
        + [row_stats] * count,
        in_specs=[smem] + [vmem] * (3 + count),
        out_specs=[vmem] * (4 + count),
        scratch_shapes=[pltpu.VMEM((count * cap, 3, tokens), jnp.float32)],
        compiler_params=params,
        name="statistics",
    )(table, queries, out_grad, own_rows, *fetched)
    stats = [swapped(block, channel) for block, channel in zip(stats, channels)]
    transposed_sums = pltpu.VMEM((heads, width, tokens), jnp.float32)
    attn_out, query_grad, key_sum, value_sum = pl.pallas_call(
        functools.partial(reader_kernel, count, cap, scale),
        out_shape=[whole] * 2 + [whole_sum] * 2,
        in_specs=[smem] + [vmem] * (10 + count),
        out_specs=[vmem] * 4,
        scratch_shapes=[transposed_sums] * 2,
        compiler_params=params,
        name="reader",
    )(
        table,
        queries,
        keys,
        values,
        out_grad,
        own_weight,
        own_prob_grad,
        own_factors,
        far_weight,
        far_prob_grad,
        far_factors,
        *fetched,
    )
    for number in range(count):
        last = number == count - 1
        key_sum, value_sum = pl.pallas_call(
            functools.partial(owner_kernel, count, cap, scale, number),
            out_shape=[whole if last else whole_sum] * 2,
            in_specs=[smem] + [vmem] * 6,
            out_specs=[vmem] * 2,
            scratch_shapes=[whole_sum] * 2,
            compiler_params=params,
            name="owner",
        )(table, keys, values, key_sum, value_sum, arrived[number], stats[number])
    return attn_out, query_grad, key_sum, value_sum


def solution(mesh):
    tokens_placed = P("mp", ("clips", "seq"), None)
    return jax.shard_map(
        per_device,
        mesh=mesh,
        in_specs=(tokens_placed,) * 4 + (P("mp", None, None),),
        out_specs=(tokens_placed,) * 4,
        check_vma=False,
    )
```

time: 52.7 us -> 46.9 us (0.89)
  the two profiles are of different devices: /device:TPU:8 before, /device:TPU:14 now
where the time goes in v2:
time: 46.9 us; the launch traced here: 46.1 us
  Pallas kernels  16 us (34%)
  starting transfers between devices  14.7 us (31%)
  waiting for transfers between devices  14.6 us (31%)
  between operations  0.76 us (2%)
    ppermute x6, starting transfers between devices, swapped(): return lax.ppermute(block, 'seq', swap_route(channel, lax.axis_size('seq')))  14.7 us
    ppermute x6, waiting for transfers between devices, swapped(): return lax.ppermute(block, 'seq', swap_route(channel, lax.axis_size('seq')))  14.6 us
    pallas_call x1, Pallas kernels, per_device(): pl.pallas_call(functools.partial(own_kernel, count, cap, scale), grid=(he...  4.51 us
    pallas_call x2, Pallas kernels, per_device(): pl.pallas_call(functools.partial(owner_kernel, count, cap, scale, number)...  3.81 us
    pallas_call x1, Pallas kernels, per_device(): pl.pallas_call(functools.partial(reader_kernel, count, cap, scale), out_s...  3.25 us
    pallas_call x1, Pallas kernels, per_device(): pl.pallas_call(functools.partial(pack_keys_kernel, channels, cap), out_sh...  2.95 us
    pallas_call x1, Pallas kernels, per_device(): pl.pallas_call(functools.partial(statistics_kernel, count, cap, scale), o...  1.44 us
  transfers between devices with their start and end apart: 6, of which 1 were waited for; matrix products, arithmetic and copies ran while one was open for 0% of the time, Pallas kernels for 23%

profile of v2, /device:TPU:14, one launch (start us, length us, event | category | flops | bytes accessed | tf_op | source)
XLA Modules:
  0.0 46.1 jit_solution(8699181670009558435)
XLA Ops:
  0.6 0.0 copy-start.2
  0.6 0.0 copy-start.3
  0.7 3.0 %pack_keys.1 = (s32[24]{0:T(128)S(1)}, bf16[2,3,256,128]{3,2,1,0:T(8,128)(2,1)S(1)}, bf16[2,3,256,128]{3,2,1,0:T(8,128)(2,1)S(1)}) custom-call(s32[6,4,8]{2,1,0:T(4,128)} %bitcast.1, bf16[6,256,128]{2,1,0:T(8,128)(2,1)} %k_ref.7, bf16[6,256,128]{2,1,0:T(8,128)(2,1)} %v_ref.7), custom_call_target="tpu_custom_call" | custom-call | tf_op jit(solution)/shard_map/pack_keys/pallas_call | solution.py:297
  3.6 0.5 %collective-permute-start = (bf16[2,3,256,128]{3,2,1,0:T(8,128)(2,1)S(1)}, bf16[2,3,256,128]{3,2,1,0:T(8,128)(2,1)S(1)}, u32[]{:S(2)}, u32[]{:S(2)}) collective-permute-start(bf16[2,3,256,128]{3,2,1,0:T(8,128)(2,1)S(1)} %get-tuple-element.30), channel_id=1, source_target_pairs={{0,2},{2,0},{4,6},{6,4},{8,10},{10,8},{12,14},{14,12},{1,3},{3,1},... | collective-permute-start | bytes 1179656 | tf_op jit(solution)/shard_map/ppermute | solution.py:37
  4.2 4.5 %collective-permute-start.1 = (bf16[2,3,256,128]{3,2,1,0:T(8,128)(2,1)S(1)}, bf16[2,3,256,128]{3,2,1,0:T(8,128)(2,1)S(1)}, u32[]{:S(2)}, u32[]{:S(2)}) collective-permute-start(bf16[2,3,256,128]{3,2,1,0:T(8,128)(2,1)S(1)} %get-tuple-element.31), channel_id=1, source_target_pairs={{2,4},{4,2},{6,8},{8,6},{10,12},{12,10},{3,5},{5,3},{7,9},{9,7},{1... | collective-permute-start | bytes 1179656 | tf_op jit(solution)/shard_map/ppermute | solution.py:37
  8.6 0.0 copy-start
  8.7 0.0 copy-start.1
  8.7 4.5 %own_scores.1 = (f32[6,256,256]{2,1,0:T(8,128)S(1)}, f32[6,256,256]{2,1,0:T(8,128)S(1)}, f32[6,3,256]{2,1,0:T(4,128)S(1)}, bf16[2,3,256,128]{3,2,1,0:T(8,128)(2,1)S(1)}, bf16[2,3,256,128]{3,2,1,0:T(8,128)(2,1)S(1)}) custom-call(s32[24]{0:T(128)S(1)} %get-tuple-element.26.table_ref, bf16[6,256,128]{2,1,0:T(8,128)(2,1)} %q_ref.5, bf16[6,256,128]{2,1,0:T(8,128)(2,1)} %k_ref.7, ...), custom_call_target="tpu_custom_call" | custom-call | tf_op jit(solution)/shard_map/own_scores/pallas_call | solution.py:309
  13.2 0.1 collective-permute-start.2
  13.3 4.6 %collective-permute-start.4 = (bf16[2,3,256,128]{3,2,1,0:T(8,128)(2,1)S(1)}, bf16[2,3,256,128]{3,2,1,0:T(8,128)(2,1)S(1)}, u32[]{:S(2)}, u32[]{:S(2)}) collective-permute-start(bf16[2,3,256,128]{3,2,1,0:T(8,128)(2,1)S(1)} %get-tuple-element.44), channel_id=1, source_target_pairs={{2,4},{4,2},{6,8},{8,6},{10,12},{12,10},{3,5},{5,3},{7,9},{9,7},{1... | collective-permute-start | bytes 1179656 | tf_op jit(solution)/shard_map/ppermute | solution.py:37
  17.9 14.6 %collective-permute-done.rest_0_.rest_6_ = bf16[2,3,256,128]{3,2,1,0:T(8,128)(2,1)S(1)} collective-permute-done((bf16[2,3,256,128]{3,2,1,0:T(8,128)(2,1)S(1)}, bf16[2,3,256,128]{3,2,1,0:T(8,128)(2,1)S(1)}, u32[]{:S(2)}, u32[]{:S(2)}) %collective-permute-start) | collective-permute-done | bytes 393248 | tf_op jit(solution)/shard_map/ppermute | solution.py:37
  32.5 0.0 collective-permute-done.1.rest_1_.rest_7_
  32.5 0.0 copy-done.2
  32.6 0.0 copy-done.3
  32.6 1.4 %statistics.1 = (f32[6,256,256]{2,1,0:T(8,128)S(1)}, f32[6,256,256]{2,1,0:T(8,128)S(1)}, f32[6,2,256]{2,1,0:T(2,128)S(1)}, f32[6,2,256]{2,1,0:T(2,128)S(1)}, f32...) custom-call(s32[24]{0:T(128)S(1)} %get-tuple-element.26.table_ref, bf16[6,256,128]{2,1,0:T(8,128)(2,1)S(1)} %copy-done.2, ...), custom_call_target="tpu_custom_call" | custom-call | tf_op jit(solution)/shard_map/statistics/pallas_call | solution.py:322
  34.0 0.5 %collective-permute-start.3 = (f32[3,2,256]{2,1,0:T(2,128)S(1)}, f32[3,2,256]{2,1,0:T(2,128)S(1)}, u32[]{:S(2)}, u32[]{:S(2)}) collective-permute-start(f32[3,2,256]{2,1,0:T(2,128)S(1)} %get-tuple-element.41), channel_id=1, source_target_pairs={{0,2},{2,0},{4,6},{6,4},{8,10},{10,8},{12,14},{14,12},{1,3},{3,1},... | collective-permute-start | bytes 18440 | tf_op jit(solution)/shard_map/ppermute | solution.py:37
  34.5 4.5 %collective-permute-start.5 = (f32[3,2,256]{2,1,0:T(2,128)S(1)}, f32[3,2,256]{2,1,0:T(2,128)S(1)}, u32[]{:S(2)}, u32[]{:S(2)}) collective-permute-start(f32[3,2,256]{2,1,0:T(2,128)S(1)} %get-tuple-element.45), channel_id=1, source_target_pairs={{2,4},{4,2},{6,8},{8,6},{10,12},{12,10},{3,5},{5,3},{7,9},{9,7},{1... | collective-permute-start | bytes 18440 | tf_op jit(solution)/shard_map/ppermute | solution.py:37
  39.0 3.3 %reader.1 = (bf16[6,256,128]{2,1,0:T(8,128)(2,1)}, bf16[6,256,128]{2,1,0:T(8,128)(2,1)}, f32[6,256,128]{2,1,0:T(8,128)S(1)}, f32[6,256,128]{2,1,0:T(8,128)S(1)}) custom-call(s32[24]{0:T(128)S(1)} %get-tuple-element.26.table_ref, bf16[6,256,128]{2,1,0:T(8,128)(2,1)S(1)} %copy-done.2, bf16[6,256,128]{2,1,0:T(8,128)(2,1)S(1)} %copy-done, ...), custom_call_target="tpu_custom_call" | custom-call | tf_op jit(solution)/shard_map/reader/pallas_call | solution.py:336
  42.3 0.0 collective-permute-done.2.rest_0_
  42.3 0.0 collective-permute-done.3.rest_1_
  42.3 1.5 %owner.2 = (f32[6,256,128]{2,1,0:T(8,128)S(1)}, f32[6,256,128]{2,1,0:T(8,128)S(1)}) custom-call(s32[24]{0:T(128)S(1)} %get-tuple-element.26.table_ref, bf16[6,256,128]{2,1,0:T(8,128)(2,1)S(1)} %copy-done, bf16[6,256,128]{2,1,0:T(8,128)(2,1)S(1)} %copy-done.1, f32[6,256,128]{2,1,0:T(8,128)S(1)} %get-tuple-element.38.dk_in, ...), custom_call_target="tpu_custom_call" | custom-call | tf_op jit(solution)/shard_map/owner/pallas_call | solution.py:360
  43.8 0.0 collective-permute-done.4.rest_0_
  43.8 0.0 collective-permute-done.5.rest_1_
  43.8 2.3 %owner.3 = (bf16[6,256,128]{2,1,0:T(8,128)(2,1)}, bf16[6,256,128]{2,1,0:T(8,128)(2,1)}) custom-call(s32[24]{0:T(128)S(1)} %get-tuple-element.26.table_ref, bf16[6,256,128]{2,1,0:T(8,128)(2,1)S(1)} %copy-done, bf16[6,256,128]{2,1,0:T(8,128)(2,1)S(1)} %copy-done.1, f32[6,256,128]{2,1,0:T(8,128)S(1)} %get-tuple-element.42.dk_in, ...), custom_call_target="tpu_custom_call" | custom-call | tf_op jit(solution)/shard_map/owner/pallas_call | solution.py:360
  (2 shorter events, 0.0 us)
Async XLA Ops:
  0.6 31.9 %copy-start.2 = (bf16[6,256,128]{2,1,0:T(8,128)(2,1)S(1)}, bf16[6,256,128]{2,1,0:T(8,128)(2,1)}, u32[]{:S(2)}) copy-start(bf16[6,256,128]{2,1,0:T(8,128)(2,1)} %q_ref.5) | copy-start | bytes 1179652
  0.6 31.9 %copy-start.3 = (bf16[6,256,128]{2,1,0:T(8,128)(2,1)S(1)}, bf16[6,256,128]{2,1,0:T(8,128)(2,1)}, u32[]{:S(2)}) copy-start(bf16[6,256,128]{2,1,0:T(8,128)(2,1)} %g_ref.5) | copy-start | bytes 1179652
  3.6 28.9 %collective-permute-start = (bf16[2,3,256,128]{3,2,1,0:T(8,128)(2,1)S(1)}, bf16[2,3,256,128]{3,2,1,0:T(8,128)(2,1)S(1)}, u32[]{:S(2)}, u32[]{:S(2)}) collective-permute-start(bf16[2,3,256,128]{3,2,1,0:T(8,128)(2,1)S(1)} %get-tuple-element.30), channel_id=1, source_target_pairs={{0,2},{2,0},{4,6},{6,4},{8,10},{10,8},{12,14},{14,12},{1,3},{3,1},... | collective-permute-start | bytes 1179656 | tf_op jit(solution)/shard_map/ppermute | solution.py:37
  4.2 28.4 %collective-permute-start.1 = (bf16[2,3,256,128]{3,2,1,0:T(8,128)(2,1)S(1)}, bf16[2,3,256,128]{3,2,1,0:T(8,128)(2,1)S(1)}, u32[]{:S(2)}, u32[]{:S(2)}) collective-permute-start(bf16[2,3,256,128]{3,2,1,0:T(8,128)(2,1)S(1)} %get-tuple-element.31), channel_id=1, source_target_pairs={{2,4},{4,2},{6,8},{8,6},{10,12},{12,10},{3,5},{5,3},{7,9},{9,7},{1... | collective-permute-start | bytes 1179656 | tf_op jit(solution)/shard_map/ppermute | solution.py:37
  8.6 30.4 %copy-start = (bf16[6,256,128]{2,1,0:T(8,128)(2,1)S(1)}, bf16[6,256,128]{2,1,0:T(8,128)(2,1)}, u32[]{:S(2)}) copy-start(bf16[6,256,128]{2,1,0:T(8,128)(2,1)} %k_ref.7) | copy-start | bytes 1179652
  8.7 30.4 %copy-start.1 = (bf16[6,256,128]{2,1,0:T(8,128)(2,1)S(1)}, bf16[6,256,128]{2,1,0:T(8,128)(2,1)}, u32[]{:S(2)}) copy-start(bf16[6,256,128]{2,1,0:T(8,128)(2,1)} %v_ref.7) | copy-start | bytes 1179652
  13.2 29.1 %collective-permute-start.2 = (bf16[2,3,256,128]{3,2,1,0:T(8,128)(2,1)S(1)}, bf16[2,3,256,128]{3,2,1,0:T(8,128)(2,1)S(1)}, u32[]{:S(2)}, u32[]{:S(2)}) collective-permute-start(bf16[2,3,256,128]{3,2,1,0:T(8,128)(2,1)S(1)} %get-tuple-element.40), channel_id=1, source_target_pairs={{0,2},{2,0},{4,6},{6,4},{8,10},{10,8},{12,14},{14,12},{1,3},{3,1},... | collective-permute-start | bytes 1179656 | tf_op jit(solution)/shard_map/ppermute | solution.py:37
  13.3 30.5 %collective-permute-start.4 = (bf16[2,3,256,128]{3,2,1,0:T(8,128)(2,1)S(1)}, bf16[2,3,256,128]{3,2,1,0:T(8,128)(2,1)S(1)}, u32[]{:S(2)}, u32[]{:S(2)}) collective-permute-start(bf16[2,3,256,128]{3,2,1,0:T(8,128)(2,1)S(1)} %get-tuple-element.44), channel_id=1, source_target_pairs={{2,4},{4,2},{6,8},{8,6},{10,12},{12,10},{3,5},{5,3},{7,9},{9,7},{1... | collective-permute-start | bytes 1179656 | tf_op jit(solution)/shard_map/ppermute | solution.py:37
  34.0 8.3 %collective-permute-start.3 = (f32[3,2,256]{2,1,0:T(2,128)S(1)}, f32[3,2,256]{2,1,0:T(2,128)S(1)}, u32[]{:S(2)}, u32[]{:S(2)}) collective-permute-start(f32[3,2,256]{2,1,0:T(2,128)S(1)} %get-tuple-element.41), channel_id=1, source_target_pairs={{0,2},{2,0},{4,6},{6,4},{8,10},{10,8},{12,14},{14,12},{1,3},{3,1},... | collective-permute-start | bytes 18440 | tf_op jit(solution)/shard_map/ppermute | solution.py:37
  34.5 9.3 %collective-permute-start.5 = (f32[3,2,256]{2,1,0:T(2,128)S(1)}, f32[3,2,256]{2,1,0:T(2,128)S(1)}, u32[]{:S(2)}, u32[]{:S(2)}) collective-permute-start(f32[3,2,256]{2,1,0:T(2,128)S(1)} %get-tuple-element.45), channel_id=1, source_target_pairs={{2,4},{4,2},{6,8},{8,6},{10,12},{12,10},{3,5},{5,3},{7,9},{9,7},{1... | collective-permute-start | bytes 18440 | tf_op jit(solution)/shard_map/ppermute | solution.py:37

commit v3 on v2

--- a/solution.py
+++ b/solution.py
@@ -72,13 +72,62 @@
         return self.owner_at(self.count - 1, self.cap - 1) + 1
 
 
-def pack_keys_kernel(channels, cap, lists, keys, values, table_ref, *rest):
-    *targets, sems = rest
-    heads, entries, tile_count = lists.shape
-    count = len(channels)
-    table = Table(table_ref, heads, count, cap)
+def names(lists, head, reader, tile):
+    entries = range(1, lists.shape[1])
+    return functools.reduce(jnp.logical_or, [lists[head, entry, reader] == tile for entry in entries])
+
+
+def pack_keys_kernel(cap, channel, lists_hbm, keys, values, target, lists, held, sems):
+    heads, _, tile_count = lists.shape
+    loads = [pltpu.make_async_copy(lists_hbm, lists, sems.at[2, 0])]
+    for part, source in enumerate((keys, values)):
+        for head in range(heads):
+            loads.append(
+                pltpu.make_async_copy(source.at[head], held.at[part, head], sems.at[part, head])
+            )
+    for load in loads:
+        load.start()
+    loads[0].wait()
     own_tile = lax.axis_index("seq")
-    started = []
+    partner = partner_of(own_tile, channel)
+    inside = (partner >= 0) & (partner < tile_count)
+    reader = jnp.clip(partner, 0, tile_count - 1)
+    filled = jnp.int32(0)
+    chosen = [jnp.int32(0)] * cap
+    for head in range(heads):
+        wanted = names(lists, head, reader, own_tile) & inside
+        for slot in range(cap):
+            chosen[slot] = jnp.where(wanted & (filled == slot), head, chosen[slot])
+        filled = filled + wanted.astype(jnp.int32)
+    for load in loads[1:]:
+        load.wait()
+    for slot in range(cap):
+        for part in range(2):
+            target[part, slot] = held[part, chosen[slot]]
+
+
+def pack_more_keys_kernel(count, cap, number, table_ref, keys, values, target, sems):
+    table = Table(table_ref, keys.shape[0], count, cap)
+    for stage in ("start", "wait"):
+        for slot in range(cap):
+            head = table_ref[table.owner_at(number, slot)]
+
+            @pl.when(head >= 0)
+            def _():
+                for part, source in enumerate((keys, values)):
+                    copy = pltpu.make_async_copy(
+                        source.at[head], target.at[part, slot], sems.at[part, slot]
+                    )
+                    if stage == "start":
+                        copy.start()
+                    else:
+                        copy.wait()
+
+
+def table_kernel(channels, cap, lists, table_ref):
+    heads, _, tile_count = lists.shape
+    table = Table(table_ref, heads, len(channels), cap)
+    own_tile = lax.axis_index("seq")
     for number, channel in enumerate(channels):
         partner = partner_of(own_tile, channel)
         inside = (partner >= 0) & (partner < tile_count)
@@ -86,47 +135,21 @@
         for slot in range(cap):
             table_ref[table.owner_at(number, slot)] = -1
             table_ref[table.reader_at(number, slot)] = -1
-        slot = jnp.int32(0)
+        filled = [jnp.int32(0), jnp.int32(0)]
         for head in range(heads):
-            wanted = lists[head, 1, reader] == own_tile
-            for entry in range(2, entries):
-                wanted = wanted | (lists[head, entry, reader] == own_tile)
-            wanted = wanted & inside & (slot < cap)
-
-            @pl.when(wanted)
+            given = names(lists, head, reader, own_tile) & inside & (filled[0] < cap)
+            named = names(lists, head, own_tile, partner) & inside & (filled[1] < cap)
+            table_ref[table.slot_at(head, number)] = jnp.where(named, filled[1], -1)
+
+            @pl.when(given)
             def _():
-                table_ref[table.owner_at(number, slot)] = head
-                for part, source in enumerate((keys, values)):
-                    pltpu.make_async_copy(
-                        source.at[head], targets[number].at[part, slot], sems.at[number, part, slot]
-                    ).start()
-
-            slot = slot + wanted.astype(jnp.int32)
-        started.append(slot)
-    for number, channel in enumerate(channels):
-        partner = partner_of(own_tile, channel)
-        slot = jnp.int32(0)
-        for head in range(heads):
-            named = lists[head, 1, own_tile] == partner
-            for entry in range(2, entries):
-                named = named | (lists[head, entry, own_tile] == partner)
-            named = named & (partner >= 0) & (partner < tile_count) & (slot < cap)
-            table_ref[table.slot_at(head, number)] = jnp.where(named, slot, -1)
+                table_ref[table.owner_at(number, filled[0])] = head
 
             @pl.when(named)
             def _():
-                table_ref[table.reader_at(number, slot)] = head
-
-            slot = slot + named.astype(jnp.int32)
-    for number in range(count):
-        for slot in range(cap):
-
-            @pl.when(slot < started[number])
-            def _():
-                for part, source in enumerate((keys, values)):
-                    pltpu.make_async_copy(
-                        source.at[0], targets[number].at[part, slot], sems.at[number, part, slot]
-                    ).wait()
+                table_ref[table.reader_at(number, filled[1])] = head
+
+            filled = [filled[0] + given.astype(jnp.int32), filled[1] + named.astype(jnp.int32)]
 
 
 def own_kernel(count, cap, scale, table_ref, q_ref, k_ref, v_ref, g_ref, queries, grads, *rest):
@@ -248,28 +271,56 @@
         dq_ref[head] = (dq_sum[head] * scale).T.astype(jnp.bfloat16)
 
 
+def owner_terms(table, number, scale, k_ref, v_ref, arrived, stats, slot):
+    found = table.ref[table.owner_at(number, slot)]
+    head = jnp.maximum(found, 0)
+    query, grad = arrived[0, slot], arrived[1, slot]
+    score = dot_nt(k_ref[head], query) * (scale * LOG2E)
+    prob = jnp.exp2(score - stats[slot, 0:1])
+    prob_grad = dot_nt(v_ref[head], grad)
+    score_grad = (prob * (prob_grad - stats[slot, 1:2])).astype(jnp.bfloat16)
+    dk_term = dot_nn(score_grad, query) * scale
+    dv_term = dot_nn(prob.astype(jnp.bfloat16), grad)
+    return found, head, jnp.where(found >= 0, dk_term, 0.0), jnp.where(found >= 0, dv_term, 0.0)
+
+
 def owner_kernel(count, cap, scale, number, table_ref, k_ref, v_ref, dk_in, dv_in, *rest):
-    arrived, stats, dk_ref, dv_ref, dk_sum, dv_sum = rest
+    arrived, stats, dk_sum, dv_sum, *rounded = rest
     heads = k_ref.shape[0]
     table = Table(table_ref, heads, count, cap)
     for head in range(heads):
         dk_sum[head] = dk_in[head]
         dv_sum[head] = dv_in[head]
     for slot in range(cap):
-        found = table_ref[table.owner_at(number, slot)]
-        head = jnp.maximum(found, 0)
-        query, grad = arrived[0, slot], arrived[1, slot]
-        score = dot_nt(k_ref[head], query) * (scale * LOG2E)
-        prob = jnp.exp2(score - stats[slot, 0:1])
-        prob_grad = dot_nt(v_ref[head], grad)
-        score_grad = (prob * (prob_grad - stats[slot, 1:2])).astype(jnp.bfloat16)
-        dk_term = dot_nn(score_grad, query) * scale
-        dv_term = dot_nn(prob.astype(jnp.bfloat16), grad)
-        dk_sum[head] += jnp.where(found >= 0, dk_term, 0.0)
-        dv_sum[head] += jnp.where(found >= 0, dv_term, 0.0)
-    for head in range(heads):
-        dk_ref[head] = dk_sum[head].astype(dk_ref.dtype)
-        dv_ref[head] = dv_sum[head].astype(dv_ref.dtype)
+        _, head, dk_term, dv_term = owner_terms(
+            table, number, scale, k_ref, v_ref, arrived, stats, slot
+        )
+        dk_sum[head] += dk_term
+        dv_sum[head] += dv_term
+    for head in range(heads if rounded else 0):
+        rounded[0][head] = dk_sum[head].astype(jnp.bfloat16)
+        rounded[1][head] = dv_sum[head].astype(jnp.bfloat16)
+
+
+def last_owner_kernel(count, cap, scale, table_ref, k_ref, v_ref, dk_in, dv_in, *rest):
+    arrived, stats, _, _, dk_out, dv_out, staged, sems = rest
+    table = Table(table_ref, k_ref.shape[0], count, cap)
+    copies = []
+    for slot in range(cap):
+        found, head, dk_term, dv_term = owner_terms(
+            table, 0, scale, k_ref, v_ref, arrived, stats, slot
+        )
+        staged[0, slot] = (dk_in[head] + dk_term).astype(jnp.bfloat16)
+        staged[1, slot] = (dv_in[head] + dv_term).astype(jnp.bfloat16)
+        for part, result in enumerate((dk_out, dv_out)):
+            copy = pltpu.make_async_copy(
+                staged.at[part, slot], result.at[head], sems.at[part, slot]
+            )
+            copies.append((found, copy))
+    for found, copy in copies:
+        pl.when(found >= 0)(copy.start)
+    for found, copy in copies:
+        pl.when(found >= 0)(copy.wait)
 
 
 def per_device(queries, keys, values, out_grad, tile_lists):
@@ -283,6 +334,7 @@
     anywhere = pl.BlockSpec(memory_space=pl.ANY)
     vmem = pl.BlockSpec(memory_space=pltpu.VMEM)
     params = pltpu.CompilerParams(vmem_limit_bytes=VMEM_LIMIT)
+    brief = pl.CostEstimate(flops=1, bytes_accessed=1, transcendentals=0)
     packed = pltpu.VMEM((2, cap, tokens, width), jnp.bfloat16)
     whole = jax.ShapeDtypeStruct((heads, tokens, width), jnp.bfloat16)
     whole_sum = pltpu.VMEM((heads, tokens, width), jnp.float32)
@@ -294,16 +346,40 @@
         pltpu.with_memory_space_constraint(array, pltpu.HBM)
         for array in (jnp.swapaxes(tile_lists, 1, 2), queries, keys, values, out_grad)
     )
-    table, *key_value = pl.pallas_call(
-        functools.partial(pack_keys_kernel, channels, cap),
-        out_shape=[jax.ShapeDtypeStruct((table_size,), jnp.int32)] + [packed] * count,
-        in_specs=[smem, anywhere, anywhere],
-        out_specs=[smem] + [vmem] * count,
-        scratch_shapes=[copies],
+    table = pl.pallas_call(
+        functools.partial(table_kernel, channels, cap),
+        out_shape=jax.ShapeDtypeStruct((table_size,), jnp.int32),
+        in_specs=[smem],
+        out_specs=smem,
         compiler_params=params,
-        name="pack_keys",
-    )(lists, k_far, v_far)
-    fetched = [swapped(block, channel) for block, channel in zip(key_value, channels)]
+        cost_estimate=brief,
+        name="table",
+    )(lists)
+    fetched = []
+    for number, channel in enumerate(channels):
+        first = number == 0
+        pack = (
+            functools.partial(pack_keys_kernel, cap, channel)
+            if first
+            else functools.partial(pack_more_keys_kernel, count, cap, number)
+        )
+        key_value = pl.pallas_call(
+            pack,
+            out_shape=packed,
+            in_specs=[anywhere if first else smem, anywhere, anywhere],
+            out_specs=vmem,
+            scratch_shapes=[
+                pltpu.SMEM(lists.shape, jnp.int32),
+                pltpu.VMEM((2, heads, tokens, width), jnp.bfloat16),
+                pltpu.SemaphoreType.DMA((3, heads)),
+            ]
+            if first
+            else [pltpu.SemaphoreType.DMA((2, cap))],
+            compiler_params=params,
+            cost_estimate=brief,
+            name="pack_keys",
+        )(lists if first else table, k_far, v_far)
+        fetched.append(swapped(key_value, channel))
     one_head = pl.BlockSpec((1, tokens, width), lambda head: (head, 0, 0))
     one_square = pl.BlockSpec((1, tokens, tokens), lambda head: (head, 0, 0))
     own_weight, own_prob_grad, own_rows, *query_grads = pl.pallas_call(
@@ -316,8 +392,10 @@
         + [pl.BlockSpec(memory_space=pltpu.VMEM)] * count,
         scratch_shapes=[copies],
         compiler_params=params,
+        cost_estimate=brief,
         name="own_scores",
     )(table, q_far, k_far, v_far, g_far, q_far, g_far)
+    query_grads[1:], fetched[0] = lax.optimization_barrier((query_grads[1:], fetched[0]))
     arrived = [swapped(block, channel) for block, channel in zip(query_grads, channels)]
     far_weight, far_prob_grad, own_factors, far_factors, *stats = pl.pallas_call(
         functools.partial(statistics_kernel, count, cap, scale),
@@ -329,6 +407,7 @@
         out_specs=[vmem] * (4 + count),
         scratch_shapes=[pltpu.VMEM((count * cap, 3, tokens), jnp.float32)],
         compiler_params=params,
+        cost_estimate=brief,
         name="statistics",
     )(table, queries, out_grad, own_rows, *fetched)
     stats = [swapped(block, channel) for block, channel in zip(stats, channels)]
@@ -340,6 +419,7 @@
         out_specs=[vmem] * 4,
         scratch_shapes=[transposed_sums] * 2,
         compiler_params=params,
+        cost_estimate=pl.CostEstimate(flops=100000000000, bytes_accessed=1, transcendentals=0),
         name="reader",
     )(
         table,
@@ -355,18 +435,35 @@
         far_factors,
         *fetched,
     )
-    for number in range(count):
-        last = number == count - 1
-        key_sum, value_sum = pl.pallas_call(
+    sums = [key_sum, value_sum]
+    for number in range(count - 1, 0, -1):
+        closing = number == 1
+        sums = pl.pallas_call(
             functools.partial(owner_kernel, count, cap, scale, number),
-            out_shape=[whole if last else whole_sum] * 2,
+            out_shape=[whole_sum] * 2 + [whole] * (2 if closing else 0),
             in_specs=[smem] + [vmem] * 6,
-            out_specs=[vmem] * 2,
-            scratch_shapes=[whole_sum] * 2,
+            out_specs=[vmem] * (4 if closing else 2),
             compiler_params=params,
+            cost_estimate=brief,
             name="owner",
-        )(table, keys, values, key_sum, value_sum, arrived[number], stats[number])
-    return attn_out, query_grad, key_sum, value_sum
+        )(table, keys, values, *sums[:2], arrived[number], stats[number])
+    key_sum, value_sum, *rounded = sums
+    last, key_sum = lax.optimization_barrier((arrived[0], key_sum))
+    key_grad, value_grad = pl.pallas_call(
+        functools.partial(last_owner_kernel, count, cap, scale),
+        out_shape=[whole] * 2,
+        in_specs=[smem] + [vmem] * 6 + [anywhere] * 2,
+        out_specs=[anywhere] * 2,
+        scratch_shapes=[
+            pltpu.VMEM((2, cap, tokens, width), jnp.bfloat16),
+            pltpu.SemaphoreType.DMA((2, cap)),
+        ],
+        input_output_aliases={7: 0, 8: 1},
+        compiler_params=params,
+        cost_estimate=brief,
+        name="last_owner",
+    )(table, keys, values, key_sum, value_sum, last, stats[0], *rounded)
+    return attn_out, query_grad, key_grad, value_grad
 
 
 def solution(mesh):

time: 46.9 us -> 41.8 us (0.89)
  the two profiles are of different devices: /device:TPU:14 before, /device:TPU:0 now
where the time goes in v3:
time: 41.8 us; the launch traced here: 41.4 us
  starting transfers between devices  18.4 us (44%)
  Pallas kernels  17.2 us (41%)
  waiting for transfers between devices  5.05 us (12%)
  between operations  0.75 us (2%)
    ppermute x6, starting transfers between devices, swapped(): return lax.ppermute(block, 'seq', swap_route(channel, lax.axis_size('seq')))  18.4 us
    ppermute x6, waiting for transfers between devices, swapped(): return lax.ppermute(block, 'seq', swap_route(channel, lax.axis_size('seq')))  5.05 us
    pallas_call x1, Pallas kernels, per_device(): pl.pallas_call(functools.partial(own_kernel, count, cap, scale), grid=(he...  4.45 us
    pallas_call x1, Pallas kernels, per_device(): pl.pallas_call(functools.partial(reader_kernel, count, cap, scale), out_s...  3.25 us
    pallas_call x1, Pallas kernels, per_device(): pl.pallas_call(functools.partial(owner_kernel, count, cap, scale, number)...  2.3 us
    pallas_call x1, Pallas kernels, per_device(): pl.pallas_call(functools.partial(last_owner_kernel, count, cap, scale), o...  2.15 us
    pallas_call x2, Pallas kernels, per_device(): pl.pallas_call(pack, out_shape=packed, in_specs=[anywhere if first else s...  1.96 us
    pallas_call x1, Pallas kernels, per_device(): pl.pallas_call(functools.partial(table_kernel, channels, cap), out_shape=...  1.62 us
  transfers between devices with their start and end apart: 6, of which 1 were waited for; matrix products, arithmetic and copies ran while one was open for 0% of the time, Pallas kernels for 33%

profile of v3, /device:TPU:0, one launch (start us, length us, event | category | flops | bytes accessed | tf_op | source)
XLA Modules:
  0.0 41.4 jit_solution(6406182836499704427)
XLA Ops:
  0.6 1.3 %pack_keys.2 = bf16[2,3,256,128]{3,2,1,0:T(8,128)(2,1)S(1)} custom-call(s32[6,4,8]{2,1,0:T(4,128)} %bitcast.1, bf16[6,256,128]{2,1,0:T(8,128)(2,1)} %k_ref.7, bf16[6,256,128]{2,1,0:T(8,128)(2,1)} %v_ref.7), custom_call_target="tpu_custom_call" | custom-call | flops 1 | bytes 1 | tf_op jit(solution)/shard_map/pack_keys/pallas_call | solution.py:366
  2.0 3.0 %collective-permute-start = (bf16[2,3,256,128]{3,2,1,0:T(8,128)(2,1)S(1)}, bf16[2,3,256,128]{3,2,1,0:T(8,128)(2,1)S(1)}, u32[]{:S(2)}, u32[]{:S(2)}) collective-permute-start(bf16[2,3,256,128]{3,2,1,0:T(8,128)(2,1)S(1)} %pack_keys.2), channel_id=1, source_target_pairs={{0,2},{2,0},{4,6},{6,4},{8,10},{10,8},{12,14},{14,12},{1,3},{3,1},... | collective-permute-start | bytes 1179656 | tf_op jit(solution)/shard_map/ppermute | solution.py:37
  5.0 1.6 %table.1.table_ref = s32[24]{0:T(128)S(1)} custom-call(s32[6,4,8]{2,1,0:T(4,128)} %bitcast.2), custom_call_target="tpu_custom_call" | custom-call | flops 1 | bytes 1 | tf_op jit(solution)/shard_map/table/pallas_call | solution.py:349
  6.6 0.0 copy-start.2
  6.6 0.0 copy-start.3
  6.6 0.6 %pack_keys.3 = bf16[2,3,256,128]{3,2,1,0:T(8,128)(2,1)S(1)} custom-call(s32[24]{0:T(128)S(1)} %table.1.table_ref, bf16[6,256,128]{2,1,0:T(8,128)(2,1)} %k_ref.7, bf16[6,256,128]{2,1,0:T(8,128)(2,1)} %v_ref.7), custom_call_target="tpu_custom_call" | custom-call | flops 1 | bytes 1 | tf_op jit(solution)/shard_map/pack_keys/pallas_call | solution.py:366
  7.3 0.0 copy-start
  7.3 0.0 copy-start.1
  7.3 0.8 %collective-permute-start.1 = (bf16[2,3,256,128]{3,2,1,0:T(8,128)(2,1)S(1)}, bf16[2,3,256,128]{3,2,1,0:T(8,128)(2,1)S(1)}, u32[]{:S(2)}, u32[]{:S(2)}) collective-permute-start(bf16[2,3,256,128]{3,2,1,0:T(8,128)(2,1)S(1)} %pack_keys.3), channel_id=1, source_target_pairs={{2,4},{4,2},{6,8},{8,6},{10,12},{12,10},{3,5},{5,3},{7,9},{9,7},{1... | collective-permute-start | bytes 1179656 | tf_op jit(solution)/shard_map/ppermute | solution.py:37
  8.1 4.4 %own_scores.1 = (f32[6,256,256]{2,1,0:T(8,128)S(1)}, f32[6,256,256]{2,1,0:T(8,128)S(1)}, f32[6,3,256]{2,1,0:T(4,128)S(1)}, bf16[2,3,256,128]{3,2,1,0:T(8,128)(2,1)S(1)}, bf16[2,3,256,128]{3,2,1,0:T(8,128)(2,1)S(1)}) custom-call(s32[24]{0:T(128)S(1)} %table.1.table_ref, bf16[6,256,128]{2,1,0:T(8,128)(2,1)} %q_ref.5, bf16[6,256,128]{2,1,0:T(8,128)(2,1)} %k_ref.7, ...), custom_call_target="tpu_custom_call" | custom-call | flops 1 | bytes 1 | tf_op jit(solution)/shard_map/own_scores/pallas_call | solution.py:385
  12.6 5.3 %collective-permute-start.2 = (bf16[2,3,256,128]{3,2,1,0:T(8,128)(2,1)S(1)}, bf16[2,3,256,128]{3,2,1,0:T(8,128)(2,1)S(1)}, u32[]{:S(2)}, u32[]{:S(2)}) collective-permute-start(bf16[2,3,256,128]{3,2,1,0:T(8,128)(2,1)S(1)} %get-tuple-element.40), channel_id=1, source_target_pairs={{0,2},{2,0},{4,6},{6,4},{8,10},{10,8},{12,14},{14,12},{1,3},{3,1},... | collective-permute-start | bytes 1179656 | tf_op jit(solution)/shard_map/ppermute | solution.py:37
  17.9 5.0 %collective-permute-done.rest_0_.rest_6_ = bf16[2,3,256,128]{3,2,1,0:T(8,128)(2,1)S(1)} collective-permute-done((bf16[2,3,256,128]{3,2,1,0:T(8,128)(2,1)S(1)}, bf16[2,3,256,128]{3,2,1,0:T(8,128)(2,1)S(1)}, u32[]{:S(2)}, u32[]{:S(2)}) %collective-permute-start) | collective-permute-done | bytes 393248 | tf_op jit(solution)/shard_map/ppermute | solution.py:37
  22.9 0.7 %collective-permute-start.3 = (bf16[2,3,256,128]{3,2,1,0:T(8,128)(2,1)S(1)}, bf16[2,3,256,128]{3,2,1,0:T(8,128)(2,1)S(1)}, u32[]{:S(2)}, u32[]{:S(2)}) collective-permute-start(bf16[2,3,256,128]{3,2,1,0:T(8,128)(2,1)S(1)} %get-tuple-element.43), channel_id=1, source_target_pairs={{2,4},{4,2},{6,8},{8,6},{10,12},{12,10},{3,5},{5,3},{7,9},{9,7},{1... | collective-permute-start | bytes 1179656 | tf_op jit(solution)/shard_map/ppermute | solution.py:37
  23.6 0.0 collective-permute-done.1.rest_1_.rest_7_
  23.6 1.4 %statistics.1 = (f32[6,256,256]{2,1,0:T(8,128)S(1)}, f32[6,256,256]{2,1,0:T(8,128)S(1)}, f32[6,2,256]{2,1,0:T(2,128)S(1)}, f32[6,2,256]{2,1,0:T(2,128)S(1)}, f32...) custom-call(s32[24]{0:T(128)S(1)} %table.1.table_ref, bf16[6,256,128]{2,1,0:T(8,128)(2,1)S(1)} %copy-done.2, ...), custom_call_target="tpu_custom_call" | custom-call | flops 1 | bytes 1 | tf_op jit(solution)/shard_map/statistics/pallas_call | solution.py:400
  25.1 0.7 %collective-permute-start.4 = (f32[3,2,256]{2,1,0:T(2,128)S(1)}, f32[3,2,256]{2,1,0:T(2,128)S(1)}, u32[]{:S(2)}, u32[]{:S(2)}) collective-permute-start(f32[3,2,256]{2,1,0:T(2,128)S(1)} %get-tuple-element.44), channel_id=1, source_target_pairs={{2,4},{4,2},{6,8},{8,6},{10,12},{12,10},{3,5},{5,3},{7,9},{9,7},{1... | collective-permute-start | bytes 18440 | tf_op jit(solution)/shard_map/ppermute | solution.py:37
  25.8 7.9 %collective-permute-start.5 = (f32[3,2,256]{2,1,0:T(2,128)S(1)}, f32[3,2,256]{2,1,0:T(2,128)S(1)}, u32[]{:S(2)}, u32[]{:S(2)}) collective-permute-start(f32[3,2,256]{2,1,0:T(2,128)S(1)} %get-tuple-element.49), channel_id=1, source_target_pairs={{0,2},{2,0},{4,6},{6,4},{8,10},{10,8},{12,14},{14,12},{1,3},{3,1},... | collective-permute-start | bytes 18440 | tf_op jit(solution)/shard_map/ppermute | solution.py:37
  33.7 3.2 %reader.1 = (bf16[6,256,128]{2,1,0:T(8,128)(2,1)}, bf16[6,256,128]{2,1,0:T(8,128)(2,1)}, f32[6,256,128]{2,1,0:T(8,128)S(1)}, f32[6,256,128]{2,1,0:T(8,128)S(1)}) custom-call(s32[24]{0:T(128)S(1)} %table.1.table_ref, bf16[6,256,128]{2,1,0:T(8,128)(2,1)S(1)} %copy-done.2, bf16[6,256,128]{2,1,0:T(8,128)(2,1)S(1)} %copy-done, ...), custom_call_target="tpu_custom_call" | custom-call | flops 99999997952 | bytes 1 | tf_op jit(solution)/shard_map/reader/pallas_call | solution.py:415
  37.0 0.0 collective-permute-done.4.rest_1_
  37.0 0.0 collective-permute-done.3.rest_0_
  37.0 2.3 %owner.1 = (f32[6,256,128]{2,1,0:T(8,128)S(1)}, f32[6,256,128]{2,1,0:T(8,128)S(1)}, bf16[6,256,128]{2,1,0:T(8,128)(2,1)}, bf16[6,256,128]{2,1,0:T(8,128)(2,1)}) custom-call(s32[24]{0:T(128)S(1)} %table.1.table_ref, bf16[6,256,128]{2,1,0:T(8,128)(2,1)S(1)} %copy-done, bf16[6,256,128]{2,1,0:T(8,128)(2,1)S(1)} %copy-done.1, ...), custom_call_target="tpu_custom_call" | custom-call | flops 1 | bytes 1 | tf_op jit(solution)/shard_map/owner/pallas_call | solution.py:441
  39.3 0.0 collective-permute-done.2.rest_0_
  39.3 0.0 collective-permute-done.5.rest_1_
  39.3 2.1 %last_owner.1 = (bf16[6,256,128]{2,1,0:T(8,128)(2,1)}, bf16[6,256,128]{2,1,0:T(8,128)(2,1)}) custom-call(s32[24]{0:T(128)S(1)} %table.1.table_ref, bf16[6,256,128]{2,1,0:T(8,128)(2,1)S(1)} %copy-done, bf16[6,256,128]{2,1,0:T(8,128)(2,1)S(1)} %copy-done.1, f32[6,256,128]{2,1,0:T(8,128)S(1)} %get-tuple-element.46.dk_in, ...), custom_call_target="tpu_custom_call", output_to_operand_aliasing={{0}: (7, {}), {1}: (8, {})} | custom-call | flops 1 | bytes 1 | tf_op jit(solution)/shard_map/last_owner/pallas_call | solution.py:452
  (4 shorter events, 0.0 us)
Async XLA Ops:
  2.0 21.0 %collective-permute-start = (bf16[2,3,256,128]{3,2,1,0:T(8,128)(2,1)S(1)}, bf16[2,3,256,128]{3,2,1,0:T(8,128)(2,1)S(1)}, u32[]{:S(2)}, u32[]{:S(2)}) collective-permute-start(bf16[2,3,256,128]{3,2,1,0:T(8,128)(2,1)S(1)} %pack_keys.2), channel_id=1, source_target_pairs={{0,2},{2,0},{4,6},{6,4},{8,10},{10,8},{12,14},{14,12},{1,3},{3,1},... | collective-permute-start | bytes 1179656 | tf_op jit(solution)/shard_map/ppermute | solution.py:37
  6.6 17.0 %copy-start.2 = (bf16[6,256,128]{2,1,0:T(8,128)(2,1)S(1)}, bf16[6,256,128]{2,1,0:T(8,128)(2,1)}, u32[]{:S(2)}) copy-start(bf16[6,256,128]{2,1,0:T(8,128)(2,1)} %q_ref.5) | copy-start | bytes 1179652
  6.6 17.0 %copy-start.3 = (bf16[6,256,128]{2,1,0:T(8,128)(2,1)S(1)}, bf16[6,256,128]{2,1,0:T(8,128)(2,1)}, u32[]{:S(2)}) copy-start(bf16[6,256,128]{2,1,0:T(8,128)(2,1)} %g_ref.5) | copy-start | bytes 1179652
  7.3 26.4 %copy-start = (bf16[6,256,128]{2,1,0:T(8,128)(2,1)S(1)}, bf16[6,256,128]{2,1,0:T(8,128)(2,1)}, u32[]{:S(2)}) copy-start(bf16[6,256,128]{2,1,0:T(8,128)(2,1)} %k_ref.7) | copy-start | bytes 1179652
  7.3 26.4 %copy-start.1 = (bf16[6,256,128]{2,1,0:T(8,128)(2,1)S(1)}, bf16[6,256,128]{2,1,0:T(8,128)(2,1)}, u32[]{:S(2)}) copy-start(bf16[6,256,128]{2,1,0:T(8,128)(2,1)} %v_ref.7) | copy-start | bytes 1179652
  7.3 16.3 %collective-permute-start.1 = (bf16[2,3,256,128]{3,2,1,0:T(8,128)(2,1)S(1)}, bf16[2,3,256,128]{3,2,1,0:T(8,128)(2,1)S(1)}, u32[]{:S(2)}, u32[]{:S(2)}) collective-permute-start(bf16[2,3,256,128]{3,2,1,0:T(8,128)(2,1)S(1)} %pack_keys.3), channel_id=1, source_target_pairs={{2,4},{4,2},{6,8},{8,6},{10,12},{12,10},{3,5},{5,3},{7,9},{9,7},{1... | collective-permute-start | bytes 1179656 | tf_op jit(solution)/shard_map/ppermute | solution.py:37
  12.6 26.7 %collective-permute-start.2 = (bf16[2,3,256,128]{3,2,1,0:T(8,128)(2,1)S(1)}, bf16[2,3,256,128]{3,2,1,0:T(8,128)(2,1)S(1)}, u32[]{:S(2)}, u32[]{:S(2)}) collective-permute-start(bf16[2,3,256,128]{3,2,1,0:T(8,128)(2,1)S(1)} %get-tuple-element.40), channel_id=1, source_target_pairs={{0,2},{2,0},{4,6},{6,4},{8,10},{10,8},{12,14},{14,12},{1,3},{3,1},... | collective-permute-start | bytes 1179656 | tf_op jit(solution)/shard_map/ppermute | solution.py:37
  22.9 14.0 %collective-permute-start.3 = (bf16[2,3,256,128]{3,2,1,0:T(8,128)(2,1)S(1)}, bf16[2,3,256,128]{3,2,1,0:T(8,128)(2,1)S(1)}, u32[]{:S(2)}, u32[]{:S(2)}) collective-permute-start(bf16[2,3,256,128]{3,2,1,0:T(8,128)(2,1)S(1)} %get-tuple-element.43), channel_id=1, source_target_pairs={{2,4},{4,2},{6,8},{8,6},{10,12},{12,10},{3,5},{5,3},{7,9},{9,7},{1... | collective-permute-start | bytes 1179656 | tf_op jit(solution)/shard_map/ppermute | solution.py:37
  25.1 11.9 %collective-permute-start.4 = (f32[3,2,256]{2,1,0:T(2,128)S(1)}, f32[3,2,256]{2,1,0:T(2,128)S(1)}, u32[]{:S(2)}, u32[]{:S(2)}) collective-permute-start(f32[3,2,256]{2,1,0:T(2,128)S(1)} %get-tuple-element.44), channel_id=1, source_target_pairs={{2,4},{4,2},{6,8},{8,6},{10,12},{12,10},{3,5},{5,3},{7,9},{9,7},{1... | collective-permute-start | bytes 18440 | tf_op jit(solution)/shard_map/ppermute | solution.py:37
  25.8 13.5 %collective-permute-start.5 = (f32[3,2,256]{2,1,0:T(2,128)S(1)}, f32[3,2,256]{2,1,0:T(2,128)S(1)}, u32[]{:S(2)}, u32[]{:S(2)}) collective-permute-start(f32[3,2,256]{2,1,0:T(2,128)S(1)} %get-tuple-element.49), channel_id=1, source_target_pairs={{0,2},{2,0},{4,6},{6,4},{8,10},{10,8},{12,14},{14,12},{1,3},{3,1},... | collective-permute-start | bytes 18440 | tf_op jit(solution)/shard_map/ppermute | solution.py:37

commit v4 on v3

--- a/solution.py
+++ b/solution.py
@@ -284,28 +284,33 @@
     return found, head, jnp.where(found >= 0, dk_term, 0.0), jnp.where(found >= 0, dv_term, 0.0)
 
 
-def owner_kernel(count, cap, scale, number, table_ref, k_ref, v_ref, dk_in, dv_in, *rest):
-    arrived, stats, dk_sum, dv_sum, *rounded = rest
-    heads = k_ref.shape[0]
-    table = Table(table_ref, heads, count, cap)
-    for head in range(heads):
-        dk_sum[head] = dk_in[head]
-        dv_sum[head] = dv_in[head]
+def owner_kernel(count, cap, scale, number, table_ref, k_ref, v_ref, *rest):
+    arrived, stats, _, _, dk_sum, dv_sum = rest
+    table = Table(table_ref, k_ref.shape[0], count, cap)
     for slot in range(cap):
         _, head, dk_term, dv_term = owner_terms(
             table, number, scale, k_ref, v_ref, arrived, stats, slot
         )
         dk_sum[head] += dk_term
         dv_sum[head] += dv_term
-    for head in range(heads if rounded else 0):
-        rounded[0][head] = dk_sum[head].astype(jnp.bfloat16)
-        rounded[1][head] = dv_sum[head].astype(jnp.bfloat16)
-
-
-def last_owner_kernel(count, cap, scale, table_ref, k_ref, v_ref, dk_in, dv_in, *rest):
-    arrived, stats, _, _, dk_out, dv_out, staged, sems = rest
-    table = Table(table_ref, k_ref.shape[0], count, cap)
+
+
+def last_owner_kernel(count, cap, scale, table_ref, k_ref, v_ref, *rest):
+    arrived, stats, dk_in, dv_in, dk_out, dv_out, rounded, staged, sems, staged_sems = rest
+    heads = k_ref.shape[0]
+    table = Table(table_ref, heads, count, cap)
+    owners = [table_ref[table.owner_at(0, slot)] for slot in range(cap)]
     copies = []
+    for head in range(heads):
+        untouched = functools.reduce(jnp.logical_and, [owner != head for owner in owners])
+        for part, (total, result) in enumerate(((dk_in, dk_out), (dv_in, dv_out))):
+            rounded[part, head] = total[head].astype(jnp.bfloat16)
+            copy = pltpu.make_async_copy(
+                rounded.at[part, head], result.at[head], sems.at[part, head]
+            )
+            copies.append((untouched, copy))
+    for wanted, copy in copies:
+        pl.when(wanted)(copy.start)
     for slot in range(cap):
         found, head, dk_term, dv_term = owner_terms(
             table, 0, scale, k_ref, v_ref, arrived, stats, slot
@@ -314,13 +319,12 @@
         staged[1, slot] = (dv_in[head] + dv_term).astype(jnp.bfloat16)
         for part, result in enumerate((dk_out, dv_out)):
             copy = pltpu.make_async_copy(
-                staged.at[part, slot], result.at[head], sems.at[part, slot]
+                staged.at[part, slot], result.at[head], staged_sems.at[part, slot]
             )
-            copies.append((found, copy))
-    for found, copy in copies:
-        pl.when(found >= 0)(copy.start)
-    for found, copy in copies:
-        pl.when(found >= 0)(copy.wait)
+            copies.append((found >= 0, copy))
+            pl.when(found >= 0)(copy.start)
+    for wanted, copy in copies:
+        pl.when(wanted)(copy.wait)
 
 
 def per_device(queries, keys, values, out_grad, tile_lists):
@@ -346,40 +350,41 @@
         pltpu.with_memory_space_constraint(array, pltpu.HBM)
         for array in (jnp.swapaxes(tile_lists, 1, 2), queries, keys, values, out_grad)
     )
+    key_value, lists = pl.pallas_call(
+        functools.partial(pack_keys_kernel, cap, channels[0]),
+        out_shape=[packed, pltpu.SMEM(lists.shape, jnp.int32)],
+        in_specs=[anywhere] * 3,
+        out_specs=[vmem, smem],
+        scratch_shapes=[
+            pltpu.VMEM((2, heads, tokens, width), jnp.bfloat16),
+            pltpu.SemaphoreType.DMA((3, heads)),
+        ],
+        compiler_params=params,
+        cost_estimate=brief,
+        name="pack_keys",
+    )(lists, k_far, v_far)
+    fetched = [swapped(key_value, channels[0])]
     table = pl.pallas_call(
         functools.partial(table_kernel, channels, cap),
-        out_shape=jax.ShapeDtypeStruct((table_size,), jnp.int32),
+        out_shape=pltpu.SMEM((table_size,), jnp.int32),
         in_specs=[smem],
         out_specs=smem,
         compiler_params=params,
         cost_estimate=brief,
         name="table",
     )(lists)
-    fetched = []
-    for number, channel in enumerate(channels):
-        first = number == 0
-        pack = (
-            functools.partial(pack_keys_kernel, cap, channel)
-            if first
-            else functools.partial(pack_more_keys_kernel, count, cap, number)
-        )
+    for number in range(1, count):
         key_value = pl.pallas_call(
-            pack,
+            functools.partial(pack_more_keys_kernel, count, cap, number),
             out_shape=packed,
-            in_specs=[anywhere if first else smem, anywhere, anywhere],
+            in_specs=[smem, anywhere, anywhere],
             out_specs=vmem,
-            scratch_shapes=[
-                pltpu.SMEM(lists.shape, jnp.int32),
-                pltpu.VMEM((2, heads, tokens, width), jnp.bfloat16),
-                pltpu.SemaphoreType.DMA((3, heads)),
-            ]
-            if first
-            else [pltpu.SemaphoreType.DMA((2, cap))],
+            scratch_shapes=[pltpu.SemaphoreType.DMA((2, cap))],
             compiler_params=params,
             cost_estimate=brief,
-            name="pack_keys",
-        )(lists if first else table, k_far, v_far)
-        fetched.append(swapped(key_value, channel))
+            name="pack_more_keys",
+        )(table, k_far, v_far)
+        fetched.append(swapped(key_value, channels[number]))
     one_head = pl.BlockSpec((1, tokens, width), lambda head: (head, 0, 0))
     one_square = pl.BlockSpec((1, tokens, tokens), lambda head: (head, 0, 0))
     own_weight, own_prob_grad, own_rows, *query_grads = pl.pallas_call(
@@ -435,34 +440,33 @@
         far_factors,
         *fetched,
     )
-    sums = [key_sum, value_sum]
     for number in range(count - 1, 0, -1):
-        closing = number == 1
-        sums = pl.pallas_call(
+        key_sum, value_sum = pl.pallas_call(
             functools.partial(owner_kernel, count, cap, scale, number),
-            out_shape=[whole_sum] * 2 + [whole] * (2 if closing else 0),
+            out_shape=[whole_sum] * 2,
             in_specs=[smem] + [vmem] * 6,
-            out_specs=[vmem] * (4 if closing else 2),
+            out_specs=[vmem] * 2,
+            input_output_aliases={5: 0, 6: 1},
             compiler_params=params,
             cost_estimate=brief,
             name="owner",
-        )(table, keys, values, *sums[:2], arrived[number], stats[number])
-    key_sum, value_sum, *rounded = sums
+        )(table, keys, values, arrived[number], stats[number], key_sum, value_sum)
     last, key_sum = lax.optimization_barrier((arrived[0], key_sum))
     key_grad, value_grad = pl.pallas_call(
         functools.partial(last_owner_kernel, count, cap, scale),
         out_shape=[whole] * 2,
-        in_specs=[smem] + [vmem] * 6 + [anywhere] * 2,
+        in_specs=[smem] + [vmem] * 6,
         out_specs=[anywhere] * 2,
         scratch_shapes=[
+            pltpu.VMEM((2, heads, tokens, width), jnp.bfloat16),
             pltpu.VMEM((2, cap, tokens, width), jnp.bfloat16),
+            pltpu.SemaphoreType.DMA((2, heads)),
             pltpu.SemaphoreType.DMA((2, cap)),
         ],
-        input_output_aliases={7: 0, 8: 1},
         compiler_params=params,
         cost_estimate=brief,
         name="last_owner",
-    )(table, keys, values, key_sum, value_sum, last, stats[0], *rounded)
+    )(table, keys, values, last, stats[0], key_sum, value_sum)
     return attn_out, query_grad, key_grad, value_grad
 
 

time: 41.8 us -> 41 us (0.981)
  Pallas kernels: 17.2 us -> 11.9 us
  waiting for transfers between devices: 5.05 us -> 9.37 us
    ppermute x6, waiting for transfers between devices: 5.05 us -> 9.37 us  [swapped(): return lax.ppermute(block, 'seq', swap_route(channel, lax.axis_size('seq')))]
    pallas_call x1, Pallas kernels: 1.62 us -> 0.01 us  [per_device(): pl.pallas_call(functools.partial(table_kernel, channels, cap), out_shape=...]
    pallas_call x1, Pallas kernels: 2.3 us -> 0.81 us  [per_device(): pl.pallas_call(functools.partial(owner_kernel, count, cap, scale, number)...]
    pallas_call x2, Pallas kernels: 1.96 us -> 1.4 us  [the longest x1 1.34 us: per_device(): pl.pallas_call(functools.partial(pack_keys_kernel, cap, channels[0]), out...]
    pallas_call x1, Pallas kernels: 1.44 us -> 0.89 us  [per_device(): pl.pallas_call(functools.partial(statistics_kernel, count, cap, scale), o...]
    pallas_call x1, Pallas kernels: 3.25 us -> 2.73 us  [per_device(): pl.pallas_call(functools.partial(reader_kernel, count, cap, scale), out_s...]
    pallas_call x1, Pallas kernels: 2.15 us -> 1.65 us  [per_device(): pl.pallas_call(functools.partial(last_owner_kernel, count, cap, scale), o...]
  transfers between devices with their start and end apart: 6 -> 6, of which waited for: 1 -> 3; matrix products, arithmetic and copies ran while one was open for 0% -> 0% of each run, Pallas kernels for 33% -> 22%
where the time goes in v4:
time: 41 us; the launch traced here: 40.6 us
  starting transfers between devices  18.5 us (45%)
  Pallas kernels  11.9 us (29%)
  waiting for transfers between devices  9.37 us (23%)
  between operations  0.74 us (2%)
    ppermute x6, starting transfers between devices, swapped(): return lax.ppermute(block, 'seq', swap_route(channel, lax.axis_size('seq')))  18.5 us
    ppermute x6, waiting for transfers between devices, swapped(): return lax.ppermute(block, 'seq', swap_route(channel, lax.axis_size('seq')))  9.37 us
    pallas_call x1, Pallas kernels, per_device(): pl.pallas_call(functools.partial(own_kernel, count, cap, scale), grid=(he...  4.43 us
    pallas_call x1, Pallas kernels, per_device(): pl.pallas_call(functools.partial(reader_kernel, count, cap, scale), out_s...  2.73 us
    pallas_call x1, Pallas kernels, per_device(): pl.pallas_call(functools.partial(last_owner_kernel, count, cap, scale), o...  1.65 us
    pallas_call x1, Pallas kernels, per_device(): pl.pallas_call(functools.partial(pack_keys_kernel, cap, channels[0]), out...  1.34 us
    pallas_call x1, Pallas kernels, per_device(): pl.pallas_call(functools.partial(statistics_kernel, count, cap, scale), o...  0.89 us
  transfers between devices with their start and end apart: 6, of which 3 were waited for; matrix products, arithmetic and copies ran while one was open for 0% of the time, Pallas kernels for 22%

profile of v4, /device:TPU:0, one launch (start us, length us, event | category | flops | bytes accessed | tf_op | source)
XLA Modules:
  0.0 40.6 jit_solution(10695346508939918413)
XLA Ops:
  0.6 1.3 %pack_keys.1 = (bf16[2,3,256,128]{3,2,1,0:T(8,128)(2,1)S(1)}, s32[6,4,8]{2,1,0:T(4,128)S(4)}) custom-call(s32[6,4,8]{2,1,0:T(4,128)} %bitcast.1, bf16[6,256,128]{2,1,0:T(8,128)(2,1)} %k_ref.7, bf16[6,256,128]{2,1,0:T(8,128)(2,1)} %v_ref.7), custom_call_target="tpu_custom_call" | custom-call | flops 1 | bytes 1 | tf_op jit(solution)/shard_map/pack_keys/pallas_call | solution.py:353
  2.0 3.0 %collective-permute-start = (bf16[2,3,256,128]{3,2,1,0:T(8,128)(2,1)S(1)}, bf16[2,3,256,128]{3,2,1,0:T(8,128)(2,1)S(1)}, u32[]{:S(2)}, u32[]{:S(2)}) collective-permute-start(bf16[2,3,256,128]{3,2,1,0:T(8,128)(2,1)S(1)} %get-tuple-element.34), channel_id=1, source_target_pairs={{0,2},{2,0},{4,6},{6,4},{8,10},{10,8},{12,14},{14,12},{1,3},{3,1},... | collective-permute-start | bytes 1179656 | tf_op jit(solution)/shard_map/ppermute | solution.py:37
  5.0 0.1 pack_more_keys.1
  5.1 0.0 copy-start
  5.1 0.0 copy-start.1
  5.1 0.8 %collective-permute-start.1 = (bf16[2,3,256,128]{3,2,1,0:T(8,128)(2,1)S(1)}, bf16[2,3,256,128]{3,2,1,0:T(8,128)(2,1)S(1)}, u32[]{:S(2)}, u32[]{:S(2)}) collective-permute-start(bf16[2,3,256,128]{3,2,1,0:T(8,128)(2,1)S(1)} %pack_more_keys.1), channel_id=1, source_target_pairs={{2,4},{4,2},{6,8},{8,6},{10,12},{12,10},{3,5},{5,3},{7,9},{9,7},{1... | collective-permute-start | bytes 1179656 | tf_op jit(solution)/shard_map/ppermute | solution.py:37
  5.9 4.4 %own_scores.1 = (f32[6,256,256]{2,1,0:T(8,128)S(1)}, f32[6,256,256]{2,1,0:T(8,128)S(1)}, f32[6,3,256]{2,1,0:T(4,128)S(1)}, bf16[2,3,256,128]{3,2,1,0:T(8,128)(2,1)S(1)}, bf16[2,3,256,128]{3,2,1,0:T(8,128)(2,1)S(1)}) custom-call(s32[24]{0:T(128)S(4)} %table.1.table_ref, bf16[6,256,128]{2,1,0:T(8,128)(2,1)} %q_ref.5, bf16[6,256,128]{2,1,0:T(8,128)(2,1)} %k_ref.7, ...), custom_call_target="tpu_custom_call" | custom-call | flops 1 | bytes 1 | tf_op jit(solution)/shard_map/own_scores/pallas_call | solution.py:390
  10.3 5.4 %collective-permute-start.2 = (bf16[2,3,256,128]{3,2,1,0:T(8,128)(2,1)S(1)}, bf16[2,3,256,128]{3,2,1,0:T(8,128)(2,1)S(1)}, u32[]{:S(2)}, u32[]{:S(2)}) collective-permute-start(bf16[2,3,256,128]{3,2,1,0:T(8,128)(2,1)S(1)} %get-tuple-element.42), channel_id=1, source_target_pairs={{0,2},{2,0},{4,6},{6,4},{8,10},{10,8},{12,14},{14,12},{1,3},{3,1},... | collective-permute-start | bytes 1179656 | tf_op jit(solution)/shard_map/ppermute | solution.py:37
  15.7 7.2 %collective-permute-done.rest_0_.rest_6_ = bf16[2,3,256,128]{3,2,1,0:T(8,128)(2,1)S(1)} collective-permute-done((bf16[2,3,256,128]{3,2,1,0:T(8,128)(2,1)S(1)}, bf16[2,3,256,128]{3,2,1,0:T(8,128)(2,1)S(1)}, u32[]{:S(2)}, u32[]{:S(2)}) %collective-permute-start) | collective-permute-done | bytes 393248 | tf_op jit(solution)/shard_map/ppermute | solution.py:37
  22.9 0.7 %collective-permute-start.3 = (bf16[2,3,256,128]{3,2,1,0:T(8,128)(2,1)S(1)}, bf16[2,3,256,128]{3,2,1,0:T(8,128)(2,1)S(1)}, u32[]{:S(2)}, u32[]{:S(2)}) collective-permute-start(bf16[2,3,256,128]{3,2,1,0:T(8,128)(2,1)S(1)} %get-tuple-element.43), channel_id=1, source_target_pairs={{2,4},{4,2},{6,8},{8,6},{10,12},{12,10},{3,5},{5,3},{7,9},{9,7},{1... | collective-permute-start | bytes 1179656 | tf_op jit(solution)/shard_map/ppermute | solution.py:37
  23.6 0.0 collective-permute-done.1.rest_1_.rest_7_
  23.6 0.0 copy-done.2
  23.6 0.0 copy-done.3
  23.6 0.9 %statistics.1 = (f32[6,256,256]{2,1,0:T(8,128)S(1)}, f32[6,256,256]{2,1,0:T(8,128)S(1)}, f32[6,2,256]{2,1,0:T(2,128)S(1)}, f32[6,2,256]{2,1,0:T(2,128)S(1)}, f32...) custom-call(s32[24]{0:T(128)S(4)} %table.1.table_ref, bf16[6,256,128]{2,1,0:T(8,128)(2,1)S(1)} %copy-done.2, ...), custom_call_target="tpu_custom_call" | custom-call | flops 1 | bytes 1 | tf_op jit(solution)/shard_map/statistics/pallas_call | solution.py:405
  24.5 0.7 %collective-permute-start.4 = (f32[3,2,256]{2,1,0:T(2,128)S(1)}, f32[3,2,256]{2,1,0:T(2,128)S(1)}, u32[]{:S(2)}, u32[]{:S(2)}) collective-permute-start(f32[3,2,256]{2,1,0:T(2,128)S(1)} %get-tuple-element.44), channel_id=1, source_target_pairs={{2,4},{4,2},{6,8},{8,6},{10,12},{12,10},{3,5},{5,3},{7,9},{9,7},{1... | collective-permute-start | bytes 18440 | tf_op jit(solution)/shard_map/ppermute | solution.py:37
  25.2 7.9 %collective-permute-start.5 = (f32[3,2,256]{2,1,0:T(2,128)S(1)}, f32[3,2,256]{2,1,0:T(2,128)S(1)}, u32[]{:S(2)}, u32[]{:S(2)}) collective-permute-start(f32[3,2,256]{2,1,0:T(2,128)S(1)} %get-tuple-element.49), channel_id=1, source_target_pairs={{0,2},{2,0},{4,6},{6,4},{8,10},{10,8},{12,14},{14,12},{1,3},{3,1},... | collective-permute-start | bytes 18440 | tf_op jit(solution)/shard_map/ppermute | solution.py:37
  33.2 0.0 copy-done.1
  33.2 2.7 %reader.1 = (bf16[6,256,128]{2,1,0:T(8,128)(2,1)}, bf16[6,256,128]{2,1,0:T(8,128)(2,1)}, f32[6,256,128]{2,1,0:T(8,128)S(1)}, f32[6,256,128]{2,1,0:T(8,128)S(1)}) custom-call(s32[24]{0:T(128)S(4)} %table.1.table_ref, bf16[6,256,128]{2,1,0:T(8,128)(2,1)S(1)} %copy-done.2, bf16[6,256,128]{2,1,0:T(8,128)(2,1)S(1)} %copy-done, ...), custom_call_target="tpu_custom_call" | custom-call | flops 99999997952 | bytes 1 | tf_op jit(solution)/shard_map/reader/pallas_call | solution.py:420
  35.9 0.0 collective-permute-done.4.rest_1_
  35.9 0.0 collective-permute-done.3.rest_0_
  35.9 0.8 %owner.1 = (f32[6,256,128]{2,1,0:T(8,128)S(1)}, f32[6,256,128]{2,1,0:T(8,128)S(1)}) custom-call(s32[24]{0:T(128)S(4)} %table.1.table_ref, bf16[6,256,128]{2,1,0:T(8,128)(2,1)S(1)} %copy-done, bf16[6,256,128]{2,1,0:T(8,128)(2,1)S(1)} %copy-done.1, ...), custom_call_target="tpu_custom_call", output_to_operand_aliasing={{0}: (5, {}), {1}: (6, {})} | custom-call | flops 1 | bytes 1 | tf_op jit(solution)/shard_map/owner/pallas_call | solution.py:444
  36.7 2.1 %collective-permute-done.2.rest_0_ = bf16[2,3,256,128]{3,2,1,0:T(8,128)(2,1)S(1)} collective-permute-done((bf16[2,3,256,128]{3,2,1,0:T(8,128)(2,1)S(1)}, bf16[2,3,256,128]{3,2,1,0:T(8,128)(2,1)S(1)}, u32[]{:S(2)}, u32[]{:S(2)}) %collective-permute-start.2) | collective-permute-done | bytes 393248 | tf_op jit(solution)/shard_map/ppermute | solution.py:37
  38.8 0.1 collective-permute-done.5.rest_1_
  38.9 1.7 %last_owner.1 = (bf16[6,256,128]{2,1,0:T(8,128)(2,1)}, bf16[6,256,128]{2,1,0:T(8,128)(2,1)}) custom-call(s32[24]{0:T(128)S(4)} %table.1.table_ref, bf16[6,256,128]{2,1,0:T(8,128)(2,1)S(1)} %copy-done, bf16[6,256,128]{2,1,0:T(8,128)(2,1)S(1)} %copy-done.1, bf16[2,3,256,128]{3,2,1,0:T(8,128)(2,1)S(1)} %collective-permute-done.2.rest_0_, ...), custom_call_target="tpu_custom_call" | custom-call | flops 1 | bytes 1 | tf_op jit(solution)/shard_map/last_owner/pallas_call | solution.py:455
  (4 shorter events, 0.0 us)
Async XLA Ops:
  2.0 21.0 %collective-permute-start = (bf16[2,3,256,128]{3,2,1,0:T(8,128)(2,1)S(1)}, bf16[2,3,256,128]{3,2,1,0:T(8,128)(2,1)S(1)}, u32[]{:S(2)}, u32[]{:S(2)}) collective-permute-start(bf16[2,3,256,128]{3,2,1,0:T(8,128)(2,1)S(1)} %get-tuple-element.34), channel_id=1, source_target_pairs={{0,2},{2,0},{4,6},{6,4},{8,10},{10,8},{12,14},{14,12},{1,3},{3,1},... | collective-permute-start | bytes 1179656 | tf_op jit(solution)/shard_map/ppermute | solution.py:37
  5.0 18.6 %copy-start.2 = (bf16[6,256,128]{2,1,0:T(8,128)(2,1)S(1)}, bf16[6,256,128]{2,1,0:T(8,128)(2,1)}, u32[]{:S(2)}) copy-start(bf16[6,256,128]{2,1,0:T(8,128)(2,1)} %q_ref.5) | copy-start | bytes 1179652
  5.0 18.6 %copy-start.3 = (bf16[6,256,128]{2,1,0:T(8,128)(2,1)S(1)}, bf16[6,256,128]{2,1,0:T(8,128)(2,1)}, u32[]{:S(2)}) copy-start(bf16[6,256,128]{2,1,0:T(8,128)(2,1)} %g_ref.5) | copy-start | bytes 1179652
  5.1 28.1 %copy-start = (bf16[6,256,128]{2,1,0:T(8,128)(2,1)S(1)}, bf16[6,256,128]{2,1,0:T(8,128)(2,1)}, u32[]{:S(2)}) copy-start(bf16[6,256,128]{2,1,0:T(8,128)(2,1)} %k_ref.7) | copy-start | bytes 1179652
  5.1 28.1 %copy-start.1 = (bf16[6,256,128]{2,1,0:T(8,128)(2,1)S(1)}, bf16[6,256,128]{2,1,0:T(8,128)(2,1)}, u32[]{:S(2)}) copy-start(bf16[6,256,128]{2,1,0:T(8,128)(2,1)} %v_ref.7) | copy-start | bytes 1179652
  5.1 18.5 %collective-permute-start.1 = (bf16[2,3,256,128]{3,2,1,0:T(8,128)(2,1)S(1)}, bf16[2,3,256,128]{3,2,1,0:T(8,128)(2,1)S(1)}, u32[]{:S(2)}, u32[]{:S(2)}) collective-permute-start(bf16[2,3,256,128]{3,2,1,0:T(8,128)(2,1)S(1)} %pack_more_keys.1), channel_id=1, source_target_pairs={{2,4},{4,2},{6,8},{8,6},{10,12},{12,10},{3,5},{5,3},{7,9},{9,7},{1... | collective-permute-start | bytes 1179656 | tf_op jit(solution)/shard_map/ppermute | solution.py:37
  10.3 28.5 %collective-permute-start.2 = (bf16[2,3,256,128]{3,2,1,0:T(8,128)(2,1)S(1)}, bf16[2,3,256,128]{3,2,1,0:T(8,128)(2,1)S(1)}, u32[]{:S(2)}, u32[]{:S(2)}) collective-permute-start(bf16[2,3,256,128]{3,2,1,0:T(8,128)(2,1)S(1)} %get-tuple-element.42), channel_id=1, source_target_pairs={{0,2},{2,0},{4,6},{6,4},{8,10},{10,8},{12,14},{14,12},{1,3},{3,1},... | collective-permute-start | bytes 1179656 | tf_op jit(solution)/shard_map/ppermute | solution.py:37
  22.9 13.0 %collective-permute-start.3 = (bf16[2,3,256,128]{3,2,1,0:T(8,128)(2,1)S(1)}, bf16[2,3,256,128]{3,2,1,0:T(8,128)(2,1)S(1)}, u32[]{:S(2)}, u32[]{:S(2)}) collective-permute-start(bf16[2,3,256,128]{3,2,1,0:T(8,128)(2,1)S(1)} %get-tuple-element.43), channel_id=1, source_target_pairs={{2,4},{4,2},{6,8},{8,6},{10,12},{12,10},{3,5},{5,3},{7,9},{9,7},{1... | collective-permute-start | bytes 1179656 | tf_op jit(solution)/shard_map/ppermute | solution.py:37
  24.5 11.4 %collective-permute-start.4 = (f32[3,2,256]{2,1,0:T(2,128)S(1)}, f32[3,2,256]{2,1,0:T(2,128)S(1)}, u32[]{:S(2)}, u32[]{:S(2)}) collective-permute-start(f32[3,2,256]{2,1,0:T(2,128)S(1)} %get-tuple-element.44), channel_id=1, source_target_pairs={{2,4},{4,2},{6,8},{8,6},{10,12},{12,10},{3,5},{5,3},{7,9},{9,7},{1... | collective-permute-start | bytes 18440 | tf_op jit(solution)/shard_map/ppermute | solution.py:37
  25.2 13.7 %collective-permute-start.5 = (f32[3,2,256]{2,1,0:T(2,128)S(1)}, f32[3,2,256]{2,1,0:T(2,128)S(1)}, u32[]{:S(2)}, u32[]{:S(2)}) collective-permute-start(f32[3,2,256]{2,1,0:T(2,128)S(1)} %get-tuple-element.49), channel_id=1, source_target_pairs={{0,2},{2,0},{4,6},{6,4},{8,10},{10,8},{12,14},{14,12},{1,3},{3,1},... | collective-permute-start | bytes 18440 | tf_op jit(solution)/shard_map/ppermute | solution.py:37

commit v5 on v4

--- a/solution.py
+++ b/solution.py
@@ -77,13 +77,14 @@
     return functools.reduce(jnp.logical_or, [lists[head, entry, reader] == tile for entry in entries])
 
 
-def pack_keys_kernel(cap, channel, lists_hbm, keys, values, target, lists, held, sems):
+def pack_keys_kernel(cap, channel, lists_hbm, keys, values, target, lists, *rest):
+    *held, sems = rest
     heads, _, tile_count = lists.shape
     loads = [pltpu.make_async_copy(lists_hbm, lists, sems.at[2, 0])]
     for part, source in enumerate((keys, values)):
         for head in range(heads):
             loads.append(
-                pltpu.make_async_copy(source.at[head], held.at[part, head], sems.at[part, head])
+                pltpu.make_async_copy(source.at[head], held[part].at[head], sems.at[part, head])
             )
     for load in loads:
         load.start()
@@ -103,7 +104,7 @@
         load.wait()
     for slot in range(cap):
         for part in range(2):
-            target[part, slot] = held[part, chosen[slot]]
+            target[part, slot] = held[part][chosen[slot]]
 
 
 def pack_more_keys_kernel(count, cap, number, table_ref, keys, values, target, sems):
@@ -159,7 +160,7 @@
 
     def copies(stage):
         for number in range(count):
-            for slot in range(cap):
+            for slot in range(targets[number].shape[1]):
                 head = table_ref[table.reader_at(number, slot)]
 
                 @pl.when(head >= 0)
@@ -235,18 +236,32 @@
                 stats[number][slots[number], 1:2] = delta
 
 
+def softmax_grad(weight, prob_grad, factors):
+    prob = weight * factors[0:1]
+    score_grad = prob * (prob_grad - factors[1:2])
+    return prob.astype(jnp.bfloat16), score_grad.astype(jnp.bfloat16)
+
+
+def returned_kernel(count, cap, scale, table_ref, q_ref, g_ref, *rest):
+    far_weight, far_prob_grad, far_factors, terms = rest
+    table = Table(table_ref, q_ref.shape[0], count, cap)
+    returned = terms.shape[1]
+    for number in range(returned):
+        place = cap - returned + number
+        head = jnp.maximum(table_ref[table.reader_at(0, place)], 0)
+        prob, score_grad = softmax_grad(
+            far_weight[place], far_prob_grad[place], far_factors[place]
+        )
+        terms[0, number] = (dot_nn(score_grad, q_ref[head]) * scale).astype(jnp.bfloat16)
+        terms[1, number] = dot_nn(prob, g_ref[head]).astype(jnp.bfloat16)
+
+
 def reader_kernel(count, cap, scale, table_ref, q_ref, k_ref, v_ref, g_ref, *rest):
     own_weight, own_prob_grad, own_factors, far_weight, far_prob_grad, far_factors = rest[:6]
     fetched, rest = rest[6 : 6 + count], rest[6 + count :]
     o_ref, dq_ref, dk_ref, dv_ref, o_sum, dq_sum = rest
     heads = q_ref.shape[0]
     table = Table(table_ref, heads, count, cap)
-
-    def softmax_grad(weight, prob_grad, factors):
-        prob = weight * factors[0:1]
-        score_grad = prob * (prob_grad - factors[1:2])
-        return prob.astype(jnp.bfloat16), score_grad.astype(jnp.bfloat16)
-
     for head in range(heads):
         prob, score_grad = softmax_grad(own_weight[head], own_prob_grad[head], own_factors[head])
         o_sum[head] = dot_tn(v_ref[head], prob)
@@ -255,17 +270,16 @@
         dv_ref[head] = dot_nn(prob, g_ref[head])
     for number in range(count):
         for slot in range(cap):
-            head = table_ref[table.reader_at(number, slot)]
+            found = table_ref[table.reader_at(number, slot)]
+            head = jnp.maximum(found, 0)
             place = number * cap + slot
-
-            @pl.when(head >= 0)
-            def _():
-                prob, score_grad = softmax_grad(
-                    far_weight[place], far_prob_grad[place], far_factors[place]
-                )
-                o_sum[head] += dot_tn(fetched[number][1, slot], prob)
-                dq_sum[head] += dot_tn(fetched[number][0, slot], score_grad)
-
+            prob, score_grad = softmax_grad(
+                far_weight[place], far_prob_grad[place], far_factors[place]
+            )
+            o_term = dot_tn(fetched[number][1, slot], prob)
+            dq_term = dot_tn(fetched[number][0, slot], score_grad)
+            o_sum[head] += jnp.where(found >= 0, o_term, 0.0)
+            dq_sum[head] += jnp.where(found >= 0, dq_term, 0.0)
     for head in range(heads):
         o_ref[head] = o_sum[head].T.astype(jnp.bfloat16)
         dq_ref[head] = (dq_sum[head] * scale).T.astype(jnp.bfloat16)
@@ -284,45 +298,78 @@
     return found, head, jnp.where(found >= 0, dk_term, 0.0), jnp.where(found >= 0, dv_term, 0.0)
 
 
-def owner_kernel(count, cap, scale, number, table_ref, k_ref, v_ref, *rest):
-    arrived, stats, _, _, dk_sum, dv_sum = rest
-    table = Table(table_ref, k_ref.shape[0], count, cap)
+def owner_kernel(count, cap, scale, number, table_ref, k_ref, v_ref, arrived, stats, *rest):
+    *rest, dk_sum, dv_sum, rounded, sems, rounded_sems = rest
+    heads = k_ref.shape[0]
+    table = Table(table_ref, heads, count, cap)
+    closing = number == 1
+    results = rest[2:]
+    if closing:
+        *results, dk_out, dv_out = results
+    copies = []
+    for part in range(len(results) // 2):
+        for head in range(heads):
+            source, result = results[part], results[part + len(results) // 2]
+            copies.append(
+                pltpu.make_async_copy(source.at[head], result.at[head], sems.at[part, head])
+            )
+    for copy in copies:
+        copy.start()
     for slot in range(cap):
         _, head, dk_term, dv_term = owner_terms(
             table, number, scale, k_ref, v_ref, arrived, stats, slot
         )
         dk_sum[head] += dk_term
         dv_sum[head] += dv_term
-
-
-def last_owner_kernel(count, cap, scale, table_ref, k_ref, v_ref, *rest):
-    arrived, stats, dk_in, dv_in, dk_out, dv_out, rounded, staged, sems, staged_sems = rest
-    heads = k_ref.shape[0]
-    table = Table(table_ref, heads, count, cap)
-    owners = [table_ref[table.owner_at(0, slot)] for slot in range(cap)]
+    complete = []
+    if closing:
+        awaited = [table_ref[table.owner_at(0, slot)] for slot in range(cap)]
+        for head in range(heads):
+            wanted = functools.reduce(jnp.logical_and, [owner != head for owner in awaited])
+            for part, (total, result) in enumerate(((dk_sum, dk_out), (dv_sum, dv_out))):
+                rounded[part, head] = total[head].astype(jnp.bfloat16)
+                copy = pltpu.make_async_copy(
+                    rounded.at[part, head], result.at[head], rounded_sems.at[part, head]
+                )
+                complete.append((wanted, copy))
+    for wanted, copy in complete:
+        pl.when(wanted)(copy.start)
+    for copy in copies:
+        copy.wait()
+    for wanted, copy in complete:
+        pl.when(wanted)(copy.wait)
+
+
+def first_owner_kernel(count, cap, scale, table_ref, k_ref, v_ref, arrived, stats, *rest):
+    _, _, dk_sum, dv_sum = rest
+    table = Table(table_ref, k_ref.shape[0], count, cap)
+    for slot in range(arrived.shape[1]):
+        _, head, dk_term, dv_term = owner_terms(
+            table, 0, scale, k_ref, v_ref, arrived, stats, slot
+        )
+        dk_sum[head] += dk_term
+        dv_sum[head] += dv_term
+
+
+def closing_kernel(count, cap, table_ref, terms, dk_in, dv_in, *rest):
+    _, _, dk_out, dv_out, staged, sems = rest
+    table = Table(table_ref, dk_in.shape[0], count, cap)
+    early = cap - terms.shape[1]
     copies = []
-    for head in range(heads):
-        untouched = functools.reduce(jnp.logical_and, [owner != head for owner in owners])
+    for slot in range(cap):
+        found = table_ref[table.owner_at(0, slot)]
+        head = jnp.maximum(found, 0)
         for part, (total, result) in enumerate(((dk_in, dk_out), (dv_in, dv_out))):
-            rounded[part, head] = total[head].astype(jnp.bfloat16)
+            value = total[head]
+            if slot >= early:
+                value = value + terms[part, slot - early].astype(jnp.float32)
+            staged[part, slot] = value.astype(jnp.bfloat16)
             copy = pltpu.make_async_copy(
-                rounded.at[part, head], result.at[head], sems.at[part, head]
+                staged.at[part, slot], result.at[head], sems.at[part, slot]
             )
-            copies.append((untouched, copy))
+            copies.append((found >= 0, copy))
     for wanted, copy in copies:
         pl.when(wanted)(copy.start)
-    for slot in range(cap):
-        found, head, dk_term, dv_term = owner_terms(
-            table, 0, scale, k_ref, v_ref, arrived, stats, slot
-        )
-        staged[0, slot] = (dk_in[head] + dk_term).astype(jnp.bfloat16)
-        staged[1, slot] = (dv_in[head] + dv_term).astype(jnp.bfloat16)
-        for part, result in enumerate((dk_out, dv_out)):
-            copy = pltpu.make_async_copy(
-                staged.at[part, slot], result.at[head], staged_sems.at[part, slot]
-            )
-            copies.append((found >= 0, copy))
-            pl.when(found >= 0)(copy.start)
     for wanted, copy in copies:
         pl.when(wanted)(copy.wait)
 
@@ -332,6 +379,7 @@
     channels = channel_list(lax.axis_size("seq"))
     count = len(channels)
     cap = heads // 2
+    early = cap - 1
     scale = width ** (-0.5)
     table_size = Table(None, heads, count, cap).size()
     smem = pl.BlockSpec(memory_space=pltpu.SMEM)
@@ -339,8 +387,12 @@
     vmem = pl.BlockSpec(memory_space=pltpu.VMEM)
     params = pltpu.CompilerParams(vmem_limit_bytes=VMEM_LIMIT)
     brief = pl.CostEstimate(flops=1, bytes_accessed=1, transcendentals=0)
+    lengthy = pl.CostEstimate(flops=10**11, bytes_accessed=1, transcendentals=0)
     packed = pltpu.VMEM((2, cap, tokens, width), jnp.bfloat16)
     whole = jax.ShapeDtypeStruct((heads, tokens, width), jnp.bfloat16)
+    whole_near = pltpu.VMEM((heads, tokens, width), jnp.bfloat16)
+    whole_pair = pltpu.VMEM((2, heads, tokens, width), jnp.bfloat16)
+    copies_whole = pltpu.SemaphoreType.DMA((2, heads))
     whole_sum = pltpu.VMEM((heads, tokens, width), jnp.float32)
     squares = pltpu.VMEM((heads, tokens, tokens), jnp.float32)
     far_squares = pltpu.VMEM((count * cap, tokens, tokens), jnp.float32)
@@ -350,15 +402,12 @@
         pltpu.with_memory_space_constraint(array, pltpu.HBM)
         for array in (jnp.swapaxes(tile_lists, 1, 2), queries, keys, values, out_grad)
     )
-    key_value, lists = pl.pallas_call(
+    key_value, lists, keys, values = pl.pallas_call(
         functools.partial(pack_keys_kernel, cap, channels[0]),
-        out_shape=[packed, pltpu.SMEM(lists.shape, jnp.int32)],
+        out_shape=[packed, pltpu.SMEM(lists.shape, jnp.int32)] + [whole_near] * 2,
         in_specs=[anywhere] * 3,
-        out_specs=[vmem, smem],
-        scratch_shapes=[
-            pltpu.VMEM((2, heads, tokens, width), jnp.bfloat16),
-            pltpu.SemaphoreType.DMA((3, heads)),
-        ],
+        out_specs=[vmem, smem, vmem, vmem],
+        scratch_shapes=[pltpu.SemaphoreType.DMA((3, heads))],
         compiler_params=params,
         cost_estimate=brief,
         name="pack_keys",
@@ -377,20 +426,21 @@
         key_value = pl.pallas_call(
             functools.partial(pack_more_keys_kernel, count, cap, number),
             out_shape=packed,
-            in_specs=[smem, anywhere, anywhere],
+            in_specs=[smem, vmem, vmem],
             out_specs=vmem,
             scratch_shapes=[pltpu.SemaphoreType.DMA((2, cap))],
             compiler_params=params,
             cost_estimate=brief,
             name="pack_more_keys",
-        )(table, k_far, v_far)
+        )(table, keys, values)
         fetched.append(swapped(key_value, channels[number]))
     one_head = pl.BlockSpec((1, tokens, width), lambda head: (head, 0, 0))
     one_square = pl.BlockSpec((1, tokens, tokens), lambda head: (head, 0, 0))
+    sent = [pltpu.VMEM((2, early, tokens, width), jnp.bfloat16)] + [packed] * (count - 1)
     own_weight, own_prob_grad, own_rows, *query_grads = pl.pallas_call(
         functools.partial(own_kernel, count, cap, scale),
         grid=(heads,),
-        out_shape=[squares] * 2 + [pltpu.VMEM((heads, 3, tokens), jnp.float32)] + [packed] * count,
+        out_shape=[squares] * 2 + [pltpu.VMEM((heads, 3, tokens), jnp.float32)] + sent,
         in_specs=[smem] + [one_head] * 4 + [anywhere] * 2,
         out_specs=[one_square] * 2
         + [pl.BlockSpec((1, 3, tokens), lambda head: (head, 0, 0))]
@@ -399,7 +449,7 @@
         compiler_params=params,
         cost_estimate=brief,
         name="own_scores",
-    )(table, q_far, k_far, v_far, g_far, q_far, g_far)
+    )(table, q_far, keys, values, g_far, q_far, g_far)
     query_grads[1:], fetched[0] = lax.optimization_barrier((query_grads[1:], fetched[0]))
     arrived = [swapped(block, channel) for block, channel in zip(query_grads, channels)]
     far_weight, far_prob_grad, own_factors, far_factors, *stats = pl.pallas_call(
@@ -416,15 +466,25 @@
         name="statistics",
     )(table, queries, out_grad, own_rows, *fetched)
     stats = [swapped(block, channel) for block, channel in zip(stats, channels)]
+    terms = pl.pallas_call(
+        functools.partial(returned_kernel, count, cap, scale),
+        out_shape=pltpu.VMEM((2, cap - early, tokens, width), jnp.bfloat16),
+        in_specs=[smem] + [vmem] * 5,
+        out_specs=vmem,
+        compiler_params=params,
+        cost_estimate=brief,
+        name="returned",
+    )(table, queries, out_grad, far_weight, far_prob_grad, far_factors)
+    terms = swapped(terms, channels[0])
     transposed_sums = pltpu.VMEM((heads, width, tokens), jnp.float32)
-    attn_out, query_grad, key_sum, value_sum = pl.pallas_call(
+    *finished, key_sum, value_sum = pl.pallas_call(
         functools.partial(reader_kernel, count, cap, scale),
-        out_shape=[whole] * 2 + [whole_sum] * 2,
+        out_shape=[whole_near] * 2 + [whole_sum] * 2,
         in_specs=[smem] + [vmem] * (10 + count),
         out_specs=[vmem] * 4,
         scratch_shapes=[transposed_sums] * 2,
         compiler_params=params,
-        cost_estimate=pl.CostEstimate(flops=100000000000, bytes_accessed=1, transcendentals=0),
+        cost_estimate=lengthy,
         name="reader",
     )(
         table,
@@ -440,34 +500,59 @@
         far_factors,
         *fetched,
     )
+    results = []
     for number in range(count - 1, 0, -1):
-        key_sum, value_sum = pl.pallas_call(
+        stored = 2 if number == count - 1 else 0
+        outputs = stored + (2 if number == 1 else 0)
+        *stored_now, key_sum, value_sum = pl.pallas_call(
             functools.partial(owner_kernel, count, cap, scale, number),
-            out_shape=[whole_sum] * 2,
-            in_specs=[smem] + [vmem] * 6,
-            out_specs=[vmem] * 2,
-            input_output_aliases={5: 0, 6: 1},
+            out_shape=[whole] * outputs + [whole_sum] * 2,
+            in_specs=[smem] + [vmem] * (6 + stored),
+            out_specs=[anywhere] * outputs + [vmem] * 2,
+            scratch_shapes=[whole_pair, copies_whole, copies_whole],
+            input_output_aliases={5: outputs, 6: outputs + 1},
             compiler_params=params,
             cost_estimate=brief,
             name="owner",
-        )(table, keys, values, arrived[number], stats[number], key_sum, value_sum)
-    last, key_sum = lax.optimization_barrier((arrived[0], key_sum))
+        )(
+            table,
+            keys,
+            values,
+            arrived[number],
+            stats[number],
+            key_sum,
+            value_sum,
+            *(finished if stored else []),
+        )
+        results += stored_now
+    *results, key_grad, value_grad = results
+    first, key_sum = lax.optimization_barrier((arrived[0], key_sum))
+    key_sum, value_sum = pl.pallas_call(
+        functools.partial(first_owner_kernel, count, cap, scale),
+        out_shape=[whole_sum] * 2,
+        in_specs=[smem] + [vmem] * 6,
+        out_specs=[vmem] * 2,
+        input_output_aliases={5: 0, 6: 1},
+        compiler_params=params,
+        cost_estimate=brief,
+        name="first_owner",
+    )(table, keys, values, first, stats[0], key_sum, value_sum)
+    terms, key_sum = lax.optimization_barrier((terms, key_sum))
     key_grad, value_grad = pl.pallas_call(
-        functools.partial(last_owner_kernel, count, cap, scale),
+        functools.partial(closing_kernel, count, cap),
         out_shape=[whole] * 2,
-        in_specs=[smem] + [vmem] * 6,
+        in_specs=[smem] + [vmem] * 3 + [anywhere] * 2,
         out_specs=[anywhere] * 2,
         scratch_shapes=[
-            pltpu.VMEM((2, heads, tokens, width), jnp.bfloat16),
             pltpu.VMEM((2, cap, tokens, width), jnp.bfloat16),
-            pltpu.SemaphoreType.DMA((2, heads)),
             pltpu.SemaphoreType.DMA((2, cap)),
         ],
-        compiler_params=params,
-        cost_estimate=brief,
-        name="last_owner",
-    )(table, keys, values, last, stats[0], key_sum, value_sum)
-    return attn_out, query_grad, key_grad, value_grad
+        input_output_aliases={4: 0, 5: 1},
+        compiler_params=params,
+        cost_estimate=brief,
+        name="closing",
+    )(table, terms, key_sum, value_sum, key_grad, value_grad)
+    return *results, key_grad, value_grad
 
 
 def solution(mesh):

time: 41 us -> 40.1 us (0.978)
  starting transfers between devices: 18.5 us -> 17.5 us
    pallas_call x1, Pallas kernels: 0.81 us -> 2.09 us  [per_device(): pl.pallas_call(functools.partial(owner_kernel, count, cap, scale, number)...]
    pallas_call x1, Pallas kernels: 2.73 us -> 1.53 us  [per_device(): pl.pallas_call(functools.partial(reader_kernel, count, cap, scale), out_s...]
    ppermute x6 -> x7, starting transfers between devices: 18.5 us -> 17.5 us  [swapped(): return lax.ppermute(block, 'seq', swap_route(channel, lax.axis_size('seq')))]
    ppermute x6 -> x7, waiting for transfers between devices: 9.37 us -> 9.7 us  [swapped(): return lax.ppermute(block, 'seq', swap_route(channel, lax.axis_size('seq')))]
    pallas_call x1 -> x3, Pallas kernels: 1.65 us -> 1.59 us  [the longest x1 0.76 us: per_device(): pl.pallas_call(functools.partial(closing_kernel, count, cap), out_shape=[...]
  transfers between devices with their start and end apart: 6 -> 7, of which waited for: 3 -> 3; matrix products, arithmetic and copies ran while one was open for 0% -> 0% of each run, Pallas kernels for 22% -> 24%
where the time goes in v5:
time: 40.1 us; the launch traced here: 39.7 us
  starting transfers between devices  17.5 us (44%)
  Pallas kernels  11.7 us (29%)
  waiting for transfers between devices  9.7 us (24%)
  between operations  0.77 us (2%)
    ppermute x7, starting transfers between devices, swapped(): return lax.ppermute(block, 'seq', swap_route(channel, lax.axis_size('seq')))  17.5 us
    ppermute x7, waiting for transfers between devices, swapped(): return lax.ppermute(block, 'seq', swap_route(channel, lax.axis_size('seq')))  9.7 us
    pallas_call x1, Pallas kernels, per_device(): pl.pallas_call(functools.partial(own_kernel, count, cap, scale), grid=(he...  4.2 us
    pallas_call x1, Pallas kernels, per_device(): pl.pallas_call(functools.partial(owner_kernel, count, cap, scale, number)...  2.09 us
    pallas_call x1, Pallas kernels, per_device(): pl.pallas_call(functools.partial(reader_kernel, count, cap, scale), out_s...  1.53 us
    pallas_call x1, Pallas kernels, per_device(): pl.pallas_call(functools.partial(pack_keys_kernel, cap, channels[0]), out...  1.34 us
    pallas_call x1, Pallas kernels, per_device(): pl.pallas_call(functools.partial(statistics_kernel, count, cap, scale), o...  0.89 us
  transfers between devices with their start and end apart: 7, of which 3 were waited for; matrix products, arithmetic and copies ran while one was open for 0% of the time, Pallas kernels for 24%

profile of v5, /device:TPU:0, one launch (start us, length us, event | category | flops | bytes accessed | tf_op | source)
XLA Modules:
  0.0 39.7 jit_solution(14828883965740938440)
XLA Ops:
  0.6 1.3 %pack_keys.1 = (bf16[2,3,256,128]{3,2,1,0:T(8,128)(2,1)S(1)}, s32[6,4,8]{2,1,0:T(4,128)S(4)}, bf16[6,256,128]{2,1,0:T(8,128)(2,1)S(1)}, bf16[6,256,128]{2,1,0:T(8,128)(2,1)S(1)}) custom-call(s32[6,4,8]{2,1,0:T(4,128)} %bitcast.1, bf16[6,256,128]{2,1,0:T(8,128)(2,1)} %keys.1, bf16[6,256,128]{2,1,0:T(8,128)(2,1)} %values.1), custom_call_target="tpu_custom_call" | custom-call | flops 1 | bytes 1 | tf_op jit(solution)/shard_map/pack_keys/pallas_call | solution.py:405
  2.0 3.0 %collective-permute-start = (bf16[2,3,256,128]{3,2,1,0:T(8,128)(2,1)S(1)}, bf16[2,3,256,128]{3,2,1,0:T(8,128)(2,1)S(1)}, u32[]{:S(2)}, u32[]{:S(2)}) collective-permute-start(bf16[2,3,256,128]{3,2,1,0:T(8,128)(2,1)S(1)} %get-tuple-element.43), channel_id=1, source_target_pairs={{0,2},{2,0},{4,6},{6,4},{8,10},{10,8},{12,14},{14,12},{1,3},{3,1},... | collective-permute-start | bytes 1179656 | tf_op jit(solution)/shard_map/ppermute | solution.py:37
  5.0 0.1 pack_more_keys.1
  5.1 0.8 %collective-permute-start.2 = (bf16[2,3,256,128]{3,2,1,0:T(8,128)(2,1)S(1)}, bf16[2,3,256,128]{3,2,1,0:T(8,128)(2,1)S(1)}, u32[]{:S(2)}, u32[]{:S(2)}) collective-permute-start(bf16[2,3,256,128]{3,2,1,0:T(8,128)(2,1)S(1)} %pack_more_keys.1), channel_id=1, source_target_pairs={{2,4},{4,2},{6,8},{8,6},{10,12},{12,10},{3,5},{5,3},{7,9},{9,7},{1... | collective-permute-start | bytes 1179656 | tf_op jit(solution)/shard_map/ppermute | solution.py:37
  5.9 4.2 %own_scores.1 = (f32[6,256,256]{2,1,0:T(8,128)S(1)}, f32[6,256,256]{2,1,0:T(8,128)S(1)}, f32[6,3,256]{2,1,0:T(4,128)S(1)}, bf16[2,2,256,128]{3,2,1,0:T(8,128)(2,1)S(1)}, bf16[2,3,256,128]{3,2,1,0:T(8,128)(2,1)S(1)}) custom-call(s32[24]{0:T(128)S(4)} %table.1.table_ref, bf16[6,256,128]{2,1,0:T(8,128)(2,1)} %q_ref.7, ...), custom_call_target="tpu_custom_call" | custom-call | flops 1 | bytes 1 | tf_op jit(solution)/shard_map/own_scores/pallas_call | solution.py:440
  10.1 4.3 %collective-permute-start.5 = (bf16[2,2,256,128]{3,2,1,0:T(8,128)(2,1)S(1)}, bf16[2,2,256,128]{3,2,1,0:T(8,128)(2,1)S(1)}, u32[]{:S(2)}, u32[]{:S(2)}) collective-permute-start(bf16[2,2,256,128]{3,2,1,0:T(8,128)(2,1)S(1)} %get-tuple-element.60), channel_id=1, source_target_pairs={{0,2},{2,0},{4,6},{6,4},{8,10},{10,8},{12,14},{14,12},{1,3},{3,1},... | collective-permute-start | bytes 786440 | tf_op jit(solution)/shard_map/ppermute | solution.py:37
  14.4 8.5 %collective-permute-done.rest_0_.rest_6_ = bf16[2,3,256,128]{3,2,1,0:T(8,128)(2,1)S(1)} collective-permute-done((bf16[2,3,256,128]{3,2,1,0:T(8,128)(2,1)S(1)}, bf16[2,3,256,128]{3,2,1,0:T(8,128)(2,1)S(1)}, u32[]{:S(2)}, u32[]{:S(2)}) %collective-permute-start) | collective-permute-done | bytes 393248 | tf_op jit(solution)/shard_map/ppermute | solution.py:37
  22.9 0.7 %collective-permute-start.1 = (bf16[2,3,256,128]{3,2,1,0:T(8,128)(2,1)S(1)}, bf16[2,3,256,128]{3,2,1,0:T(8,128)(2,1)S(1)}, u32[]{:S(2)}, u32[]{:S(2)}) collective-permute-start(bf16[2,3,256,128]{3,2,1,0:T(8,128)(2,1)S(1)} %get-tuple-element.44), channel_id=1, source_target_pairs={{2,4},{4,2},{6,8},{8,6},{10,12},{12,10},{3,5},{5,3},{7,9},{9,7},{1... | collective-permute-start | bytes 1179656 | tf_op jit(solution)/shard_map/ppermute | solution.py:37
  23.6 0.0 collective-permute-done.2.rest_1_.rest_7_
  23.6 0.0 copy-done
  23.6 0.9 %statistics.1 = (f32[6,256,256]{2,1,0:T(8,128)S(1)}, f32[6,256,256]{2,1,0:T(8,128)S(1)}, f32[6,2,256]{2,1,0:T(2,128)S(1)}, f32[6,2,256]{2,1,0:T(2,128)S(1)}, f32...) custom-call(s32[24]{0:T(128)S(4)} %table.1.table_ref, bf16[6,256,128]{2,1,0:T(8,128)(2,1)S(1)} %copy-done, ...), custom_call_target="tpu_custom_call" | custom-call | flops 1 | bytes 1 | tf_op jit(solution)/shard_map/statistics/pallas_call | solution.py:455
  24.5 0.7 %collective-permute-start.3 = (f32[3,2,256]{2,1,0:T(2,128)S(1)}, f32[3,2,256]{2,1,0:T(2,128)S(1)}, u32[]{:S(2)}, u32[]{:S(2)}) collective-permute-start(f32[3,2,256]{2,1,0:T(2,128)S(1)} %get-tuple-element.47), channel_id=1, source_target_pairs={{2,4},{4,2},{6,8},{8,6},{10,12},{12,10},{3,5},{5,3},{7,9},{9,7},{1... | collective-permute-start | bytes 18440 | tf_op jit(solution)/shard_map/ppermute | solution.py:37
  25.2 7.9 %collective-permute-start.6 = (f32[3,2,256]{2,1,0:T(2,128)S(1)}, f32[3,2,256]{2,1,0:T(2,128)S(1)}, u32[]{:S(2)}, u32[]{:S(2)}) collective-permute-start(f32[3,2,256]{2,1,0:T(2,128)S(1)} %get-tuple-element.63), channel_id=1, source_target_pairs={{0,2},{2,0},{4,6},{6,4},{8,10},{10,8},{12,14},{14,12},{1,3},{3,1},... | collective-permute-start | bytes 18440 | tf_op jit(solution)/shard_map/ppermute | solution.py:37
  33.2 0.2 returned.1
  33.4 0.1 collective-permute-start.4
  33.5 1.5 %reader.1 = (bf16[6,256,128]{2,1,0:T(8,128)(2,1)S(1)}, bf16[6,256,128]{2,1,0:T(8,128)(2,1)S(1)}, f32[6,256,128]{2,1,0:T(8,128)S(1)}, f32[6,256,128]{2,1,0:T(8,128)S(1)}) custom-call(s32[24]{0:T(128)S(4)} %table.1.table_ref, bf16[6,256,128]{2,1,0:T(8,128)(2,1)S(1)} %copy-done, bf16[6,256,128]{2,1,0:T(8,128)(2,1)S(1)} %get-tuple-element.40.k_ref.keys, ...), custom_call_target="tpu_custom_call" | custom-call | flops 99999997952 | bytes 1 | tf_op jit(solution)/shard_map/reader/pallas_call | solution.py:480
  35.0 0.0 collective-permute-done.3.stats
  35.0 0.0 collective-permute-done.1.arrived
  35.0 2.1 %owner.1 = (bf16[6,256,128]{2,1,0:T(8,128)(2,1)}, bf16[6,256,128]{2,1,0:T(8,128)(2,1)}, bf16[6,256,128]{2,1,0:T(8,128)(2,1)}, bf16[6,256,128]{2,1,0:T(8,128)(2,1...) custom-call(s32[24]{0:T(128)S(4)} %table.1.table_ref, ...), custom_call_target="tpu_custom_call", output_to_operand_aliasing={{4}: (5, {}), {5}: (6, {})} | custom-call | flops 1 | bytes 1 | tf_op jit(solution)/shard_map/owner/pallas_call | solution.py:507
  37.1 0.0 collective-permute-done.5.arrived
  37.1 0.1 collective-permute-done.6.stats
  37.2 0.6 %first_owner.1 = (f32[6,256,128]{2,1,0:T(8,128)S(1)}, f32[6,256,128]{2,1,0:T(8,128)S(1)}) custom-call(s32[24]{0:T(128)S(4)} %table.1.table_ref, bf16[6,256,128]{2,1,0:T(8,128)(2,1)S(1)} %get-tuple-element.40.k_ref.keys, bf16[6,256,128]{2,1,0:T(8,128)(2,1)S(1)} %get-tuple-element.41.v_ref.values, ...), custom_call_target="tpu_custom_call", output_to_operand_aliasing={{0}: (5, {}), {1}: (6, {})} | custom-call | flops 1 | bytes 1 | tf_op jit(solution)/shard_map/first_owner/pallas_call | solution.py:530
  37.8 1.1 %collective-permute-done.4.terms = bf16[2,1,256,128]{3,2,1,0:T(8,128)(2,1)S(1)} collective-permute-done((bf16[2,1,256,128]{3,2,1,0:T(8,128)(2,1)S(1)}, bf16[2,1,256,128]{3,2,1,0:T(8,128)(2,1)S(1)}, u32[]{:S(2)}, u32[]{:S(2)}) %collective-permute-start.4) | collective-permute-done | bytes 131104 | tf_op jit(solution)/shard_map/ppermute | solution.py:37
  38.9 0.8 %closing.1 = (bf16[6,256,128]{2,1,0:T(8,128)(2,1)}, bf16[6,256,128]{2,1,0:T(8,128)(2,1)}) custom-call(s32[24]{0:T(128)S(4)} %table.1.table_ref, bf16[2,1,256,128]{3,2,1,0:T(8,128)(2,1)S(1)} %collective-permute-done.4.terms, f32[6,256,128]{2,1,0:T(8,128)S(1)} %get-tuple-element.68.dk_in, ...), custom_call_target="tpu_custom_call", output_to_operand_aliasing={{0}: (4, {}), {1}: (5, {})} | custom-call | flops 1 | bytes 1 | tf_op jit(solution)/shard_map/closing/pallas_call | solution.py:541
  (4 shorter events, 0.0 us)
Async XLA Ops:
  2.0 21.0 %collective-permute-start = (bf16[2,3,256,128]{3,2,1,0:T(8,128)(2,1)S(1)}, bf16[2,3,256,128]{3,2,1,0:T(8,128)(2,1)S(1)}, u32[]{:S(2)}, u32[]{:S(2)}) collective-permute-start(bf16[2,3,256,128]{3,2,1,0:T(8,128)(2,1)S(1)} %get-tuple-element.43), channel_id=1, source_target_pairs={{0,2},{2,0},{4,6},{6,4},{8,10},{10,8},{12,14},{14,12},{1,3},{3,1},... | collective-permute-start | bytes 1179656 | tf_op jit(solution)/shard_map/ppermute | solution.py:37
  5.0 18.6 %copy-start = (bf16[6,256,128]{2,1,0:T(8,128)(2,1)S(1)}, bf16[6,256,128]{2,1,0:T(8,128)(2,1)}, u32[]{:S(2)}) copy-start(bf16[6,256,128]{2,1,0:T(8,128)(2,1)} %q_ref.7) | copy-start | bytes 1179652
  5.0 18.6 %copy-start.1 = (bf16[6,256,128]{2,1,0:T(8,128)(2,1)S(1)}, bf16[6,256,128]{2,1,0:T(8,128)(2,1)}, u32[]{:S(2)}) copy-start(bf16[6,256,128]{2,1,0:T(8,128)(2,1)} %g_ref.7) | copy-start | bytes 1179652
  5.1 18.6 %collective-permute-start.2 = (bf16[2,3,256,128]{3,2,1,0:T(8,128)(2,1)S(1)}, bf16[2,3,256,128]{3,2,1,0:T(8,128)(2,1)S(1)}, u32[]{:S(2)}, u32[]{:S(2)}) collective-permute-start(bf16[2,3,256,128]{3,2,1,0:T(8,128)(2,1)S(1)} %pack_more_keys.1), channel_id=1, source_target_pairs={{2,4},{4,2},{6,8},{8,6},{10,12},{12,10},{3,5},{5,3},{7,9},{9,7},{1... | collective-permute-start | bytes 1179656 | tf_op jit(solution)/shard_map/ppermute | solution.py:37
  10.1 27.1 %collective-permute-start.5 = (bf16[2,2,256,128]{3,2,1,0:T(8,128)(2,1)S(1)}, bf16[2,2,256,128]{3,2,1,0:T(8,128)(2,1)S(1)}, u32[]{:S(2)}, u32[]{:S(2)}) collective-permute-start(bf16[2,2,256,128]{3,2,1,0:T(8,128)(2,1)S(1)} %get-tuple-element.60), channel_id=1, source_target_pairs={{0,2},{2,0},{4,6},{6,4},{8,10},{10,8},{12,14},{14,12},{1,3},{3,1},... | collective-permute-start | bytes 786440 | tf_op jit(solution)/shard_map/ppermute | solution.py:37
  22.9 12.1 %collective-permute-start.1 = (bf16[2,3,256,128]{3,2,1,0:T(8,128)(2,1)S(1)}, bf16[2,3,256,128]{3,2,1,0:T(8,128)(2,1)S(1)}, u32[]{:S(2)}, u32[]{:S(2)}) collective-permute-start(bf16[2,3,256,128]{3,2,1,0:T(8,128)(2,1)S(1)} %get-tuple-element.44), channel_id=1, source_target_pairs={{2,4},{4,2},{6,8},{8,6},{10,12},{12,10},{3,5},{5,3},{7,9},{9,7},{1... | collective-permute-start | bytes 1179656 | tf_op jit(solution)/shard_map/ppermute | solution.py:37
  24.5 10.5 %collective-permute-start.3 = (f32[3,2,256]{2,1,0:T(2,128)S(1)}, f32[3,2,256]{2,1,0:T(2,128)S(1)}, u32[]{:S(2)}, u32[]{:S(2)}) collective-permute-start(f32[3,2,256]{2,1,0:T(2,128)S(1)} %get-tuple-element.47), channel_id=1, source_target_pairs={{2,4},{4,2},{6,8},{8,6},{10,12},{12,10},{3,5},{5,3},{7,9},{9,7},{1... | collective-permute-start | bytes 18440 | tf_op jit(solution)/shard_map/ppermute | solution.py:37
  25.2 12.0 %collective-permute-start.6 = (f32[3,2,256]{2,1,0:T(2,128)S(1)}, f32[3,2,256]{2,1,0:T(2,128)S(1)}, u32[]{:S(2)}, u32[]{:S(2)}) collective-permute-start(f32[3,2,256]{2,1,0:T(2,128)S(1)} %get-tuple-element.63), channel_id=1, source_target_pairs={{0,2},{2,0},{4,6},{6,4},{8,10},{10,8},{12,14},{14,12},{1,3},{3,1},... | collective-permute-start | bytes 18440 | tf_op jit(solution)/shard_map/ppermute | solution.py:37
  33.4 5.5 %collective-permute-start.4 = (bf16[2,1,256,128]{3,2,1,0:T(8,128)(2,1)S(1)}, bf16[2,1,256,128]{3,2,1,0:T(8,128)(2,1)S(1)}, u32[]{:S(2)}, u32[]{:S(2)}) collective-permute-start(bf16[2,1,256,128]{3,2,1,0:T(8,128)(2,1)S(1)} %returned.1), channel_id=1, source_target_pairs={{0,2},{2,0},{4,6},{6,4},{8,10},{10,8},{12,14},{14,12},{1,3},{3,1},... | collective-permute-start | bytes 393224 | tf_op jit(solution)/shard_map/ppermute | solution.py:37

commit v6 on v5

--- a/solution.py
+++ b/solution.py
@@ -341,37 +341,44 @@
 
 
 def first_owner_kernel(count, cap, scale, table_ref, k_ref, v_ref, arrived, stats, *rest):
-    _, _, dk_sum, dv_sum = rest
+    dk_in, dv_in, _, _, dk_out, dv_out, staged, sems = rest
     table = Table(table_ref, k_ref.shape[0], count, cap)
+    stores = []
     for slot in range(arrived.shape[1]):
-        _, head, dk_term, dv_term = owner_terms(
+        found, head, *terms = owner_terms(
             table, 0, scale, k_ref, v_ref, arrived, stats, slot
         )
-        dk_sum[head] += dk_term
-        dv_sum[head] += dv_term
+        for part, (total, result) in enumerate(((dk_in, dk_out), (dv_in, dv_out))):
+            staged[part, slot] = (total[head] + terms[part]).astype(jnp.bfloat16)
+            store = pltpu.make_async_copy(
+                staged.at[part, slot], result.at[head], sems.at[part, slot]
+            )
+            stores.append((found >= 0, store))
+    for wanted, store in stores:
+        pl.when(wanted)(store.start)
+    for wanted, store in stores:
+        pl.when(wanted)(store.wait)
 
 
 def closing_kernel(count, cap, table_ref, terms, dk_in, dv_in, *rest):
     _, _, dk_out, dv_out, staged, sems = rest
     table = Table(table_ref, dk_in.shape[0], count, cap)
-    early = cap - terms.shape[1]
-    copies = []
-    for slot in range(cap):
-        found = table_ref[table.owner_at(0, slot)]
+    returned = terms.shape[1]
+    stores = []
+    for number in range(returned):
+        found = table_ref[table.owner_at(0, cap - returned + number)]
         head = jnp.maximum(found, 0)
         for part, (total, result) in enumerate(((dk_in, dk_out), (dv_in, dv_out))):
-            value = total[head]
-            if slot >= early:
-                value = value + terms[part, slot - early].astype(jnp.float32)
-            staged[part, slot] = value.astype(jnp.bfloat16)
-            copy = pltpu.make_async_copy(
-                staged.at[part, slot], result.at[head], sems.at[part, slot]
+            term = terms[part, number].astype(jnp.float32)
+            staged[part, number] = (total[head] + term).astype(jnp.bfloat16)
+            store = pltpu.make_async_copy(
+                staged.at[part, number], result.at[head], sems.at[part, number]
             )
-            copies.append((found >= 0, copy))
-    for wanted, copy in copies:
-        pl.when(wanted)(copy.start)
-    for wanted, copy in copies:
-        pl.when(wanted)(copy.wait)
+            stores.append((found >= 0, store))
+    for wanted, store in stores:
+        pl.when(wanted)(store.start)
+    for wanted, store in stores:
+        pl.when(wanted)(store.wait)
 
 
 def per_device(queries, keys, values, out_grad, tile_lists):
@@ -527,26 +534,24 @@
         results += stored_now
     *results, key_grad, value_grad = results
     first, key_sum = lax.optimization_barrier((arrived[0], key_sum))
-    key_sum, value_sum = pl.pallas_call(
+    key_grad, value_grad = pl.pallas_call(
         functools.partial(first_owner_kernel, count, cap, scale),
-        out_shape=[whole_sum] * 2,
-        in_specs=[smem] + [vmem] * 6,
-        out_specs=[vmem] * 2,
-        input_output_aliases={5: 0, 6: 1},
+        out_shape=[whole] * 2,
+        in_specs=[smem] + [vmem] * 6 + [anywhere] * 2,
+        out_specs=[anywhere] * 2,
+        scratch_shapes=[packed, pltpu.SemaphoreType.DMA((2, cap))],
+        input_output_aliases={7: 0, 8: 1},
         compiler_params=params,
         cost_estimate=brief,
         name="first_owner",
-    )(table, keys, values, first, stats[0], key_sum, value_sum)
-    terms, key_sum = lax.optimization_barrier((terms, key_sum))
+    )(table, keys, values, first, stats[0], key_sum, value_sum, key_grad, value_grad)
+    terms, key_grad = lax.optimization_barrier((terms, key_grad))
     key_grad, value_grad = pl.pallas_call(
         functools.partial(closing_kernel, count, cap),
         out_shape=[whole] * 2,
         in_specs=[smem] + [vmem] * 3 + [anywhere] * 2,
         out_specs=[anywhere] * 2,
-        scratch_shapes=[
-            pltpu.VMEM((2, cap, tokens, width), jnp.bfloat16),
-            pltpu.SemaphoreType.DMA((2, cap)),
-        ],
+        scratch_shapes=[packed, pltpu.SemaphoreType.DMA((2, cap))],
         input_output_aliases={4: 0, 5: 1},
         compiler_params=params,
         cost_estimate=brief,

time: 40.1 us -> 40 us (level)
  waiting for transfers between devices: 9.7 us -> 8.62 us
  Pallas kernels: 11.7 us -> 12.3 us
    ppermute x7, waiting for transfers between devices: 9.7 us -> 8.62 us  [swapped(): return lax.ppermute(block, 'seq', swap_route(channel, lax.axis_size('seq')))]
    pallas_call x1, Pallas kernels: 0.6 us -> 1.35 us  [per_device(): pl.pallas_call(functools.partial(first_owner_kernel, count, cap, scale),...]
    ppermute x7, starting transfers between devices: 17.5 us -> 17.9 us  [swapped(): return lax.ppermute(block, 'seq', swap_route(channel, lax.axis_size('seq')))]
  transfers between devices with their start and end apart: 7 -> 7, of which waited for: 3 -> 4; matrix products, arithmetic and copies ran while one was open for 0% -> 0% of each run, Pallas kernels for 24% -> 26%
where the time goes in v6:
time: 40 us; the launch traced here: 39.6 us
  starting transfers between devices  17.9 us (45%)
  Pallas kernels  12.3 us (31%)
  waiting for transfers between devices  8.62 us (22%)
  between operations  0.76 us (2%)
    ppermute x7, starting transfers between devices, swapped(): return lax.ppermute(block, 'seq', swap_route(channel, lax.axis_size('seq')))  17.9 us
    ppermute x7, waiting for transfers between devices, swapped(): return lax.ppermute(block, 'seq', swap_route(channel, lax.axis_size('seq')))  8.62 us
    pallas_call x1, Pallas kernels, per_device(): pl.pallas_call(functools.partial(own_kernel, count, cap, scale), grid=(he...  4.18 us
    pallas_call x1, Pallas kernels, per_device(): pl.pallas_call(functools.partial(owner_kernel, count, cap, scale, number)...  2 us
    pallas_call x1, Pallas kernels, per_device(): pl.pallas_call(functools.partial(reader_kernel, count, cap, scale), out_s...  1.53 us
    pallas_call x1, Pallas kernels, per_device(): pl.pallas_call(functools.partial(first_owner_kernel, count, cap, scale),...  1.35 us
    pallas_call x1, Pallas kernels, per_device(): pl.pallas_call(functools.partial(pack_keys_kernel, cap, channels[0]), out...  1.34 us
    pallas_call x1, Pallas kernels, per_device(): pl.pallas_call(functools.partial(statistics_kernel, count, cap, scale), o...  0.89 us
  transfers between devices with their start and end apart: 7, of which 4 were waited for; matrix products, arithmetic and copies ran while one was open for 0% of the time, Pallas kernels for 26%

profile of v6, /device:TPU:0, one launch (start us, length us, event | category | flops | bytes accessed | tf_op | source)
XLA Modules:
  0.0 39.6 jit_solution(16538406973648240045)
XLA Ops:
  0.6 1.3 %pack_keys.1 = (bf16[2,3,256,128]{3,2,1,0:T(8,128)(2,1)S(1)}, s32[6,4,8]{2,1,0:T(4,128)S(4)}, bf16[6,256,128]{2,1,0:T(8,128)(2,1)S(1)}, bf16[6,256,128]{2,1,0:T(8,128)(2,1)S(1)}) custom-call(s32[6,4,8]{2,1,0:T(4,128)} %bitcast.1, bf16[6,256,128]{2,1,0:T(8,128)(2,1)} %keys.1, bf16[6,256,128]{2,1,0:T(8,128)(2,1)} %values.1), custom_call_target="tpu_custom_call" | custom-call | flops 1 | bytes 1 | tf_op jit(solution)/shard_map/pack_keys/pallas_call | solution.py:412
  2.0 3.0 %collective-permute-start = (bf16[2,3,256,128]{3,2,1,0:T(8,128)(2,1)S(1)}, bf16[2,3,256,128]{3,2,1,0:T(8,128)(2,1)S(1)}, u32[]{:S(2)}, u32[]{:S(2)}) collective-permute-start(bf16[2,3,256,128]{3,2,1,0:T(8,128)(2,1)S(1)} %get-tuple-element.43), channel_id=1, source_target_pairs={{0,2},{2,0},{4,6},{6,4},{8,10},{10,8},{12,14},{14,12},{1,3},{3,1},... | collective-permute-start | bytes 1179656 | tf_op jit(solution)/shard_map/ppermute | solution.py:37
  5.0 0.1 pack_more_keys.1
  5.1 0.8 %collective-permute-start.2 = (bf16[2,3,256,128]{3,2,1,0:T(8,128)(2,1)S(1)}, bf16[2,3,256,128]{3,2,1,0:T(8,128)(2,1)S(1)}, u32[]{:S(2)}, u32[]{:S(2)}) collective-permute-start(bf16[2,3,256,128]{3,2,1,0:T(8,128)(2,1)S(1)} %pack_more_keys.1), channel_id=1, source_target_pairs={{2,4},{4,2},{6,8},{8,6},{10,12},{12,10},{3,5},{5,3},{7,9},{9,7},{1... | collective-permute-start | bytes 1179656 | tf_op jit(solution)/shard_map/ppermute | solution.py:37
  5.9 4.2 %own_scores.1 = (f32[6,256,256]{2,1,0:T(8,128)S(1)}, f32[6,256,256]{2,1,0:T(8,128)S(1)}, f32[6,3,256]{2,1,0:T(4,128)S(1)}, bf16[2,2,256,128]{3,2,1,0:T(8,128)(2,1)S(1)}, bf16[2,3,256,128]{3,2,1,0:T(8,128)(2,1)S(1)}) custom-call(s32[24]{0:T(128)S(4)} %table.1.table_ref, bf16[6,256,128]{2,1,0:T(8,128)(2,1)} %q_ref.7, ...), custom_call_target="tpu_custom_call" | custom-call | flops 1 | bytes 1 | tf_op jit(solution)/shard_map/own_scores/pallas_call | solution.py:447
  10.1 4.8 %collective-permute-start.5 = (bf16[2,2,256,128]{3,2,1,0:T(8,128)(2,1)S(1)}, bf16[2,2,256,128]{3,2,1,0:T(8,128)(2,1)S(1)}, u32[]{:S(2)}, u32[]{:S(2)}) collective-permute-start(bf16[2,2,256,128]{3,2,1,0:T(8,128)(2,1)S(1)} %get-tuple-element.60), channel_id=1, source_target_pairs={{0,2},{2,0},{4,6},{6,4},{8,10},{10,8},{12,14},{14,12},{1,3},{3,1},... | collective-permute-start | bytes 786440 | tf_op jit(solution)/shard_map/ppermute | solution.py:37
  14.8 8.1 %collective-permute-done.rest_0_.rest_6_ = bf16[2,3,256,128]{3,2,1,0:T(8,128)(2,1)S(1)} collective-permute-done((bf16[2,3,256,128]{3,2,1,0:T(8,128)(2,1)S(1)}, bf16[2,3,256,128]{3,2,1,0:T(8,128)(2,1)S(1)}, u32[]{:S(2)}, u32[]{:S(2)}) %collective-permute-start) | collective-permute-done | bytes 393248 | tf_op jit(solution)/shard_map/ppermute | solution.py:37
  22.9 0.7 %collective-permute-start.1 = (bf16[2,3,256,128]{3,2,1,0:T(8,128)(2,1)S(1)}, bf16[2,3,256,128]{3,2,1,0:T(8,128)(2,1)S(1)}, u32[]{:S(2)}, u32[]{:S(2)}) collective-permute-start(bf16[2,3,256,128]{3,2,1,0:T(8,128)(2,1)S(1)} %get-tuple-element.44), channel_id=1, source_target_pairs={{2,4},{4,2},{6,8},{8,6},{10,12},{12,10},{3,5},{5,3},{7,9},{9,7},{1... | collective-permute-start | bytes 1179656 | tf_op jit(solution)/shard_map/ppermute | solution.py:37
  23.6 0.0 collective-permute-done.2.rest_1_.rest_7_
  23.6 0.0 copy-done
  23.6 0.9 %statistics.1 = (f32[6,256,256]{2,1,0:T(8,128)S(1)}, f32[6,256,256]{2,1,0:T(8,128)S(1)}, f32[6,2,256]{2,1,0:T(2,128)S(1)}, f32[6,2,256]{2,1,0:T(2,128)S(1)}, f32...) custom-call(s32[24]{0:T(128)S(4)} %table.1.table_ref, bf16[6,256,128]{2,1,0:T(8,128)(2,1)S(1)} %copy-done, ...), custom_call_target="tpu_custom_call" | custom-call | flops 1 | bytes 1 | tf_op jit(solution)/shard_map/statistics/pallas_call | solution.py:462
  24.5 0.7 %collective-permute-start.3 = (f32[3,2,256]{2,1,0:T(2,128)S(1)}, f32[3,2,256]{2,1,0:T(2,128)S(1)}, u32[]{:S(2)}, u32[]{:S(2)}) collective-permute-start(f32[3,2,256]{2,1,0:T(2,128)S(1)} %get-tuple-element.47), channel_id=1, source_target_pairs={{2,4},{4,2},{6,8},{8,6},{10,12},{12,10},{3,5},{5,3},{7,9},{9,7},{1... | collective-permute-start | bytes 18440 | tf_op jit(solution)/shard_map/ppermute | solution.py:37
  25.2 7.9 %collective-permute-start.6 = (f32[3,2,256]{2,1,0:T(2,128)S(1)}, f32[3,2,256]{2,1,0:T(2,128)S(1)}, u32[]{:S(2)}, u32[]{:S(2)}) collective-permute-start(f32[3,2,256]{2,1,0:T(2,128)S(1)} %get-tuple-element.63), channel_id=1, source_target_pairs={{0,2},{2,0},{4,6},{6,4},{8,10},{10,8},{12,14},{14,12},{1,3},{3,1},... | collective-permute-start | bytes 18440 | tf_op jit(solution)/shard_map/ppermute | solution.py:37
  33.1 0.2 returned.1
  33.4 0.1 collective-permute-start.4
  33.5 1.5 %reader.1 = (bf16[6,256,128]{2,1,0:T(8,128)(2,1)S(1)}, bf16[6,256,128]{2,1,0:T(8,128)(2,1)S(1)}, f32[6,256,128]{2,1,0:T(8,128)S(1)}, f32[6,256,128]{2,1,0:T(8,128)S(1)}) custom-call(s32[24]{0:T(128)S(4)} %table.1.table_ref, bf16[6,256,128]{2,1,0:T(8,128)(2,1)S(1)} %copy-done, bf16[6,256,128]{2,1,0:T(8,128)(2,1)S(1)} %get-tuple-element.40.k_ref.keys, ...), custom_call_target="tpu_custom_call" | custom-call | flops 99999997952 | bytes 1 | tf_op jit(solution)/shard_map/reader/pallas_call | solution.py:487
  35.0 0.0 collective-permute-done.3.stats
  35.0 0.0 collective-permute-done.1.arrived
  35.0 2.0 %owner.1 = (bf16[6,256,128]{2,1,0:T(8,128)(2,1)}, bf16[6,256,128]{2,1,0:T(8,128)(2,1)}, bf16[6,256,128]{2,1,0:T(8,128)(2,1)}, bf16[6,256,128]{2,1,0:T(8,128)(2,1...) custom-call(s32[24]{0:T(128)S(4)} %table.1.table_ref, ...), custom_call_target="tpu_custom_call", output_to_operand_aliasing={{4}: (5, {}), {5}: (6, {})} | custom-call | flops 1 | bytes 1 | tf_op jit(solution)/shard_map/owner/pallas_call | solution.py:514
  37.0 0.1 collective-permute-done.5.arrived
  37.1 0.1 collective-permute-done.6.stats
  37.2 1.3 %first_owner.1 = (bf16[6,256,128]{2,1,0:T(8,128)(2,1)}, bf16[6,256,128]{2,1,0:T(8,128)(2,1)}) custom-call(s32[24]{0:T(128)S(4)} %table.1.table_ref, bf16[6,256,128]{2,1,0:T(8,128)(2,1)S(1)} %get-tuple-element.40.k_ref.keys, bf16[6,256,128]{2,1,0:T(8,128)(2,1)S(1)} %get-tuple-element.41.v_ref.values, ...), custom_call_target="tpu_custom_call", output_to_operand_aliasing={{0}: (7, {}), {1}: (8, {})} | custom-call | flops 1 | bytes 1 | tf_op jit(solution)/shard_map/first_owner/pallas_call | solution.py:537
  38.6 0.3 collective-permute-done.4.terms
  38.9 0.7 %closing.1 = (bf16[6,256,128]{2,1,0:T(8,128)(2,1)}, bf16[6,256,128]{2,1,0:T(8,128)(2,1)}) custom-call(s32[24]{0:T(128)S(4)} %table.1.table_ref, bf16[2,1,256,128]{3,2,1,0:T(8,128)(2,1)S(1)} %collective-permute-done.4.terms, f32[6,256,128]{2,1,0:T(8,128)S(1)} %get-tuple-element.64.rest_0_.dk_in, ...), custom_call_target="tpu_custom_call", output_to_operand_aliasing={{0}: (4, {}), {1}: (5, {})} | custom-call | flops 1 | bytes 1 | tf_op jit(solution)/shard_map/closing/pallas_call | solution.py:549
  (4 shorter events, 0.0 us)
Async XLA Ops:
  2.0 21.0 %collective-permute-start = (bf16[2,3,256,128]{3,2,1,0:T(8,128)(2,1)S(1)}, bf16[2,3,256,128]{3,2,1,0:T(8,128)(2,1)S(1)}, u32[]{:S(2)}, u32[]{:S(2)}) collective-permute-start(bf16[2,3,256,128]{3,2,1,0:T(8,128)(2,1)S(1)} %get-tuple-element.43), channel_id=1, source_target_pairs={{0,2},{2,0},{4,6},{6,4},{8,10},{10,8},{12,14},{14,12},{1,3},{3,1},... | collective-permute-start | bytes 1179656 | tf_op jit(solution)/shard_map/ppermute | solution.py:37
  5.0 18.6 %copy-start = (bf16[6,256,128]{2,1,0:T(8,128)(2,1)S(1)}, bf16[6,256,128]{2,1,0:T(8,128)(2,1)}, u32[]{:S(2)}) copy-start(bf16[6,256,128]{2,1,0:T(8,128)(2,1)} %q_ref.7) | copy-start | bytes 1179652
  5.0 18.6 %copy-start.1 = (bf16[6,256,128]{2,1,0:T(8,128)(2,1)S(1)}, bf16[6,256,128]{2,1,0:T(8,128)(2,1)}, u32[]{:S(2)}) copy-start(bf16[6,256,128]{2,1,0:T(8,128)(2,1)} %g_ref.7) | copy-start | bytes 1179652
  5.1 18.6 %collective-permute-start.2 = (bf16[2,3,256,128]{3,2,1,0:T(8,128)(2,1)S(1)}, bf16[2,3,256,128]{3,2,1,0:T(8,128)(2,1)S(1)}, u32[]{:S(2)}, u32[]{:S(2)}) collective-permute-start(bf16[2,3,256,128]{3,2,1,0:T(8,128)(2,1)S(1)} %pack_more_keys.1), channel_id=1, source_target_pairs={{2,4},{4,2},{6,8},{8,6},{10,12},{12,10},{3,5},{5,3},{7,9},{9,7},{1... | collective-permute-start | bytes 1179656 | tf_op jit(solution)/shard_map/ppermute | solution.py:37
  10.1 27.0 %collective-permute-start.5 = (bf16[2,2,256,128]{3,2,1,0:T(8,128)(2,1)S(1)}, bf16[2,2,256,128]{3,2,1,0:T(8,128)(2,1)S(1)}, u32[]{:S(2)}, u32[]{:S(2)}) collective-permute-start(bf16[2,2,256,128]{3,2,1,0:T(8,128)(2,1)S(1)} %get-tuple-element.60), channel_id=1, source_target_pairs={{0,2},{2,0},{4,6},{6,4},{8,10},{10,8},{12,14},{14,12},{1,3},{3,1},... | collective-permute-start | bytes 786440 | tf_op jit(solution)/shard_map/ppermute | solution.py:37
  22.9 12.1 %collective-permute-start.1 = (bf16[2,3,256,128]{3,2,1,0:T(8,128)(2,1)S(1)}, bf16[2,3,256,128]{3,2,1,0:T(8,128)(2,1)S(1)}, u32[]{:S(2)}, u32[]{:S(2)}) collective-permute-start(bf16[2,3,256,128]{3,2,1,0:T(8,128)(2,1)S(1)} %get-tuple-element.44), channel_id=1, source_target_pairs={{2,4},{4,2},{6,8},{8,6},{10,12},{12,10},{3,5},{5,3},{7,9},{9,7},{1... | collective-permute-start | bytes 1179656 | tf_op jit(solution)/shard_map/ppermute | solution.py:37
  24.5 10.5 %collective-permute-start.3 = (f32[3,2,256]{2,1,0:T(2,128)S(1)}, f32[3,2,256]{2,1,0:T(2,128)S(1)}, u32[]{:S(2)}, u32[]{:S(2)}) collective-permute-start(f32[3,2,256]{2,1,0:T(2,128)S(1)} %get-tuple-element.47), channel_id=1, source_target_pairs={{2,4},{4,2},{6,8},{8,6},{10,12},{12,10},{3,5},{5,3},{7,9},{9,7},{1... | collective-permute-start | bytes 18440 | tf_op jit(solution)/shard_map/ppermute | solution.py:37
  25.2 12.0 %collective-permute-start.6 = (f32[3,2,256]{2,1,0:T(2,128)S(1)}, f32[3,2,256]{2,1,0:T(2,128)S(1)}, u32[]{:S(2)}, u32[]{:S(2)}) collective-permute-start(f32[3,2,256]{2,1,0:T(2,128)S(1)} %get-tuple-element.63), channel_id=1, source_target_pairs={{0,2},{2,0},{4,6},{6,4},{8,10},{10,8},{12,14},{14,12},{1,3},{3,1},... | collective-permute-start | bytes 18440 | tf_op jit(solution)/shard_map/ppermute | solution.py:37
  33.4 5.5 %collective-permute-start.4 = (bf16[2,1,256,128]{3,2,1,0:T(8,128)(2,1)S(1)}, bf16[2,1,256,128]{3,2,1,0:T(8,128)(2,1)S(1)}, u32[]{:S(2)}, u32[]{:S(2)}) collective-permute-start(bf16[2,1,256,128]{3,2,1,0:T(8,128)(2,1)S(1)} %returned.1), channel_id=1, source_target_pairs={{0,2},{2,0},{4,6},{6,4},{8,10},{10,8},{12,14},{14,12},{1,3},{3,1},... | collective-permute-start | bytes 393224 | tf_op jit(solution)/shard_map/ppermute | solution.py:37

commit v7 on v6

--- a/solution.py
+++ b/solution.py
@@ -303,6 +303,9 @@
     heads = k_ref.shape[0]
     table = Table(table_ref, heads, count, cap)
     closing = number == 1
+    for total, given in zip((dk_sum, dv_sum), rest):
+        for head in range(heads):
+            total[head] = given[head]
     results = rest[2:]
     if closing:
         *results, dk_out, dv_out = results
@@ -517,7 +520,6 @@
             in_specs=[smem] + [vmem] * (6 + stored),
             out_specs=[anywhere] * outputs + [vmem] * 2,
             scratch_shapes=[whole_pair, copies_whole, copies_whole],
-            input_output_aliases={5: outputs, 6: outputs + 1},
             compiler_params=params,
             cost_estimate=brief,
             name="owner",

time: 40 us -> 40 us (level)
  no operation moved by 1% of the time
where the time goes in v7:
time: 40 us; the launch traced here: 39.6 us
  starting transfers between devices  17.7 us (44%)
  Pallas kernels  12.2 us (30%)
  waiting for transfers between devices  8.9 us (22%)
  between operations  0.76 us (2%)
    ppermute x7, starting transfers between devices, swapped(): return lax.ppermute(block, 'seq', swap_route(channel, lax.axis_size('seq')))  17.7 us
    ppermute x7, waiting for transfers between devices, swapped(): return lax.ppermute(block, 'seq', swap_route(channel, lax.axis_size('seq')))  8.9 us
    pallas_call x1, Pallas kernels, per_device(): pl.pallas_call(functools.partial(own_kernel, count, cap, scale), grid=(he...  4.2 us
    pallas_call x1, Pallas kernels, per_device(): pl.pallas_call(functools.partial(owner_kernel, count, cap, scale, number)...  1.9 us
    pallas_call x1, Pallas kernels, per_device(): pl.pallas_call(functools.partial(reader_kernel, count, cap, scale), out_s...  1.53 us
    pallas_call x1, Pallas kernels, per_device(): pl.pallas_call(functools.partial(first_owner_kernel, count, cap, scale),...  1.35 us
    pallas_call x1, Pallas kernels, per_device(): pl.pallas_call(functools.partial(pack_keys_kernel, cap, channels[0]), out...  1.34 us
    pallas_call x1, Pallas kernels, per_device(): pl.pallas_call(functools.partial(statistics_kernel, count, cap, scale), o...  0.89 us
  transfers between devices with their start and end apart: 7, of which 4 were waited for; matrix products, arithmetic and copies ran while one was open for 0% of the time, Pallas kernels for 26%

profile of v7, /device:TPU:0, one launch (start us, length us, event | category | flops | bytes accessed | tf_op | source)
XLA Modules:
  0.0 39.6 jit_solution(4017216548632446909)
XLA Ops:
  0.6 1.3 %pack_keys.1 = (bf16[2,3,256,128]{3,2,1,0:T(8,128)(2,1)S(1)}, s32[6,4,8]{2,1,0:T(4,128)S(4)}, bf16[6,256,128]{2,1,0:T(8,128)(2,1)S(1)}, bf16[6,256,128]{2,1,0:T(8,128)(2,1)S(1)}) custom-call(s32[6,4,8]{2,1,0:T(4,128)} %bitcast.1, bf16[6,256,128]{2,1,0:T(8,128)(2,1)} %keys.1, bf16[6,256,128]{2,1,0:T(8,128)(2,1)} %values.1), custom_call_target="tpu_custom_call" | custom-call | flops 1 | bytes 1 | tf_op jit(solution)/shard_map/pack_keys/pallas_call | solution.py:415
  2.0 3.0 %collective-permute-start = (bf16[2,3,256,128]{3,2,1,0:T(8,128)(2,1)S(1)}, bf16[2,3,256,128]{3,2,1,0:T(8,128)(2,1)S(1)}, u32[]{:S(2)}, u32[]{:S(2)}) collective-permute-start(bf16[2,3,256,128]{3,2,1,0:T(8,128)(2,1)S(1)} %get-tuple-element.43), channel_id=1, source_target_pairs={{0,2},{2,0},{4,6},{6,4},{8,10},{10,8},{12,14},{14,12},{1,3},{3,1},... | collective-permute-start | bytes 1179656 | tf_op jit(solution)/shard_map/ppermute | solution.py:37
  5.0 0.1 pack_more_keys.1
  5.1 0.8 %collective-permute-start.2 = (bf16[2,3,256,128]{3,2,1,0:T(8,128)(2,1)S(1)}, bf16[2,3,256,128]{3,2,1,0:T(8,128)(2,1)S(1)}, u32[]{:S(2)}, u32[]{:S(2)}) collective-permute-start(bf16[2,3,256,128]{3,2,1,0:T(8,128)(2,1)S(1)} %pack_more_keys.1), channel_id=1, source_target_pairs={{2,4},{4,2},{6,8},{8,6},{10,12},{12,10},{3,5},{5,3},{7,9},{9,7},{1... | collective-permute-start | bytes 1179656 | tf_op jit(solution)/shard_map/ppermute | solution.py:37
  5.9 4.2 %own_scores.1 = (f32[6,256,256]{2,1,0:T(8,128)S(1)}, f32[6,256,256]{2,1,0:T(8,128)S(1)}, f32[6,3,256]{2,1,0:T(4,128)S(1)}, bf16[2,2,256,128]{3,2,1,0:T(8,128)(2,1)S(1)}, bf16[2,3,256,128]{3,2,1,0:T(8,128)(2,1)S(1)}) custom-call(s32[24]{0:T(128)S(4)} %table.1.table_ref, bf16[6,256,128]{2,1,0:T(8,128)(2,1)} %q_ref.7, ...), custom_call_target="tpu_custom_call" | custom-call | flops 1 | bytes 1 | tf_op jit(solution)/shard_map/own_scores/pallas_call | solution.py:450
  10.1 4.6 %collective-permute-start.5 = (bf16[2,2,256,128]{3,2,1,0:T(8,128)(2,1)S(1)}, bf16[2,2,256,128]{3,2,1,0:T(8,128)(2,1)S(1)}, u32[]{:S(2)}, u32[]{:S(2)}) collective-permute-start(bf16[2,2,256,128]{3,2,1,0:T(8,128)(2,1)S(1)} %get-tuple-element.60), channel_id=1, source_target_pairs={{0,2},{2,0},{4,6},{6,4},{8,10},{10,8},{12,14},{14,12},{1,3},{3,1},... | collective-permute-start | bytes 786440 | tf_op jit(solution)/shard_map/ppermute | solution.py:37
  14.6 8.3 %collective-permute-done.rest_0_.rest_6_ = bf16[2,3,256,128]{3,2,1,0:T(8,128)(2,1)S(1)} collective-permute-done((bf16[2,3,256,128]{3,2,1,0:T(8,128)(2,1)S(1)}, bf16[2,3,256,128]{3,2,1,0:T(8,128)(2,1)S(1)}, u32[]{:S(2)}, u32[]{:S(2)}) %collective-permute-start) | collective-permute-done | bytes 393248 | tf_op jit(solution)/shard_map/ppermute | solution.py:37
  22.9 0.7 %collective-permute-start.1 = (bf16[2,3,256,128]{3,2,1,0:T(8,128)(2,1)S(1)}, bf16[2,3,256,128]{3,2,1,0:T(8,128)(2,1)S(1)}, u32[]{:S(2)}, u32[]{:S(2)}) collective-permute-start(bf16[2,3,256,128]{3,2,1,0:T(8,128)(2,1)S(1)} %get-tuple-element.44), channel_id=1, source_target_pairs={{2,4},{4,2},{6,8},{8,6},{10,12},{12,10},{3,5},{5,3},{7,9},{9,7},{1... | collective-permute-start | bytes 1179656 | tf_op jit(solution)/shard_map/ppermute | solution.py:37
  23.6 0.0 collective-permute-done.2.rest_1_.rest_7_
  23.6 0.0 copy-done
  23.6 0.9 %statistics.1 = (f32[6,256,256]{2,1,0:T(8,128)S(1)}, f32[6,256,256]{2,1,0:T(8,128)S(1)}, f32[6,2,256]{2,1,0:T(2,128)S(1)}, f32[6,2,256]{2,1,0:T(2,128)S(1)}, f32...) custom-call(s32[24]{0:T(128)S(4)} %table.1.table_ref, bf16[6,256,128]{2,1,0:T(8,128)(2,1)S(1)} %copy-done, ...), custom_call_target="tpu_custom_call" | custom-call | flops 1 | bytes 1 | tf_op jit(solution)/shard_map/statistics/pallas_call | solution.py:465
  24.5 0.7 %collective-permute-start.3 = (f32[3,2,256]{2,1,0:T(2,128)S(1)}, f32[3,2,256]{2,1,0:T(2,128)S(1)}, u32[]{:S(2)}, u32[]{:S(2)}) collective-permute-start(f32[3,2,256]{2,1,0:T(2,128)S(1)} %get-tuple-element.47), channel_id=1, source_target_pairs={{2,4},{4,2},{6,8},{8,6},{10,12},{12,10},{3,5},{5,3},{7,9},{9,7},{1... | collective-permute-start | bytes 18440 | tf_op jit(solution)/shard_map/ppermute | solution.py:37
  25.2 7.9 %collective-permute-start.6 = (f32[3,2,256]{2,1,0:T(2,128)S(1)}, f32[3,2,256]{2,1,0:T(2,128)S(1)}, u32[]{:S(2)}, u32[]{:S(2)}) collective-permute-start(f32[3,2,256]{2,1,0:T(2,128)S(1)} %get-tuple-element.63), channel_id=1, source_target_pairs={{0,2},{2,0},{4,6},{6,4},{8,10},{10,8},{12,14},{14,12},{1,3},{3,1},... | collective-permute-start | bytes 18440 | tf_op jit(solution)/shard_map/ppermute | solution.py:37
  33.2 0.2 returned.1
  33.4 0.1 collective-permute-start.4
  33.5 1.5 %reader.1 = (bf16[6,256,128]{2,1,0:T(8,128)(2,1)S(1)}, bf16[6,256,128]{2,1,0:T(8,128)(2,1)S(1)}, f32[6,256,128]{2,1,0:T(8,128)S(1)}, f32[6,256,128]{2,1,0:T(8,128)S(1)}) custom-call(s32[24]{0:T(128)S(4)} %table.1.table_ref, bf16[6,256,128]{2,1,0:T(8,128)(2,1)S(1)} %copy-done, bf16[6,256,128]{2,1,0:T(8,128)(2,1)S(1)} %get-tuple-element.40.k_ref.keys, ...), custom_call_target="tpu_custom_call" | custom-call | flops 99999997952 | bytes 1 | tf_op jit(solution)/shard_map/reader/pallas_call | solution.py:490
  35.0 0.0 collective-permute-done.3.stats
  35.0 0.0 collective-permute-done.1.arrived
  35.0 1.9 %owner.1 = (bf16[6,256,128]{2,1,0:T(8,128)(2,1)}, bf16[6,256,128]{2,1,0:T(8,128)(2,1)}, bf16[6,256,128]{2,1,0:T(8,128)(2,1)}, bf16[6,256,128]{2,1,0:T(8,128)(2,1...) custom-call(s32[24]{0:T(128)S(4)} %table.1.table_ref, bf16[6,256,128]{2,1,0:T(8,128)(2,1)S(1)} %get-tuple-element.40.k_ref.keys, ...), custom_call_target="tpu_custom_call" | custom-call | flops 1 | bytes 1 | tf_op jit(solution)/shard_map/owner/pallas_call | solution.py:517
  36.9 0.2 collective-permute-done.5.arrived
  37.1 0.1 collective-permute-done.6.stats
  37.2 1.3 %first_owner.1 = (bf16[6,256,128]{2,1,0:T(8,128)(2,1)}, bf16[6,256,128]{2,1,0:T(8,128)(2,1)}) custom-call(s32[24]{0:T(128)S(4)} %table.1.table_ref, bf16[6,256,128]{2,1,0:T(8,128)(2,1)S(1)} %get-tuple-element.40.k_ref.keys, bf16[6,256,128]{2,1,0:T(8,128)(2,1)S(1)} %get-tuple-element.41.v_ref.values, ...), custom_call_target="tpu_custom_call", output_to_operand_aliasing={{0}: (7, {}), {1}: (8, {})} | custom-call | flops 1 | bytes 1 | tf_op jit(solution)/shard_map/first_owner/pallas_call | solution.py:539
  38.6 0.3 collective-permute-done.4.terms
  38.9 0.7 %closing.1 = (bf16[6,256,128]{2,1,0:T(8,128)(2,1)}, bf16[6,256,128]{2,1,0:T(8,128)(2,1)}) custom-call(s32[24]{0:T(128)S(4)} %table.1.table_ref, bf16[2,1,256,128]{3,2,1,0:T(8,128)(2,1)S(1)} %collective-permute-done.4.terms, f32[6,256,128]{2,1,0:T(8,128)S(1)} %get-tuple-element.64.rest_0_.dk_in, ...), custom_call_target="tpu_custom_call", output_to_operand_aliasing={{0}: (4, {}), {1}: (5, {})} | custom-call | flops 1 | bytes 1 | tf_op jit(solution)/shard_map/closing/pallas_call | solution.py:551
  (4 shorter events, 0.0 us)
Async XLA Ops:
  2.0 21.0 %collective-permute-start = (bf16[2,3,256,128]{3,2,1,0:T(8,128)(2,1)S(1)}, bf16[2,3,256,128]{3,2,1,0:T(8,128)(2,1)S(1)}, u32[]{:S(2)}, u32[]{:S(2)}) collective-permute-start(bf16[2,3,256,128]{3,2,1,0:T(8,128)(2,1)S(1)} %get-tuple-element.43), channel_id=1, source_target_pairs={{0,2},{2,0},{4,6},{6,4},{8,10},{10,8},{12,14},{14,12},{1,3},{3,1},... | collective-permute-start | bytes 1179656 | tf_op jit(solution)/shard_map/ppermute | solution.py:37
  5.0 18.6 %copy-start = (bf16[6,256,128]{2,1,0:T(8,128)(2,1)S(1)}, bf16[6,256,128]{2,1,0:T(8,128)(2,1)}, u32[]{:S(2)}) copy-start(bf16[6,256,128]{2,1,0:T(8,128)(2,1)} %q_ref.7) | copy-start | bytes 1179652
  5.0 18.6 %copy-start.1 = (bf16[6,256,128]{2,1,0:T(8,128)(2,1)S(1)}, bf16[6,256,128]{2,1,0:T(8,128)(2,1)}, u32[]{:S(2)}) copy-start(bf16[6,256,128]{2,1,0:T(8,128)(2,1)} %g_ref.7) | copy-start | bytes 1179652
  5.1 18.6 %collective-permute-start.2 = (bf16[2,3,256,128]{3,2,1,0:T(8,128)(2,1)S(1)}, bf16[2,3,256,128]{3,2,1,0:T(8,128)(2,1)S(1)}, u32[]{:S(2)}, u32[]{:S(2)}) collective-permute-start(bf16[2,3,256,128]{3,2,1,0:T(8,128)(2,1)S(1)} %pack_more_keys.1), channel_id=1, source_target_pairs={{2,4},{4,2},{6,8},{8,6},{10,12},{12,10},{3,5},{5,3},{7,9},{9,7},{1... | collective-permute-start | bytes 1179656 | tf_op jit(solution)/shard_map/ppermute | solution.py:37
  10.1 27.0 %collective-permute-start.5 = (bf16[2,2,256,128]{3,2,1,0:T(8,128)(2,1)S(1)}, bf16[2,2,256,128]{3,2,1,0:T(8,128)(2,1)S(1)}, u32[]{:S(2)}, u32[]{:S(2)}) collective-permute-start(bf16[2,2,256,128]{3,2,1,0:T(8,128)(2,1)S(1)} %get-tuple-element.60), channel_id=1, source_target_pairs={{0,2},{2,0},{4,6},{6,4},{8,10},{10,8},{12,14},{14,12},{1,3},{3,1},... | collective-permute-start | bytes 786440 | tf_op jit(solution)/shard_map/ppermute | solution.py:37
  22.9 12.1 %collective-permute-start.1 = (bf16[2,3,256,128]{3,2,1,0:T(8,128)(2,1)S(1)}, bf16[2,3,256,128]{3,2,1,0:T(8,128)(2,1)S(1)}, u32[]{:S(2)}, u32[]{:S(2)}) collective-permute-start(bf16[2,3,256,128]{3,2,1,0:T(8,128)(2,1)S(1)} %get-tuple-element.44), channel_id=1, source_target_pairs={{2,4},{4,2},{6,8},{8,6},{10,12},{12,10},{3,5},{5,3},{7,9},{9,7},{1... | collective-permute-start | bytes 1179656 | tf_op jit(solution)/shard_map/ppermute | solution.py:37
  24.5 10.5 %collective-permute-start.3 = (f32[3,2,256]{2,1,0:T(2,128)S(1)}, f32[3,2,256]{2,1,0:T(2,128)S(1)}, u32[]{:S(2)}, u32[]{:S(2)}) collective-permute-start(f32[3,2,256]{2,1,0:T(2,128)S(1)} %get-tuple-element.47), channel_id=1, source_target_pairs={{2,4},{4,2},{6,8},{8,6},{10,12},{12,10},{3,5},{5,3},{7,9},{9,7},{1... | collective-permute-start | bytes 18440 | tf_op jit(solution)/shard_map/ppermute | solution.py:37
  25.2 12.0 %collective-permute-start.6 = (f32[3,2,256]{2,1,0:T(2,128)S(1)}, f32[3,2,256]{2,1,0:T(2,128)S(1)}, u32[]{:S(2)}, u32[]{:S(2)}) collective-permute-start(f32[3,2,256]{2,1,0:T(2,128)S(1)} %get-tuple-element.63), channel_id=1, source_target_pairs={{0,2},{2,0},{4,6},{6,4},{8,10},{10,8},{12,14},{14,12},{1,3},{3,1},... | collective-permute-start | bytes 18440 | tf_op jit(solution)/shard_map/ppermute | solution.py:37
  33.4 5.5 %collective-permute-start.4 = (bf16[2,1,256,128]{3,2,1,0:T(8,128)(2,1)S(1)}, bf16[2,1,256,128]{3,2,1,0:T(8,128)(2,1)S(1)}, u32[]{:S(2)}, u32[]{:S(2)}) collective-permute-start(bf16[2,1,256,128]{3,2,1,0:T(8,128)(2,1)S(1)} %returned.1), channel_id=1, source_target_pairs={{0,2},{2,0},{4,6},{6,4},{8,10},{10,8},{12,14},{14,12},{1,3},{3,1},... | collective-permute-start | bytes 393224 | tf_op jit(solution)/shard_map/ppermute | solution.py:37

commit v8 on v6

--- a/solution.py
+++ b/solution.py
@@ -315,6 +315,9 @@
             )
     for copy in copies:
         copy.start()
+    for total, given in zip((dk_sum, dv_sum), rest):
+        for head in range(heads):
+            total[head] = given[head]
     for slot in range(cap):
         _, head, dk_term, dv_term = owner_terms(
             table, number, scale, k_ref, v_ref, arrived, stats, slot
@@ -517,7 +520,6 @@
             in_specs=[smem] + [vmem] * (6 + stored),
             out_specs=[anywhere] * outputs + [vmem] * 2,
             scratch_shapes=[whole_pair, copies_whole, copies_whole],
-            input_output_aliases={5: outputs, 6: outputs + 1},
             compiler_params=params,
             cost_estimate=brief,
             name="owner",

time: 40 us -> 39.6 us (0.990)
  Pallas kernels: 12.3 us -> 11.6 us
    pallas_call x1, Pallas kernels: 0.73 us -> 0.08 us  [per_device(): pl.pallas_call(functools.partial(closing_kernel, count, cap), out_shape=[...]
where the time goes in v8:
time: 39.6 us; the launch traced here: 39 us
  starting transfers between devices  17.9 us (45%)
  Pallas kernels  11.6 us (29%)
  waiting for transfers between devices  8.68 us (22%)
  between operations  0.76 us (2%)
    ppermute x7, starting transfers between devices, swapped(): return lax.ppermute(block, 'seq', swap_route(channel, lax.axis_size('seq')))  17.9 us
    ppermute x7, waiting for transfers between devices, swapped(): return lax.ppermute(block, 'seq', swap_route(channel, lax.axis_size('seq')))  8.68 us
    pallas_call x1, Pallas kernels, per_device(): pl.pallas_call(functools.partial(own_kernel, count, cap, scale), grid=(he...  4.2 us
    pallas_call x1, Pallas kernels, per_device(): pl.pallas_call(functools.partial(owner_kernel, count, cap, scale, number)...  1.94 us
    pallas_call x1, Pallas kernels, per_device(): pl.pallas_call(functools.partial(reader_kernel, count, cap, scale), out_s...  1.53 us
    pallas_call x1, Pallas kernels, per_device(): pl.pallas_call(functools.partial(first_owner_kernel, count, cap, scale),...  1.35 us
    pallas_call x1, Pallas kernels, per_device(): pl.pallas_call(functools.partial(pack_keys_kernel, cap, channels[0]), out...  1.34 us
    pallas_call x1, Pallas kernels, per_device(): pl.pallas_call(functools.partial(statistics_kernel, count, cap, scale), o...  0.89 us
  transfers between devices with their start and end apart: 7, of which 4 were waited for; matrix products, arithmetic and copies ran while one was open for 0% of the time, Pallas kernels for 26%

profile of v8, /device:TPU:0, one launch (start us, length us, event | category | flops | bytes accessed | tf_op | source)
XLA Modules:
  0.0 39.0 jit_solution(4017216548632446909)
XLA Ops:
  0.6 1.3 %pack_keys.1 = (bf16[2,3,256,128]{3,2,1,0:T(8,128)(2,1)S(1)}, s32[6,4,8]{2,1,0:T(4,128)S(4)}, bf16[6,256,128]{2,1,0:T(8,128)(2,1)S(1)}, bf16[6,256,128]{2,1,0:T(8,128)(2,1)S(1)}) custom-call(s32[6,4,8]{2,1,0:T(4,128)} %bitcast.1, bf16[6,256,128]{2,1,0:T(8,128)(2,1)} %keys.1, bf16[6,256,128]{2,1,0:T(8,128)(2,1)} %values.1), custom_call_target="tpu_custom_call" | custom-call | flops 1 | bytes 1 | tf_op jit(solution)/shard_map/pack_keys/pallas_call | solution.py:415
  2.0 3.0 %collective-permute-start = (bf16[2,3,256,128]{3,2,1,0:T(8,128)(2,1)S(1)}, bf16[2,3,256,128]{3,2,1,0:T(8,128)(2,1)S(1)}, u32[]{:S(2)}, u32[]{:S(2)}) collective-permute-start(bf16[2,3,256,128]{3,2,1,0:T(8,128)(2,1)S(1)} %get-tuple-element.43), channel_id=1, source_target_pairs={{0,2},{2,0},{4,6},{6,4},{8,10},{10,8},{12,14},{14,12},{1,3},{3,1},... | collective-permute-start | bytes 1179656 | tf_op jit(solution)/shard_map/ppermute | solution.py:37
  5.0 0.1 pack_more_keys.1
  5.1 0.8 %collective-permute-start.2 = (bf16[2,3,256,128]{3,2,1,0:T(8,128)(2,1)S(1)}, bf16[2,3,256,128]{3,2,1,0:T(8,128)(2,1)S(1)}, u32[]{:S(2)}, u32[]{:S(2)}) collective-permute-start(bf16[2,3,256,128]{3,2,1,0:T(8,128)(2,1)S(1)} %pack_more_keys.1), channel_id=1, source_target_pairs={{2,4},{4,2},{6,8},{8,6},{10,12},{12,10},{3,5},{5,3},{7,9},{9,7},{1... | collective-permute-start | bytes 1179656 | tf_op jit(solution)/shard_map/ppermute | solution.py:37
  5.9 4.2 %own_scores.1 = (f32[6,256,256]{2,1,0:T(8,128)S(1)}, f32[6,256,256]{2,1,0:T(8,128)S(1)}, f32[6,3,256]{2,1,0:T(4,128)S(1)}, bf16[2,2,256,128]{3,2,1,0:T(8,128)(2,1)S(1)}, bf16[2,3,256,128]{3,2,1,0:T(8,128)(2,1)S(1)}) custom-call(s32[24]{0:T(128)S(4)} %table.1.table_ref, bf16[6,256,128]{2,1,0:T(8,128)(2,1)} %q_ref.7, ...), custom_call_target="tpu_custom_call" | custom-call | flops 1 | bytes 1 | tf_op jit(solution)/shard_map/own_scores/pallas_call | solution.py:450
  10.1 4.7 %collective-permute-start.5 = (bf16[2,2,256,128]{3,2,1,0:T(8,128)(2,1)S(1)}, bf16[2,2,256,128]{3,2,1,0:T(8,128)(2,1)S(1)}, u32[]{:S(2)}, u32[]{:S(2)}) collective-permute-start(bf16[2,2,256,128]{3,2,1,0:T(8,128)(2,1)S(1)} %get-tuple-element.60), channel_id=1, source_target_pairs={{0,2},{2,0},{4,6},{6,4},{8,10},{10,8},{12,14},{14,12},{1,3},{3,1},... | collective-permute-start | bytes 786440 | tf_op jit(solution)/shard_map/ppermute | solution.py:37
  14.8 8.1 %collective-permute-done.rest_0_.rest_6_ = bf16[2,3,256,128]{3,2,1,0:T(8,128)(2,1)S(1)} collective-permute-done((bf16[2,3,256,128]{3,2,1,0:T(8,128)(2,1)S(1)}, bf16[2,3,256,128]{3,2,1,0:T(8,128)(2,1)S(1)}, u32[]{:S(2)}, u32[]{:S(2)}) %collective-permute-start) | collective-permute-done | bytes 393248 | tf_op jit(solution)/shard_map/ppermute | solution.py:37
  22.9 0.7 %collective-permute-start.1 = (bf16[2,3,256,128]{3,2,1,0:T(8,128)(2,1)S(1)}, bf16[2,3,256,128]{3,2,1,0:T(8,128)(2,1)S(1)}, u32[]{:S(2)}, u32[]{:S(2)}) collective-permute-start(bf16[2,3,256,128]{3,2,1,0:T(8,128)(2,1)S(1)} %get-tuple-element.44), channel_id=1, source_target_pairs={{2,4},{4,2},{6,8},{8,6},{10,12},{12,10},{3,5},{5,3},{7,9},{9,7},{1... | collective-permute-start | bytes 1179656 | tf_op jit(solution)/shard_map/ppermute | solution.py:37
  23.6 0.0 collective-permute-done.2.rest_1_.rest_7_
  23.6 0.0 copy-done
  23.6 0.9 %statistics.1 = (f32[6,256,256]{2,1,0:T(8,128)S(1)}, f32[6,256,256]{2,1,0:T(8,128)S(1)}, f32[6,2,256]{2,1,0:T(2,128)S(1)}, f32[6,2,256]{2,1,0:T(2,128)S(1)}, f32...) custom-call(s32[24]{0:T(128)S(4)} %table.1.table_ref, bf16[6,256,128]{2,1,0:T(8,128)(2,1)S(1)} %copy-done, ...), custom_call_target="tpu_custom_call" | custom-call | flops 1 | bytes 1 | tf_op jit(solution)/shard_map/statistics/pallas_call | solution.py:465
  24.5 0.7 %collective-permute-start.3 = (f32[3,2,256]{2,1,0:T(2,128)S(1)}, f32[3,2,256]{2,1,0:T(2,128)S(1)}, u32[]{:S(2)}, u32[]{:S(2)}) collective-permute-start(f32[3,2,256]{2,1,0:T(2,128)S(1)} %get-tuple-element.47), channel_id=1, source_target_pairs={{2,4},{4,2},{6,8},{8,6},{10,12},{12,10},{3,5},{5,3},{7,9},{9,7},{1... | collective-permute-start | bytes 18440 | tf_op jit(solution)/shard_map/ppermute | solution.py:37
  25.2 7.9 %collective-permute-start.6 = (f32[3,2,256]{2,1,0:T(2,128)S(1)}, f32[3,2,256]{2,1,0:T(2,128)S(1)}, u32[]{:S(2)}, u32[]{:S(2)}) collective-permute-start(f32[3,2,256]{2,1,0:T(2,128)S(1)} %get-tuple-element.63), channel_id=1, source_target_pairs={{0,2},{2,0},{4,6},{6,4},{8,10},{10,8},{12,14},{14,12},{1,3},{3,1},... | collective-permute-start | bytes 18440 | tf_op jit(solution)/shard_map/ppermute | solution.py:37
  33.2 0.2 returned.1
  33.4 0.1 collective-permute-start.4
  33.5 1.5 %reader.1 = (bf16[6,256,128]{2,1,0:T(8,128)(2,1)S(1)}, bf16[6,256,128]{2,1,0:T(8,128)(2,1)S(1)}, f32[6,256,128]{2,1,0:T(8,128)S(1)}, f32[6,256,128]{2,1,0:T(8,128)S(1)}) custom-call(s32[24]{0:T(128)S(4)} %table.1.table_ref, bf16[6,256,128]{2,1,0:T(8,128)(2,1)S(1)} %copy-done, bf16[6,256,128]{2,1,0:T(8,128)(2,1)S(1)} %get-tuple-element.40.k_ref.keys, ...), custom_call_target="tpu_custom_call" | custom-call | flops 99999997952 | bytes 1 | tf_op jit(solution)/shard_map/reader/pallas_call | solution.py:490
  35.0 0.0 collective-permute-done.3.stats
  35.0 0.0 collective-permute-done.1.arrived
  35.0 1.9 %owner.1 = (bf16[6,256,128]{2,1,0:T(8,128)(2,1)}, bf16[6,256,128]{2,1,0:T(8,128)(2,1)}, bf16[6,256,128]{2,1,0:T(8,128)(2,1)}, bf16[6,256,128]{2,1,0:T(8,128)(2,1...) custom-call(s32[24]{0:T(128)S(4)} %table.1.table_ref, bf16[6,256,128]{2,1,0:T(8,128)(2,1)S(1)} %get-tuple-element.40.k_ref.keys, ...), custom_call_target="tpu_custom_call" | custom-call | flops 1 | bytes 1 | tf_op jit(solution)/shard_map/owner/pallas_call | solution.py:517
  37.0 0.1 collective-permute-done.5.arrived
  37.1 0.1 collective-permute-done.6.stats
  37.2 1.3 %first_owner.1 = (bf16[6,256,128]{2,1,0:T(8,128)(2,1)}, bf16[6,256,128]{2,1,0:T(8,128)(2,1)}) custom-call(s32[24]{0:T(128)S(4)} %table.1.table_ref, bf16[6,256,128]{2,1,0:T(8,128)(2,1)S(1)} %get-tuple-element.40.k_ref.keys, bf16[6,256,128]{2,1,0:T(8,128)(2,1)S(1)} %get-tuple-element.41.v_ref.values, ...), custom_call_target="tpu_custom_call", output_to_operand_aliasing={{0}: (7, {}), {1}: (8, {})} | custom-call | flops 1 | bytes 1 | tf_op jit(solution)/shard_map/first_owner/pallas_call | solution.py:539
  38.6 0.3 collective-permute-done.4.terms
  38.9 0.1 closing.1
  (4 shorter events, 0.0 us)
Async XLA Ops:
  2.0 21.0 %collective-permute-start = (bf16[2,3,256,128]{3,2,1,0:T(8,128)(2,1)S(1)}, bf16[2,3,256,128]{3,2,1,0:T(8,128)(2,1)S(1)}, u32[]{:S(2)}, u32[]{:S(2)}) collective-permute-start(bf16[2,3,256,128]{3,2,1,0:T(8,128)(2,1)S(1)} %get-tuple-element.43), channel_id=1, source_target_pairs={{0,2},{2,0},{4,6},{6,4},{8,10},{10,8},{12,14},{14,12},{1,3},{3,1},... | collective-permute-start | bytes 1179656 | tf_op jit(solution)/shard_map/ppermute | solution.py:37
  5.0 18.6 %copy-start = (bf16[6,256,128]{2,1,0:T(8,128)(2,1)S(1)}, bf16[6,256,128]{2,1,0:T(8,128)(2,1)}, u32[]{:S(2)}) copy-start(bf16[6,256,128]{2,1,0:T(8,128)(2,1)} %q_ref.7) | copy-start | bytes 1179652
  5.0 18.6 %copy-start.1 = (bf16[6,256,128]{2,1,0:T(8,128)(2,1)S(1)}, bf16[6,256,128]{2,1,0:T(8,128)(2,1)}, u32[]{:S(2)}) copy-start(bf16[6,256,128]{2,1,0:T(8,128)(2,1)} %g_ref.7) | copy-start | bytes 1179652
  5.1 18.6 %collective-permute-start.2 = (bf16[2,3,256,128]{3,2,1,0:T(8,128)(2,1)S(1)}, bf16[2,3,256,128]{3,2,1,0:T(8,128)(2,1)S(1)}, u32[]{:S(2)}, u32[]{:S(2)}) collective-permute-start(bf16[2,3,256,128]{3,2,1,0:T(8,128)(2,1)S(1)} %pack_more_keys.1), channel_id=1, source_target_pairs={{2,4},{4,2},{6,8},{8,6},{10,12},{12,10},{3,5},{5,3},{7,9},{9,7},{1... | collective-permute-start | bytes 1179656 | tf_op jit(solution)/shard_map/ppermute | solution.py:37
  10.1 27.0 %collective-permute-start.5 = (bf16[2,2,256,128]{3,2,1,0:T(8,128)(2,1)S(1)}, bf16[2,2,256,128]{3,2,1,0:T(8,128)(2,1)S(1)}, u32[]{:S(2)}, u32[]{:S(2)}) collective-permute-start(bf16[2,2,256,128]{3,2,1,0:T(8,128)(2,1)S(1)} %get-tuple-element.60), channel_id=1, source_target_pairs={{0,2},{2,0},{4,6},{6,4},{8,10},{10,8},{12,14},{14,12},{1,3},{3,1},... | collective-permute-start | bytes 786440 | tf_op jit(solution)/shard_map/ppermute | solution.py:37
  22.9 12.1 %collective-permute-start.1 = (bf16[2,3,256,128]{3,2,1,0:T(8,128)(2,1)S(1)}, bf16[2,3,256,128]{3,2,1,0:T(8,128)(2,1)S(1)}, u32[]{:S(2)}, u32[]{:S(2)}) collective-permute-start(bf16[2,3,256,128]{3,2,1,0:T(8,128)(2,1)S(1)} %get-tuple-element.44), channel_id=1, source_target_pairs={{2,4},{4,2},{6,8},{8,6},{10,12},{12,10},{3,5},{5,3},{7,9},{9,7},{1... | collective-permute-start | bytes 1179656 | tf_op jit(solution)/shard_map/ppermute | solution.py:37
  24.5 10.5 %collective-permute-start.3 = (f32[3,2,256]{2,1,0:T(2,128)S(1)}, f32[3,2,256]{2,1,0:T(2,128)S(1)}, u32[]{:S(2)}, u32[]{:S(2)}) collective-permute-start(f32[3,2,256]{2,1,0:T(2,128)S(1)} %get-tuple-element.47), channel_id=1, source_target_pairs={{2,4},{4,2},{6,8},{8,6},{10,12},{12,10},{3,5},{5,3},{7,9},{9,7},{1... | collective-permute-start | bytes 18440 | tf_op jit(solution)/shard_map/ppermute | solution.py:37
  25.2 12.0 %collective-permute-start.6 = (f32[3,2,256]{2,1,0:T(2,128)S(1)}, f32[3,2,256]{2,1,0:T(2,128)S(1)}, u32[]{:S(2)}, u32[]{:S(2)}) collective-permute-start(f32[3,2,256]{2,1,0:T(2,128)S(1)} %get-tuple-element.63), channel_id=1, source_target_pairs={{0,2},{2,0},{4,6},{6,4},{8,10},{10,8},{12,14},{14,12},{1,3},{3,1},... | collective-permute-start | bytes 18440 | tf_op jit(solution)/shard_map/ppermute | solution.py:37
  33.4 5.5 %collective-permute-start.4 = (bf16[2,1,256,128]{3,2,1,0:T(8,128)(2,1)S(1)}, bf16[2,1,256,128]{3,2,1,0:T(8,128)(2,1)S(1)}, u32[]{:S(2)}, u32[]{:S(2)}) collective-permute-start(bf16[2,1,256,128]{3,2,1,0:T(8,128)(2,1)S(1)} %returned.1), channel_id=1, source_target_pairs={{0,2},{2,0},{4,6},{6,4},{8,10},{10,8},{12,14},{14,12},{1,3},{3,1},... | collective-permute-start | bytes 393224 | tf_op jit(solution)/shard_map/ppermute | solution.py:37

commit v9 on v8

--- a/solution.py
+++ b/solution.py
@@ -80,12 +80,9 @@
 def pack_keys_kernel(cap, channel, lists_hbm, keys, values, target, lists, *rest):
     *held, sems = rest
     heads, _, tile_count = lists.shape
-    loads = [pltpu.make_async_copy(lists_hbm, lists, sems.at[2, 0])]
+    loads = [pltpu.make_async_copy(lists_hbm, lists, sems.at[2])]
     for part, source in enumerate((keys, values)):
-        for head in range(heads):
-            loads.append(
-                pltpu.make_async_copy(source.at[head], held[part].at[head], sems.at[part, head])
-            )
+        loads.append(pltpu.make_async_copy(source, held[part], sems.at[part]))
     for load in loads:
         load.start()
     loads[0].wait()
@@ -417,7 +414,7 @@
         out_shape=[packed, pltpu.SMEM(lists.shape, jnp.int32)] + [whole_near] * 2,
         in_specs=[anywhere] * 3,
         out_specs=[vmem, smem, vmem, vmem],
-        scratch_shapes=[pltpu.SemaphoreType.DMA((3, heads))],
+        scratch_shapes=[pltpu.SemaphoreType.DMA((3,))],
         compiler_params=params,
         cost_estimate=brief,
         name="pack_keys",

time: 39.6 us -> 39.8 us (level)
  Pallas kernels: 11.6 us -> 12 us
    pallas_call x1, Pallas kernels: 0.08 us -> 0.73 us  [per_device(): pl.pallas_call(functools.partial(closing_kernel, count, cap), out_shape=[...]
where the time goes in v9:
time: 39.8 us; the launch traced here: 39.5 us
  starting transfers between devices  18 us (45%)
  Pallas kernels  12 us (30%)
  waiting for transfers between devices  8.73 us (22%)
  between operations  0.76 us (2%)
    ppermute x7, starting transfers between devices, swapped(): return lax.ppermute(block, 'seq', swap_route(channel, lax.axis_size('seq')))  18 us
    ppermute x7, waiting for transfers between devices, swapped(): return lax.ppermute(block, 'seq', swap_route(channel, lax.axis_size('seq')))  8.73 us
    pallas_call x1, Pallas kernels, per_device(): pl.pallas_call(functools.partial(own_kernel, count, cap, scale), grid=(he...  4.17 us
    pallas_call x1, Pallas kernels, per_device(): pl.pallas_call(functools.partial(owner_kernel, count, cap, scale, number)...  1.9 us
    pallas_call x1, Pallas kernels, per_device(): pl.pallas_call(functools.partial(reader_kernel, count, cap, scale), out_s...  1.53 us
    pallas_call x1, Pallas kernels, per_device(): pl.pallas_call(functools.partial(first_owner_kernel, count, cap, scale),...  1.34 us
    pallas_call x1, Pallas kernels, per_device(): pl.pallas_call(functools.partial(pack_keys_kernel, cap, channels[0]), out...  1.17 us
    pallas_call x1, Pallas kernels, per_device(): pl.pallas_call(functools.partial(statistics_kernel, count, cap, scale), o...  0.88 us
  transfers between devices with their start and end apart: 7, of which 4 were waited for; matrix products, arithmetic and copies ran while one was open for 0% of the time, Pallas kernels for 26%

profile of v9, /device:TPU:0, one launch (start us, length us, event | category | flops | bytes accessed | tf_op | source)
XLA Modules:
  0.0 39.5 jit_solution(16535725583350116243)
XLA Ops:
  0.6 1.2 %pack_keys.1 = (bf16[2,3,256,128]{3,2,1,0:T(8,128)(2,1)S(1)}, s32[6,4,8]{2,1,0:T(4,128)S(4)}, bf16[6,256,128]{2,1,0:T(8,128)(2,1)S(1)}, bf16[6,256,128]{2,1,0:T(8,128)(2,1)S(1)}) custom-call(s32[6,4,8]{2,1,0:T(4,128)} %bitcast.1, bf16[6,256,128]{2,1,0:T(8,128)(2,1)} %keys.1, bf16[6,256,128]{2,1,0:T(8,128)(2,1)} %values.1), custom_call_target="tpu_custom_call" | custom-call | flops 1 | bytes 1 | tf_op jit(solution)/shard_map/pack_keys/pallas_call | solution.py:412
  1.8 3.0 %collective-permute-start = (bf16[2,3,256,128]{3,2,1,0:T(8,128)(2,1)S(1)}, bf16[2,3,256,128]{3,2,1,0:T(8,128)(2,1)S(1)}, u32[]{:S(2)}, u32[]{:S(2)}) collective-permute-start(bf16[2,3,256,128]{3,2,1,0:T(8,128)(2,1)S(1)} %get-tuple-element.43), channel_id=1, source_target_pairs={{0,2},{2,0},{4,6},{6,4},{8,10},{10,8},{12,14},{14,12},{1,3},{3,1},... | collective-permute-start | bytes 1179656 | tf_op jit(solution)/shard_map/ppermute | solution.py:37
  4.8 0.1 pack_more_keys.1
  4.9 0.8 %collective-permute-start.2 = (bf16[2,3,256,128]{3,2,1,0:T(8,128)(2,1)S(1)}, bf16[2,3,256,128]{3,2,1,0:T(8,128)(2,1)S(1)}, u32[]{:S(2)}, u32[]{:S(2)}) collective-permute-start(bf16[2,3,256,128]{3,2,1,0:T(8,128)(2,1)S(1)} %pack_more_keys.1), channel_id=1, source_target_pairs={{2,4},{4,2},{6,8},{8,6},{10,12},{12,10},{3,5},{5,3},{7,9},{9,7},{1... | collective-permute-start | bytes 1179656 | tf_op jit(solution)/shard_map/ppermute | solution.py:37
  5.7 4.2 %own_scores.1 = (f32[6,256,256]{2,1,0:T(8,128)S(1)}, f32[6,256,256]{2,1,0:T(8,128)S(1)}, f32[6,3,256]{2,1,0:T(4,128)S(1)}, bf16[2,2,256,128]{3,2,1,0:T(8,128)(2,1)S(1)}, bf16[2,3,256,128]{3,2,1,0:T(8,128)(2,1)S(1)}) custom-call(s32[24]{0:T(128)S(4)} %table.1.table_ref, bf16[6,256,128]{2,1,0:T(8,128)(2,1)} %q_ref.7, ...), custom_call_target="tpu_custom_call" | custom-call | flops 1 | bytes 1 | tf_op jit(solution)/shard_map/own_scores/pallas_call | solution.py:447
  9.9 4.8 %collective-permute-start.5 = (bf16[2,2,256,128]{3,2,1,0:T(8,128)(2,1)S(1)}, bf16[2,2,256,128]{3,2,1,0:T(8,128)(2,1)S(1)}, u32[]{:S(2)}, u32[]{:S(2)}) collective-permute-start(bf16[2,2,256,128]{3,2,1,0:T(8,128)(2,1)S(1)} %get-tuple-element.60), channel_id=1, source_target_pairs={{0,2},{2,0},{4,6},{6,4},{8,10},{10,8},{12,14},{14,12},{1,3},{3,1},... | collective-permute-start | bytes 786440 | tf_op jit(solution)/shard_map/ppermute | solution.py:37
  14.6 8.1 %collective-permute-done.rest_0_.rest_6_ = bf16[2,3,256,128]{3,2,1,0:T(8,128)(2,1)S(1)} collective-permute-done((bf16[2,3,256,128]{3,2,1,0:T(8,128)(2,1)S(1)}, bf16[2,3,256,128]{3,2,1,0:T(8,128)(2,1)S(1)}, u32[]{:S(2)}, u32[]{:S(2)}) %collective-permute-start) | collective-permute-done | bytes 393248 | tf_op jit(solution)/shard_map/ppermute | solution.py:37
  22.8 0.7 %collective-permute-start.1 = (bf16[2,3,256,128]{3,2,1,0:T(8,128)(2,1)S(1)}, bf16[2,3,256,128]{3,2,1,0:T(8,128)(2,1)S(1)}, u32[]{:S(2)}, u32[]{:S(2)}) collective-permute-start(bf16[2,3,256,128]{3,2,1,0:T(8,128)(2,1)S(1)} %get-tuple-element.44), channel_id=1, source_target_pairs={{2,4},{4,2},{6,8},{8,6},{10,12},{12,10},{3,5},{5,3},{7,9},{9,7},{1... | collective-permute-start | bytes 1179656 | tf_op jit(solution)/shard_map/ppermute | solution.py:37
  23.4 0.0 collective-permute-done.2.rest_1_.rest_7_
  23.4 0.0 copy-done
  23.5 0.9 %statistics.1 = (f32[6,256,256]{2,1,0:T(8,128)S(1)}, f32[6,256,256]{2,1,0:T(8,128)S(1)}, f32[6,2,256]{2,1,0:T(2,128)S(1)}, f32[6,2,256]{2,1,0:T(2,128)S(1)}, f32...) custom-call(s32[24]{0:T(128)S(4)} %table.1.table_ref, bf16[6,256,128]{2,1,0:T(8,128)(2,1)S(1)} %copy-done, ...), custom_call_target="tpu_custom_call" | custom-call | flops 1 | bytes 1 | tf_op jit(solution)/shard_map/statistics/pallas_call | solution.py:462
  24.4 0.7 %collective-permute-start.3 = (f32[3,2,256]{2,1,0:T(2,128)S(1)}, f32[3,2,256]{2,1,0:T(2,128)S(1)}, u32[]{:S(2)}, u32[]{:S(2)}) collective-permute-start(f32[3,2,256]{2,1,0:T(2,128)S(1)} %get-tuple-element.47), channel_id=1, source_target_pairs={{2,4},{4,2},{6,8},{8,6},{10,12},{12,10},{3,5},{5,3},{7,9},{9,7},{1... | collective-permute-start | bytes 18440 | tf_op jit(solution)/shard_map/ppermute | solution.py:37
  25.0 7.9 %collective-permute-start.6 = (f32[3,2,256]{2,1,0:T(2,128)S(1)}, f32[3,2,256]{2,1,0:T(2,128)S(1)}, u32[]{:S(2)}, u32[]{:S(2)}) collective-permute-start(f32[3,2,256]{2,1,0:T(2,128)S(1)} %get-tuple-element.63), channel_id=1, source_target_pairs={{0,2},{2,0},{4,6},{6,4},{8,10},{10,8},{12,14},{14,12},{1,3},{3,1},... | collective-permute-start | bytes 18440 | tf_op jit(solution)/shard_map/ppermute | solution.py:37
  33.0 0.2 returned.1
  33.2 0.1 collective-permute-start.4
  33.3 1.5 %reader.1 = (bf16[6,256,128]{2,1,0:T(8,128)(2,1)S(1)}, bf16[6,256,128]{2,1,0:T(8,128)(2,1)S(1)}, f32[6,256,128]{2,1,0:T(8,128)S(1)}, f32[6,256,128]{2,1,0:T(8,128)S(1)}) custom-call(s32[24]{0:T(128)S(4)} %table.1.table_ref, bf16[6,256,128]{2,1,0:T(8,128)(2,1)S(1)} %copy-done, bf16[6,256,128]{2,1,0:T(8,128)(2,1)S(1)} %get-tuple-element.40.k_ref.keys, ...), custom_call_target="tpu_custom_call" | custom-call | flops 99999997952 | bytes 1 | tf_op jit(solution)/shard_map/reader/pallas_call | solution.py:487
  34.8 0.0 collective-permute-done.3.stats
  34.8 0.0 collective-permute-done.1.arrived
  34.9 1.9 %owner.1 = (bf16[6,256,128]{2,1,0:T(8,128)(2,1)}, bf16[6,256,128]{2,1,0:T(8,128)(2,1)}, bf16[6,256,128]{2,1,0:T(8,128)(2,1)}, bf16[6,256,128]{2,1,0:T(8,128)(2,1...) custom-call(s32[24]{0:T(128)S(4)} %table.1.table_ref, bf16[6,256,128]{2,1,0:T(8,128)(2,1)S(1)} %get-tuple-element.40.k_ref.keys, ...), custom_call_target="tpu_custom_call" | custom-call | flops 1 | bytes 1 | tf_op jit(solution)/shard_map/owner/pallas_call | solution.py:514
  36.8 0.2 collective-permute-done.5.arrived
  36.9 0.1 collective-permute-done.6.stats
  37.1 1.3 %first_owner.1 = (bf16[6,256,128]{2,1,0:T(8,128)(2,1)}, bf16[6,256,128]{2,1,0:T(8,128)(2,1)}) custom-call(s32[24]{0:T(128)S(4)} %table.1.table_ref, bf16[6,256,128]{2,1,0:T(8,128)(2,1)S(1)} %get-tuple-element.40.k_ref.keys, bf16[6,256,128]{2,1,0:T(8,128)(2,1)S(1)} %get-tuple-element.41.v_ref.values, ...), custom_call_target="tpu_custom_call", output_to_operand_aliasing={{0}: (7, {}), {1}: (8, {})} | custom-call | flops 1 | bytes 1 | tf_op jit(solution)/shard_map/first_owner/pallas_call | solution.py:536
  38.4 0.3 collective-permute-done.4.terms
  38.7 0.7 %closing.1 = (bf16[6,256,128]{2,1,0:T(8,128)(2,1)}, bf16[6,256,128]{2,1,0:T(8,128)(2,1)}) custom-call(s32[24]{0:T(128)S(4)} %table.1.table_ref, bf16[2,1,256,128]{3,2,1,0:T(8,128)(2,1)S(1)} %collective-permute-done.4.terms, f32[6,256,128]{2,1,0:T(8,128)S(1)} %get-tuple-element.64.rest_0_.dk_in, ...), custom_call_target="tpu_custom_call", output_to_operand_aliasing={{0}: (4, {}), {1}: (5, {})} | custom-call | flops 1 | bytes 1 | tf_op jit(solution)/shard_map/closing/pallas_call | solution.py:548
  (4 shorter events, 0.0 us)
Async XLA Ops:
  1.8 21.0 %collective-permute-start = (bf16[2,3,256,128]{3,2,1,0:T(8,128)(2,1)S(1)}, bf16[2,3,256,128]{3,2,1,0:T(8,128)(2,1)S(1)}, u32[]{:S(2)}, u32[]{:S(2)}) collective-permute-start(bf16[2,3,256,128]{3,2,1,0:T(8,128)(2,1)S(1)} %get-tuple-element.43), channel_id=1, source_target_pairs={{0,2},{2,0},{4,6},{6,4},{8,10},{10,8},{12,14},{14,12},{1,3},{3,1},... | collective-permute-start | bytes 1179656 | tf_op jit(solution)/shard_map/ppermute | solution.py:37
  4.8 18.6 %copy-start = (bf16[6,256,128]{2,1,0:T(8,128)(2,1)S(1)}, bf16[6,256,128]{2,1,0:T(8,128)(2,1)}, u32[]{:S(2)}) copy-start(bf16[6,256,128]{2,1,0:T(8,128)(2,1)} %q_ref.7) | copy-start | bytes 1179652
  4.8 18.6 %copy-start.1 = (bf16[6,256,128]{2,1,0:T(8,128)(2,1)S(1)}, bf16[6,256,128]{2,1,0:T(8,128)(2,1)}, u32[]{:S(2)}) copy-start(bf16[6,256,128]{2,1,0:T(8,128)(2,1)} %g_ref.7) | copy-start | bytes 1179652
  4.9 18.6 %collective-permute-start.2 = (bf16[2,3,256,128]{3,2,1,0:T(8,128)(2,1)S(1)}, bf16[2,3,256,128]{3,2,1,0:T(8,128)(2,1)S(1)}, u32[]{:S(2)}, u32[]{:S(2)}) collective-permute-start(bf16[2,3,256,128]{3,2,1,0:T(8,128)(2,1)S(1)} %pack_more_keys.1), channel_id=1, source_target_pairs={{2,4},{4,2},{6,8},{8,6},{10,12},{12,10},{3,5},{5,3},{7,9},{9,7},{1... | collective-permute-start | bytes 1179656 | tf_op jit(solution)/shard_map/ppermute | solution.py:37
  9.9 27.1 %collective-permute-start.5 = (bf16[2,2,256,128]{3,2,1,0:T(8,128)(2,1)S(1)}, bf16[2,2,256,128]{3,2,1,0:T(8,128)(2,1)S(1)}, u32[]{:S(2)}, u32[]{:S(2)}) collective-permute-start(bf16[2,2,256,128]{3,2,1,0:T(8,128)(2,1)S(1)} %get-tuple-element.60), channel_id=1, source_target_pairs={{0,2},{2,0},{4,6},{6,4},{8,10},{10,8},{12,14},{14,12},{1,3},{3,1},... | collective-permute-start | bytes 786440 | tf_op jit(solution)/shard_map/ppermute | solution.py:37
  22.8 12.1 %collective-permute-start.1 = (bf16[2,3,256,128]{3,2,1,0:T(8,128)(2,1)S(1)}, bf16[2,3,256,128]{3,2,1,0:T(8,128)(2,1)S(1)}, u32[]{:S(2)}, u32[]{:S(2)}) collective-permute-start(bf16[2,3,256,128]{3,2,1,0:T(8,128)(2,1)S(1)} %get-tuple-element.44), channel_id=1, source_target_pairs={{2,4},{4,2},{6,8},{8,6},{10,12},{12,10},{3,5},{5,3},{7,9},{9,7},{1... | collective-permute-start | bytes 1179656 | tf_op jit(solution)/shard_map/ppermute | solution.py:37
  24.4 10.5 %collective-permute-start.3 = (f32[3,2,256]{2,1,0:T(2,128)S(1)}, f32[3,2,256]{2,1,0:T(2,128)S(1)}, u32[]{:S(2)}, u32[]{:S(2)}) collective-permute-start(f32[3,2,256]{2,1,0:T(2,128)S(1)} %get-tuple-element.47), channel_id=1, source_target_pairs={{2,4},{4,2},{6,8},{8,6},{10,12},{12,10},{3,5},{5,3},{7,9},{9,7},{1... | collective-permute-start | bytes 18440 | tf_op jit(solution)/shard_map/ppermute | solution.py:37
  25.0 12.0 %collective-permute-start.6 = (f32[3,2,256]{2,1,0:T(2,128)S(1)}, f32[3,2,256]{2,1,0:T(2,128)S(1)}, u32[]{:S(2)}, u32[]{:S(2)}) collective-permute-start(f32[3,2,256]{2,1,0:T(2,128)S(1)} %get-tuple-element.63), channel_id=1, source_target_pairs={{0,2},{2,0},{4,6},{6,4},{8,10},{10,8},{12,14},{14,12},{1,3},{3,1},... | collective-permute-start | bytes 18440 | tf_op jit(solution)/shard_map/ppermute | solution.py:37
  33.2 5.5 %collective-permute-start.4 = (bf16[2,1,256,128]{3,2,1,0:T(8,128)(2,1)S(1)}, bf16[2,1,256,128]{3,2,1,0:T(8,128)(2,1)S(1)}, u32[]{:S(2)}, u32[]{:S(2)}) collective-permute-start(bf16[2,1,256,128]{3,2,1,0:T(8,128)(2,1)S(1)} %returned.1), channel_id=1, source_target_pairs={{0,2},{2,0},{4,6},{6,4},{8,10},{10,8},{12,14},{14,12},{1,3},{3,1},... | collective-permute-start | bytes 393224 | tf_op jit(solution)/shard_map/ppermute | solution.py:37

commit v10 on v9

--- a/solution.py
+++ b/solution.py
@@ -364,21 +364,23 @@
     _, _, dk_out, dv_out, staged, sems = rest
     table = Table(table_ref, dk_in.shape[0], count, cap)
     returned = terms.shape[1]
-    stores = []
     for number in range(returned):
-        found = table_ref[table.owner_at(0, cap - returned + number)]
-        head = jnp.maximum(found, 0)
-        for part, (total, result) in enumerate(((dk_in, dk_out), (dv_in, dv_out))):
-            term = terms[part, number].astype(jnp.float32)
-            staged[part, number] = (total[head] + term).astype(jnp.bfloat16)
-            store = pltpu.make_async_copy(
-                staged.at[part, number], result.at[head], sems.at[part, number]
-            )
-            stores.append((found >= 0, store))
-    for wanted, store in stores:
-        pl.when(wanted)(store.start)
-    for wanted, store in stores:
-        pl.when(wanted)(store.wait)
+        head = table_ref[table.owner_at(0, cap - returned + number)]
+
+        @pl.when(head >= 0)
+        def _():
+            stores = []
+            for part, (total, result) in enumerate(((dk_in, dk_out), (dv_in, dv_out))):
+                term = terms[part, number].astype(jnp.float32)
+                staged[part, number] = (total[head] + term).astype(jnp.bfloat16)
+                stores.append(
+                    pltpu.make_async_copy(
+                        staged.at[part, number], result.at[head], sems.at[part, number]
+                    )
+                )
+                stores[-1].start()
+            for store in stores:
+                store.wait()
 
 
 def per_device(queries, keys, values, out_grad, tile_lists):

time: 39.8 us -> 39.4 us (0.990)
  Pallas kernels: 12 us -> 11.4 us
    pallas_call x1, Pallas kernels: 0.73 us -> 0.05 us  [per_device(): pl.pallas_call(functools.partial(closing_kernel, count, cap), out_shape=[...]
where the time goes in v10:
time: 39.4 us; the launch traced here: 38.8 us
  starting transfers between devices  17.9 us (45%)
  Pallas kernels  11.4 us (29%)
  waiting for transfers between devices  8.7 us (22%)
  between operations  0.76 us (2%)
    ppermute x7, starting transfers between devices, swapped(): return lax.ppermute(block, 'seq', swap_route(channel, lax.axis_size('seq')))  17.9 us
    ppermute x7, waiting for transfers between devices, swapped(): return lax.ppermute(block, 'seq', swap_route(channel, lax.axis_size('seq')))  8.7 us
    pallas_call x1, Pallas kernels, per_device(): pl.pallas_call(functools.partial(own_kernel, count, cap, scale), grid=(he...  4.19 us
    pallas_call x1, Pallas kernels, per_device(): pl.pallas_call(functools.partial(owner_kernel, count, cap, scale, number)...  1.99 us
    pallas_call x1, Pallas kernels, per_device(): pl.pallas_call(functools.partial(reader_kernel, count, cap, scale), out_s...  1.53 us
    pallas_call x1, Pallas kernels, per_device(): pl.pallas_call(functools.partial(first_owner_kernel, count, cap, scale),...  1.3 us
    pallas_call x1, Pallas kernels, per_device(): pl.pallas_call(functools.partial(pack_keys_kernel, cap, channels[0]), out...  1.17 us
    pallas_call x1, Pallas kernels, per_device(): pl.pallas_call(functools.partial(statistics_kernel, count, cap, scale), o...  0.88 us
  transfers between devices with their start and end apart: 7, of which 4 were waited for; matrix products, arithmetic and copies ran while one was open for 0% of the time, Pallas kernels for 26%

profile of v10, /device:TPU:0, one launch (start us, length us, event | category | flops | bytes accessed | tf_op | source)
XLA Modules:
  0.0 38.8 jit_solution(10811685346057946310)
XLA Ops:
  0.6 1.2 %pack_keys.1 = (bf16[2,3,256,128]{3,2,1,0:T(8,128)(2,1)S(1)}, s32[6,4,8]{2,1,0:T(4,128)S(4)}, bf16[6,256,128]{2,1,0:T(8,128)(2,1)S(1)}, bf16[6,256,128]{2,1,0:T(8,128)(2,1)S(1)}) custom-call(s32[6,4,8]{2,1,0:T(4,128)} %bitcast.1, bf16[6,256,128]{2,1,0:T(8,128)(2,1)} %keys.1, bf16[6,256,128]{2,1,0:T(8,128)(2,1)} %values.1), custom_call_target="tpu_custom_call" | custom-call | flops 1 | bytes 1 | tf_op jit(solution)/shard_map/pack_keys/pallas_call | solution.py:414
  1.8 3.0 %collective-permute-start = (bf16[2,3,256,128]{3,2,1,0:T(8,128)(2,1)S(1)}, bf16[2,3,256,128]{3,2,1,0:T(8,128)(2,1)S(1)}, u32[]{:S(2)}, u32[]{:S(2)}) collective-permute-start(bf16[2,3,256,128]{3,2,1,0:T(8,128)(2,1)S(1)} %get-tuple-element.43), channel_id=1, source_target_pairs={{0,2},{2,0},{4,6},{6,4},{8,10},{10,8},{12,14},{14,12},{1,3},{3,1},... | collective-permute-start | bytes 1179656 | tf_op jit(solution)/shard_map/ppermute | solution.py:37
  4.8 0.1 pack_more_keys.1
  4.9 0.8 %collective-permute-start.2 = (bf16[2,3,256,128]{3,2,1,0:T(8,128)(2,1)S(1)}, bf16[2,3,256,128]{3,2,1,0:T(8,128)(2,1)S(1)}, u32[]{:S(2)}, u32[]{:S(2)}) collective-permute-start(bf16[2,3,256,128]{3,2,1,0:T(8,128)(2,1)S(1)} %pack_more_keys.1), channel_id=1, source_target_pairs={{2,4},{4,2},{6,8},{8,6},{10,12},{12,10},{3,5},{5,3},{7,9},{9,7},{1... | collective-permute-start | bytes 1179656 | tf_op jit(solution)/shard_map/ppermute | solution.py:37
  5.7 4.2 %own_scores.1 = (f32[6,256,256]{2,1,0:T(8,128)S(1)}, f32[6,256,256]{2,1,0:T(8,128)S(1)}, f32[6,3,256]{2,1,0:T(4,128)S(1)}, bf16[2,2,256,128]{3,2,1,0:T(8,128)(2,1)S(1)}, bf16[2,3,256,128]{3,2,1,0:T(8,128)(2,1)S(1)}) custom-call(s32[24]{0:T(128)S(4)} %table.1.table_ref, bf16[6,256,128]{2,1,0:T(8,128)(2,1)} %q_ref.7, ...), custom_call_target="tpu_custom_call" | custom-call | flops 1 | bytes 1 | tf_op jit(solution)/shard_map/own_scores/pallas_call | solution.py:449
  9.9 4.7 %collective-permute-start.5 = (bf16[2,2,256,128]{3,2,1,0:T(8,128)(2,1)S(1)}, bf16[2,2,256,128]{3,2,1,0:T(8,128)(2,1)S(1)}, u32[]{:S(2)}, u32[]{:S(2)}) collective-permute-start(bf16[2,2,256,128]{3,2,1,0:T(8,128)(2,1)S(1)} %get-tuple-element.60), channel_id=1, source_target_pairs={{0,2},{2,0},{4,6},{6,4},{8,10},{10,8},{12,14},{14,12},{1,3},{3,1},... | collective-permute-start | bytes 786440 | tf_op jit(solution)/shard_map/ppermute | solution.py:37
  14.6 8.1 %collective-permute-done.rest_0_.rest_6_ = bf16[2,3,256,128]{3,2,1,0:T(8,128)(2,1)S(1)} collective-permute-done((bf16[2,3,256,128]{3,2,1,0:T(8,128)(2,1)S(1)}, bf16[2,3,256,128]{3,2,1,0:T(8,128)(2,1)S(1)}, u32[]{:S(2)}, u32[]{:S(2)}) %collective-permute-start) | collective-permute-done | bytes 393248 | tf_op jit(solution)/shard_map/ppermute | solution.py:37
  22.8 0.7 %collective-permute-start.1 = (bf16[2,3,256,128]{3,2,1,0:T(8,128)(2,1)S(1)}, bf16[2,3,256,128]{3,2,1,0:T(8,128)(2,1)S(1)}, u32[]{:S(2)}, u32[]{:S(2)}) collective-permute-start(bf16[2,3,256,128]{3,2,1,0:T(8,128)(2,1)S(1)} %get-tuple-element.44), channel_id=1, source_target_pairs={{2,4},{4,2},{6,8},{8,6},{10,12},{12,10},{3,5},{5,3},{7,9},{9,7},{1... | collective-permute-start | bytes 1179656 | tf_op jit(solution)/shard_map/ppermute | solution.py:37
  23.4 0.0 collective-permute-done.2.rest_1_.rest_7_
  23.4 0.0 copy-done
  23.5 0.9 %statistics.1 = (f32[6,256,256]{2,1,0:T(8,128)S(1)}, f32[6,256,256]{2,1,0:T(8,128)S(1)}, f32[6,2,256]{2,1,0:T(2,128)S(1)}, f32[6,2,256]{2,1,0:T(2,128)S(1)}, f32...) custom-call(s32[24]{0:T(128)S(4)} %table.1.table_ref, bf16[6,256,128]{2,1,0:T(8,128)(2,1)S(1)} %copy-done, ...), custom_call_target="tpu_custom_call" | custom-call | flops 1 | bytes 1 | tf_op jit(solution)/shard_map/statistics/pallas_call | solution.py:464
  24.4 0.7 %collective-permute-start.3 = (f32[3,2,256]{2,1,0:T(2,128)S(1)}, f32[3,2,256]{2,1,0:T(2,128)S(1)}, u32[]{:S(2)}, u32[]{:S(2)}) collective-permute-start(f32[3,2,256]{2,1,0:T(2,128)S(1)} %get-tuple-element.47), channel_id=1, source_target_pairs={{2,4},{4,2},{6,8},{8,6},{10,12},{12,10},{3,5},{5,3},{7,9},{9,7},{1... | collective-permute-start | bytes 18440 | tf_op jit(solution)/shard_map/ppermute | solution.py:37
  25.0 7.9 %collective-permute-start.6 = (f32[3,2,256]{2,1,0:T(2,128)S(1)}, f32[3,2,256]{2,1,0:T(2,128)S(1)}, u32[]{:S(2)}, u32[]{:S(2)}) collective-permute-start(f32[3,2,256]{2,1,0:T(2,128)S(1)} %get-tuple-element.63), channel_id=1, source_target_pairs={{0,2},{2,0},{4,6},{6,4},{8,10},{10,8},{12,14},{14,12},{1,3},{3,1},... | collective-permute-start | bytes 18440 | tf_op jit(solution)/shard_map/ppermute | solution.py:37
  33.0 0.2 returned.1
  33.2 0.1 collective-permute-start.4
  33.3 1.5 %reader.1 = (bf16[6,256,128]{2,1,0:T(8,128)(2,1)S(1)}, bf16[6,256,128]{2,1,0:T(8,128)(2,1)S(1)}, f32[6,256,128]{2,1,0:T(8,128)S(1)}, f32[6,256,128]{2,1,0:T(8,128)S(1)}) custom-call(s32[24]{0:T(128)S(4)} %table.1.table_ref, bf16[6,256,128]{2,1,0:T(8,128)(2,1)S(1)} %copy-done, bf16[6,256,128]{2,1,0:T(8,128)(2,1)S(1)} %get-tuple-element.40.k_ref.keys, ...), custom_call_target="tpu_custom_call" | custom-call | flops 99999997952 | bytes 1 | tf_op jit(solution)/shard_map/reader/pallas_call | solution.py:489
  34.8 0.0 collective-permute-done.3.stats
  34.8 0.0 collective-permute-done.1.arrived
  34.9 2.0 %owner.1 = (bf16[6,256,128]{2,1,0:T(8,128)(2,1)}, bf16[6,256,128]{2,1,0:T(8,128)(2,1)}, bf16[6,256,128]{2,1,0:T(8,128)(2,1)}, bf16[6,256,128]{2,1,0:T(8,128)(2,1...) custom-call(s32[24]{0:T(128)S(4)} %table.1.table_ref, bf16[6,256,128]{2,1,0:T(8,128)(2,1)S(1)} %get-tuple-element.40.k_ref.keys, ...), custom_call_target="tpu_custom_call" | custom-call | flops 1 | bytes 1 | tf_op jit(solution)/shard_map/owner/pallas_call | solution.py:516
  36.8 0.1 collective-permute-done.5.arrived
  36.9 0.1 collective-permute-done.6.stats
  37.1 1.3 %first_owner.1 = (bf16[6,256,128]{2,1,0:T(8,128)(2,1)}, bf16[6,256,128]{2,1,0:T(8,128)(2,1)}) custom-call(s32[24]{0:T(128)S(4)} %table.1.table_ref, bf16[6,256,128]{2,1,0:T(8,128)(2,1)S(1)} %get-tuple-element.40.k_ref.keys, bf16[6,256,128]{2,1,0:T(8,128)(2,1)S(1)} %get-tuple-element.41.v_ref.values, ...), custom_call_target="tpu_custom_call", output_to_operand_aliasing={{0}: (7, {}), {1}: (8, {})} | custom-call | flops 1 | bytes 1 | tf_op jit(solution)/shard_map/first_owner/pallas_call | solution.py:538
  38.4 0.4 collective-permute-done.4.terms
  38.7 0.1 closing.1
  (4 shorter events, 0.0 us)
Async XLA Ops:
  1.8 21.0 %collective-permute-start = (bf16[2,3,256,128]{3,2,1,0:T(8,128)(2,1)S(1)}, bf16[2,3,256,128]{3,2,1,0:T(8,128)(2,1)S(1)}, u32[]{:S(2)}, u32[]{:S(2)}) collective-permute-start(bf16[2,3,256,128]{3,2,1,0:T(8,128)(2,1)S(1)} %get-tuple-element.43), channel_id=1, source_target_pairs={{0,2},{2,0},{4,6},{6,4},{8,10},{10,8},{12,14},{14,12},{1,3},{3,1},... | collective-permute-start | bytes 1179656 | tf_op jit(solution)/shard_map/ppermute | solution.py:37
  4.8 18.6 %copy-start = (bf16[6,256,128]{2,1,0:T(8,128)(2,1)S(1)}, bf16[6,256,128]{2,1,0:T(8,128)(2,1)}, u32[]{:S(2)}) copy-start(bf16[6,256,128]{2,1,0:T(8,128)(2,1)} %q_ref.7) | copy-start | bytes 1179652
  4.8 18.6 %copy-start.1 = (bf16[6,256,128]{2,1,0:T(8,128)(2,1)S(1)}, bf16[6,256,128]{2,1,0:T(8,128)(2,1)}, u32[]{:S(2)}) copy-start(bf16[6,256,128]{2,1,0:T(8,128)(2,1)} %g_ref.7) | copy-start | bytes 1179652
  4.9 18.6 %collective-permute-start.2 = (bf16[2,3,256,128]{3,2,1,0:T(8,128)(2,1)S(1)}, bf16[2,3,256,128]{3,2,1,0:T(8,128)(2,1)S(1)}, u32[]{:S(2)}, u32[]{:S(2)}) collective-permute-start(bf16[2,3,256,128]{3,2,1,0:T(8,128)(2,1)S(1)} %pack_more_keys.1), channel_id=1, source_target_pairs={{2,4},{4,2},{6,8},{8,6},{10,12},{12,10},{3,5},{5,3},{7,9},{9,7},{1... | collective-permute-start | bytes 1179656 | tf_op jit(solution)/shard_map/ppermute | solution.py:37
  9.9 27.0 %collective-permute-start.5 = (bf16[2,2,256,128]{3,2,1,0:T(8,128)(2,1)S(1)}, bf16[2,2,256,128]{3,2,1,0:T(8,128)(2,1)S(1)}, u32[]{:S(2)}, u32[]{:S(2)}) collective-permute-start(bf16[2,2,256,128]{3,2,1,0:T(8,128)(2,1)S(1)} %get-tuple-element.60), channel_id=1, source_target_pairs={{0,2},{2,0},{4,6},{6,4},{8,10},{10,8},{12,14},{14,12},{1,3},{3,1},... | collective-permute-start | bytes 786440 | tf_op jit(solution)/shard_map/ppermute | solution.py:37
  22.8 12.1 %collective-permute-start.1 = (bf16[2,3,256,128]{3,2,1,0:T(8,128)(2,1)S(1)}, bf16[2,3,256,128]{3,2,1,0:T(8,128)(2,1)S(1)}, u32[]{:S(2)}, u32[]{:S(2)}) collective-permute-start(bf16[2,3,256,128]{3,2,1,0:T(8,128)(2,1)S(1)} %get-tuple-element.44), channel_id=1, source_target_pairs={{2,4},{4,2},{6,8},{8,6},{10,12},{12,10},{3,5},{5,3},{7,9},{9,7},{1... | collective-permute-start | bytes 1179656 | tf_op jit(solution)/shard_map/ppermute | solution.py:37
  24.4 10.5 %collective-permute-start.3 = (f32[3,2,256]{2,1,0:T(2,128)S(1)}, f32[3,2,256]{2,1,0:T(2,128)S(1)}, u32[]{:S(2)}, u32[]{:S(2)}) collective-permute-start(f32[3,2,256]{2,1,0:T(2,128)S(1)} %get-tuple-element.47), channel_id=1, source_target_pairs={{2,4},{4,2},{6,8},{8,6},{10,12},{12,10},{3,5},{5,3},{7,9},{9,7},{1... | collective-permute-start | bytes 18440 | tf_op jit(solution)/shard_map/ppermute | solution.py:37
  25.0 12.0 %collective-permute-start.6 = (f32[3,2,256]{2,1,0:T(2,128)S(1)}, f32[3,2,256]{2,1,0:T(2,128)S(1)}, u32[]{:S(2)}, u32[]{:S(2)}) collective-permute-start(f32[3,2,256]{2,1,0:T(2,128)S(1)} %get-tuple-element.63), channel_id=1, source_target_pairs={{0,2},{2,0},{4,6},{6,4},{8,10},{10,8},{12,14},{14,12},{1,3},{3,1},... | collective-permute-start | bytes 18440 | tf_op jit(solution)/shard_map/ppermute | solution.py:37
  33.2 5.5 %collective-permute-start.4 = (bf16[2,1,256,128]{3,2,1,0:T(8,128)(2,1)S(1)}, bf16[2,1,256,128]{3,2,1,0:T(8,128)(2,1)S(1)}, u32[]{:S(2)}, u32[]{:S(2)}) collective-permute-start(bf16[2,1,256,128]{3,2,1,0:T(8,128)(2,1)S(1)} %returned.1), channel_id=1, source_target_pairs={{0,2},{2,0},{4,6},{6,4},{8,10},{10,8},{12,14},{14,12},{1,3},{3,1},... | collective-permute-start | bytes 393224 | tf_op jit(solution)/shard_map/ppermute | solution.py:37
